TPU v7x, 256 devices: a whole 4x4x8 slice. The times are simulated.
256 devices in a mesh: seq: 64 (over z, y, core), head: 4 (over x).
Axes of the slice: x: 4, y: 4, z: 8, core: 2. Of those that a mesh axis runs over, the one named last changes fastest.
Arguments:
- inputs: bfloat16 [131072, 4096], P('seq', 'head'), may hold values from -6 to 6
- state_in: bfloat16 [131072, 128], P('seq'), may hold values from -6 to 6
- state_out: bfloat16 [131072, 128], P('seq'), may hold values from -0.046875 to 0.046875
- log_decay: float32 [64, 131072], P('head', 'seq'), may hold values from -0.6 to 0, as said below
- level_weight: float32 [7, 64, 131072], P(None, 'head', 'seq'), may hold values from 0.25 to 2
- skip: float32 [64], P('head'), may hold values from 0.5 to 1.5
- norm_gain: float32 [4096], P('head'), may hold values from 0.25 to 1.75
- resets: int32 [4], replicated, may hold values from 1 to 131071
Outputs:
- mixed: bfloat16 [131072, 4096], P('seq', 'head')
Inputs may be any that keep to these rules, and one draw needn't show every extreme that they name: `log_decay`: natural logarithm of a decay factor; every value is below zero. `resets`: positions may repeat.
All inputs are finite; a program needn't handle non-finite values.
Results may differ from a plain program's by a relative error of at most 0.005.
Values may be sent and summed in bfloat16 or wider, within the bound.
No kernel may reach another device: no remote copies, remote signals or barrier semaphores. Data moves between devices by JAX's collectives and lax.ppermute only.
A program may use at most 128 MiB of HBM per device.

v0:
```python
import jax
import jax.numpy as jnp
from jax import lax
from jax.sharding import PartitionSpec as P

HEAD_TOTAL = 64
HEAD_DIM = 64
STATE = 128
BLOCK = 256
LEVELS = 7


EPSILON = 1e-05


def partner(block, axis, bit):
    count = lax.axis_size(axis)
    route = []
    for low in range(count):
        high = low | 1 << bit
        if high != low and high < count:
            route += [(low, high), (high, low)]
    return lax.ppermute(block, axis, route)


def running_sums(log_rate, flags):
    return (jnp.cumsum(log_rate, axis=1), jnp.cumsum(flags, dtype=jnp.int32))


def stretch_state(running_log, reset_count, state_part, inputs_part):
    weight = jnp.where(
        (reset_count == reset_count[-1])[None, :], jnp.exp(running_log[:, -1:] - running_log), 0.0
    )
    scaled = (weight[:, :, None] * state_part.astype(jnp.float32)[None]).astype(jnp.bfloat16)
    return jnp.einsum("hsn,shp->hnp", scaled, inputs_part, preferred_element_type=jnp.float32)


def block_states(running_log, reset_count, state_blocks, input_blocks, stretch_count):
    heads_here = running_log.shape[0]
    log_stretches = running_log.reshape(heads_here, stretch_count, BLOCK).transpose(1, 0, 2)
    count_stretches = reset_count.reshape(stretch_count, BLOCK)

    def one_state(packed):
        return stretch_state(packed[0], packed[1], packed[2], packed[3])

    states = lax.map(one_state, (log_stretches, count_stretches, state_blocks, input_blocks))
    end_logs = log_stretches[:, :, -1]
    end_counts = count_stretches[:, -1]
    prev_ends = jnp.concatenate([jnp.zeros_like(end_logs[:1]), end_logs[:-1]], 0)
    prev_counts = jnp.concatenate([jnp.zeros_like(end_counts[:1]), end_counts[:-1]], 0)
    order = jnp.arange(stretch_count, dtype=jnp.int32)
    valid = (order[None, :] < order[:, None]) & (prev_counts[:, None] == end_counts[None, :])
    exponent = jnp.where(valid[:, :, None], prev_ends[:, None, :] - end_logs[None, :, :], -jnp.inf)
    starts = jnp.einsum(
        "ckh,khnp->chnp", jnp.exp(exponent), states, precision=lax.Precision.HIGHEST
    )
    final = jnp.where(
        (end_counts == end_counts[-1])[:, None], jnp.exp(end_logs[-1][None, :] - end_logs), 0.0
    )
    block_total = jnp.einsum("kh,khnp->hnp", final, states, precision=lax.Precision.HIGHEST)
    return (starts, block_total, prev_ends, prev_counts)


def stretch_output(
    running_log,
    reset_count,
    level_coef,
    prev_end,
    prev_count,
    stretch_start,
    state_part,
    out_part,
    inputs_part,
    level_low,
    skip,
):
    offsets = jnp.arange(BLOCK, dtype=jnp.int32)
    causal = (offsets[None, :] <= offsets[:, None]) & (reset_count[None, :] == reset_count[:, None])
    exponent = jnp.where(causal[None], running_log[:, :, None] - running_log[:, None, :], -jnp.inf)
    decay = jnp.exp(exponent) * level_coef[0][:, :, None]
    scores = jnp.einsum("tn,sn->ts", out_part, state_part, preferred_element_type=jnp.float32)
    mask_weight = (decay * scores[None]).astype(jnp.bfloat16)
    inner = jnp.einsum("hts,shp->thp", mask_weight, inputs_part, preferred_element_type=jnp.float32)
    stacked = jnp.concatenate([stretch_start.astype(jnp.bfloat16)[None], level_low], 0)
    reads = jnp.einsum("tn,lhnp->tlhp", out_part, stacked, preferred_element_type=jnp.float32)
    near = jnp.where(
        (reset_count == prev_count)[None, :], jnp.exp(running_log - prev_end[:, None]), 0.0
    )
    far_side = jnp.where((reset_count == 0)[None, :], jnp.exp(running_log), 0.0)
    multiplier_term = level_coef * jnp.concatenate(
        [near[None], jnp.broadcast_to(far_side[None], (LEVELS - 1,) + far_side.shape)], 0
    )
    carried = jnp.einsum("lht,tlhp->thp", multiplier_term, reads, precision=lax.Precision.HIGHEST)
    return inner + carried + skip[None, :, None] * inputs_part.astype(jnp.float32)


def per_device(inputs, state_in, state_out, log_decay, level_weight, skip, norm_gain, resets):
    token_count = inputs.shape[0]
    head_count = log_decay.shape[0]
    stretch_count = token_count // BLOCK
    input_blocks = inputs.reshape(stretch_count, BLOCK, head_count, HEAD_DIM)
    in_blocks = state_in.reshape(stretch_count, BLOCK, STATE)
    out_blocks = state_out.reshape(stretch_count, BLOCK, STATE)
    my_index = lax.axis_index("seq")
    position = my_index * token_count + jnp.arange(token_count, dtype=jnp.int32)
    flags = jnp.any(position[:, None] == resets[None, :], axis=1).astype(jnp.int32)
    running_log, reset_count = running_sums(log_decay, flags)
    starts, block_total, prev_ends, prev_counts = block_states(
        running_log, reset_count, in_blocks, input_blocks, stretch_count
    )
    log_total = running_log[:, -1]
    clear = (reset_count[-1] > 0).astype(jnp.float32)
    bit_count = lax.axis_size("seq").bit_length() - 1
    span = jnp.exp(log_total) * (1.0 - clear)
    grouped = block_total
    leading = jnp.ones_like(span)
    found = []
    for bit_number in range(bit_count):
        partner_state, partner_span = partner((grouped, span), "seq", bit_number)
        upper = jnp.right_shift(my_index, bit_number) % 2 == 1
        found.append(jnp.where(upper, leading[:, None, None] * partner_state, 0.0))
        grouped = jnp.where(
            upper,
            partner_state * span[:, None, None] + grouped,
            grouped * partner_span[:, None, None] + partner_state,
        )
        leading = jnp.where(upper, partner_span * leading, leading)
        span = span * partner_span
    level_low = jnp.stack(found, 0).astype(jnp.bfloat16)
    log_stretches = running_log.reshape(head_count, stretch_count, BLOCK).transpose(1, 0, 2)
    count_stretches = reset_count.reshape(stretch_count, BLOCK)
    coef_stretches = level_weight.reshape(LEVELS, head_count, stretch_count, BLOCK).transpose(
        2, 0, 1, 3
    )

    def one_stretch(parts):
        return stretch_output(
            parts[0],
            parts[1],
            parts[2],
            parts[3],
            parts[4],
            parts[5],
            parts[6],
            parts[7],
            parts[8],
            level_low,
            skip,
        )

    value_rows = lax.map(
        one_stretch,
        (
            log_stretches,
            count_stretches,
            coef_stretches,
            prev_ends,
            prev_counts,
            starts,
            in_blocks,
            out_blocks,
            input_blocks,
        ),
    )
    squares = jnp.sum(value_rows * value_rows, axis=(2, 3))
    whole_squares = lax.psum(squares, "head")
    multiplier_term = lax.rsqrt(whole_squares / (HEAD_TOTAL * HEAD_DIM) + EPSILON)
    scaled = (
        value_rows * multiplier_term[:, :, None, None] * norm_gain.reshape(head_count, HEAD_DIM)
    )
    return scaled.astype(jnp.bfloat16).reshape(token_count, head_count * HEAD_DIM)


def solution(mesh):
    placed = (
        P("seq", "head"),
        P("seq", None),
        P("seq", None),
        P("head", "seq"),
        P(None, "head", "seq"),
        P("head"),
        P("head"),
        P(),
    )
    return jax.shard_map(
        per_device, mesh=mesh, in_specs=placed, out_specs=P("seq", "head"), check_vma=False
    )
```

profile of v0, /device:TPU:16, one launch (start us, length us, event | category | flops | bytes accessed | tf_op | source)
XLA Modules:
  0.0 321.3 jit_solution(7709365570040094405)
XLA Ops:
  3.8 4.5 %reduce-window.19 = f32[16,16,128]{2,1,0:T(8,128)S(1)} reduce-window(f32[16,16,128]{2,1,0:T(8,128)S(1)} %bitcast.191, f32[]{:T(128)} %constant.101.clone.1), window={size=1x1x128 pad=0_0x0_0x127_0}, to_apply=%region_0.0 | reduce-window | flops 4161536 | bytes 262148 | tf_op jit(solution)/shard_map/reduce-window
  9.3 11.9 %reshape.275 = bf16[8,256,16,64]{3,2,1,0:T(8,128)(2,1)} reshape(bf16[2048,1024]{1,0:T(8,128)(2,1)} %param.12) | data formatting | bytes 8388608 | tf_op jit(solution)/shard_map/reshape | solution.py:101
  21.2 10.3 %copy.62 = bf16[8,256,16,64]{1,3,2,0:T(8,128)(2,1)} copy(bf16[8,256,16,64]{3,2,1,0:T(8,128)(2,1)} %reshape.275) | data formatting | bytes 8388608 | tf_op jit(solution)/shard_map/while | solution.py:151
  31.5 39.8 %while.20 = (s32[]{:T(128)}, f32[8,16,128,64]{2,3,1,0:T(8,128)}, s32[8,256]{1,0:T(8,128)S(1)}, f32[8,16,256]{2,0,1:T(8,128)S(1)}, bf16[8,256,128]{2,1,0:T(8,128)...) while((s32[]{:T(128)}, f32[8,16,128,64]{2,3,1,0:T(8,128)}, ...), condition=%wide.region_6.7_spmd, body=%wide.region_5.6_spmd.sunk | while | flops 68198656 | bytes 1526597 | solution.py:46
  33.8 2.7 fusion.81
  38.8 2.6 fusion.81
  43.7 2.6 fusion.81
  48.7 2.6 fusion.81
  53.7 2.6 fusion.81
  58.7 2.6 fusion.81
  63.6 2.6 fusion.81
  68.6 2.6 fusion.81
  71.3 2.6 multiply_reduce_fusion.2
  74.0 1.3 copy.83
  78.7 1.4 collective-permute-start.2
  82.3 10.8 %collective-permute-done.3 = f32[16]{0:T(128)S(1)} collective-permute-done((f32[16]{0:T(128)S(1)}, f32[16]{0:T(128)S(1)}, u32[]{:S(2)}, u32[]{:S(2)}) %collective-permute-start.3) | collective-permute-done | bytes 96 | tf_op jit(solution)/shard_map/ppermute | solution.py:23
  93.2 2.2 collective-permute-start.4
  95.4 1.2 pad_add_fusion
  96.6 1.5 copy.94
  99.5 1.5 collective-permute-start.5
  101.0 7.2 %collective-permute-done.5 = f32[16]{0:T(128)S(1)} collective-permute-done((f32[16]{0:T(128)S(1)}, f32[16]{0:T(128)S(1)}, u32[]{:S(2)}, u32[]{:S(2)}) %collective-permute-start.5) | collective-permute-done | bytes 96 | tf_op jit(solution)/shard_map/ppermute | solution.py:23
  108.2 1.2 add_select_fusion.2
  109.4 2.2 collective-permute-start.6
  112.5 10.1 %fusion.40 = f32[8,16,128,64]{2,0,3,1:T(8,128)} fusion(f32[8,16,128,64]{2,3,1,0:T(8,128)} %get-tuple-element.104, f32[8,16]{0,1:T(8,128)S(1)} %copy.59, f32[8,16]{0,1:T(8,128)S(1)} %copy.58, pred[8,8]{1,0:T(8,128)(4,1)S(1)} %fusion.63), kind=kOutput, calls=%fused_computation.66 | convolution fusion | flops 100665344 | bytes 8389696 | tf_op jit(solution)/shard_map/ckh,khnp->chnp/dot_general | solution.py:54
  122.8 3.4 %collective-permute-done.7 = f32[16]{0:T(128)S(1)} collective-permute-done((f32[16]{0:T(128)S(1)}, f32[16]{0:T(128)S(1)}, u32[]{:S(2)}, u32[]{:S(2)}) %collective-permute-start.7) | collective-permute-done | bytes 96 | tf_op jit(solution)/shard_map/ppermute | solution.py:23
  126.2 3.3 %collective-permute-start.9 = (f32[16]{0:T(128)S(1)}, f32[16]{0:T(128)S(1)}, u32[]{:S(2)}, u32[]{:S(2)}) collective-permute-start(f32[16]{0:T(128)S(1)} %mul.262), channel_id=1, source_target_pairs={{0,64},{64,0},{4,68},{68,4},{8,72},{72,8},{12,76},{76,12},{16,80},... | collective-permute-start | bytes 200 | tf_op jit(solution)/shard_map/ppermute | solution.py:23
  129.8 11.7 %collective-permute-done.9 = f32[16]{0:T(128)S(1)} collective-permute-done((f32[16]{0:T(128)S(1)}, f32[16]{0:T(128)S(1)}, u32[]{:S(2)}, u32[]{:S(2)}) %collective-permute-start.9) | collective-permute-done | bytes 96 | tf_op jit(solution)/shard_map/ppermute | solution.py:23
  141.7 10.8 %collective-permute-done.8 = f32[16,128,64]{1,2,0:T(8,128)S(1)} collective-permute-done((f32[16,128,64]{1,2,0:T(8,128)S(1)}, f32[16,128,64]{1,2,0:T(8,128)S(1)}, u32[]{:S(2)}, u32[]{:S(2)}) %collective-permute-start.8) | collective-permute-done | bytes 524320 | tf_op jit(solution)/shard_map/ppermute | solution.py:23
  152.7 4.8 %collective-permute-start.10 = (f32[16,128,64]{1,2,0:T(8,128)S(1)}, f32[16,128,64]{1,2,0:T(8,128)S(1)}, u32[]{:S(2)}, u32[]{:S(2)}) collective-permute-start(f32[16,128,64]{1,2,0:T(8,128)S(1)} %add_select_fusion), channel_id=1, source_target_pairs={{0,128},{128,0},{4,132},{132,4},{8,136},{136,8},{12,140},{140,12},... | collective-permute-start | bytes 1572872 | tf_op jit(solution)/shard_map/ppermute | solution.py:23
  157.5 1.2 fusion.48
  159.0 22.9 %collective-permute-done.10 = f32[16,128,64]{1,2,0:T(8,128)S(1)} collective-permute-done((f32[16,128,64]{1,2,0:T(8,128)S(1)}, f32[16,128,64]{1,2,0:T(8,128)S(1)}, u32[]{:S(2)}, u32[]{:S(2)}) %collective-permute-start.10) | collective-permute-done | bytes 524320 | tf_op jit(solution)/shard_map/ppermute | solution.py:23
  182.0 1.1 copy-done.1
  183.2 94.1 %while.21 = (s32[]{:T(128)}, f32[8,256,16,64]{1,3,2,0:T(8,128)}, bf16[8,256,16,64]{1,3,2,0:T(8,128)(2,1)}, s32[8,256]{1,0:T(8,128)S(1)}, f32[8,16,256]{2,0,1:T(8...) while((s32[]{:T(128)}, f32[8,256,16,64]{1,3,2,0:T(8,128)}, ...), condition=%wide.region_8.9_spmd, body=%wide.region_7.8_spmd.sunk | while | flops 634524160 | bytes 9936233 | solution.py:151
  184.6 2.7 constant_dynamic-slice_fusion.15
  187.3 2.8 multiply_reduce_fusion.4
  190.2 1.1 fusion.89
  191.3 3.5 %fusion.91 = f32[8,256,16,64]{1,3,2,0:T(8,128)} fusion(f32[8,256,16,64]{1,3,2,0:T(8,128)} %get-tuple-element.401, s32[]{:T(128)} %get-tuple-element.400, f32[256,16,64]{0,2,1:T(8,128)S(1)} %multiply_reduce_fusion.4, f32[256,256]{1,0:T(8,128)S(1)} %fusion.89, f32[16,256]{1,0:T(8,128)S(1)} %slice_bitcast_fusion.8, ...), kind=kOutput, calls=%fused_computation.30.clone.1 | convolution fusion | flops 140509184 | bytes 3524096 | tf_op jit(solution)/shard_map/while/body/eval_jaxpr/hts,shp->thp/dot_general | solution.py:83
  196.3 2.7 constant_dynamic-slice_fusion.15
  199.0 2.8 multiply_reduce_fusion.4
  201.9 1.1 fusion.89
  203.0 3.7 %fusion.91 = f32[8,256,16,64]{1,3,2,0:T(8,128)} fusion(f32[8,256,16,64]{1,3,2,0:T(8,128)} %get-tuple-element.401, s32[]{:T(128)} %get-tuple-element.400, f32[256,16,64]{0,2,1:T(8,128)S(1)} %multiply_reduce_fusion.4, f32[256,256]{1,0:T(8,128)S(1)} %fusion.89, f32[16,256]{1,0:T(8,128)S(1)} %slice_bitcast_fusion.8, ...), kind=kOutput, calls=%fused_computation.30.clone.1 | convolution fusion | flops 140509184 | bytes 3524096 | tf_op jit(solution)/shard_map/while/body/eval_jaxpr/hts,shp->thp/dot_general | solution.py:83
  208.1 2.7 constant_dynamic-slice_fusion.15
  210.8 2.8 multiply_reduce_fusion.4
  214.9 3.5 %fusion.91 = f32[8,256,16,64]{1,3,2,0:T(8,128)} fusion(f32[8,256,16,64]{1,3,2,0:T(8,128)} %get-tuple-element.401, s32[]{:T(128)} %get-tuple-element.400, f32[256,16,64]{0,2,1:T(8,128)S(1)} %multiply_reduce_fusion.4, f32[256,256]{1,0:T(8,128)S(1)} %fusion.89, f32[16,256]{1,0:T(8,128)S(1)} %slice_bitcast_fusion.8, ...), kind=kOutput, calls=%fused_computation.30.clone.1 | convolution fusion | flops 140509184 | bytes 3524096 | tf_op jit(solution)/shard_map/while/body/eval_jaxpr/hts,shp->thp/dot_general | solution.py:83
  219.8 2.7 constant_dynamic-slice_fusion.15
  222.5 2.8 multiply_reduce_fusion.4
  226.6 3.6 %fusion.91 = f32[8,256,16,64]{1,3,2,0:T(8,128)} fusion(f32[8,256,16,64]{1,3,2,0:T(8,128)} %get-tuple-element.401, s32[]{:T(128)} %get-tuple-element.400, f32[256,16,64]{0,2,1:T(8,128)S(1)} %multiply_reduce_fusion.4, f32[256,256]{1,0:T(8,128)S(1)} %fusion.89, f32[16,256]{1,0:T(8,128)S(1)} %slice_bitcast_fusion.8, ...), kind=kOutput, calls=%fused_computation.30.clone.1 | convolution fusion | flops 140509184 | bytes 3524096 | tf_op jit(solution)/shard_map/while/body/eval_jaxpr/hts,shp->thp/dot_general | solution.py:83
  231.6 2.7 constant_dynamic-slice_fusion.15
  234.3 2.8 multiply_reduce_fusion.4
  238.3 3.5 %fusion.91 = f32[8,256,16,64]{1,3,2,0:T(8,128)} fusion(f32[8,256,16,64]{1,3,2,0:T(8,128)} %get-tuple-element.401, s32[]{:T(128)} %get-tuple-element.400, f32[256,16,64]{0,2,1:T(8,128)S(1)} %multiply_reduce_fusion.4, f32[256,256]{1,0:T(8,128)S(1)} %fusion.89, f32[16,256]{1,0:T(8,128)S(1)} %slice_bitcast_fusion.8, ...), kind=kOutput, calls=%fused_computation.30.clone.1 | convolution fusion | flops 140509184 | bytes 3524096 | tf_op jit(solution)/shard_map/while/body/eval_jaxpr/hts,shp->thp/dot_general | solution.py:83
  243.3 2.7 constant_dynamic-slice_fusion.15
  246.0 2.8 multiply_reduce_fusion.4
  250.0 3.6 %fusion.91 = f32[8,256,16,64]{1,3,2,0:T(8,128)} fusion(f32[8,256,16,64]{1,3,2,0:T(8,128)} %get-tuple-element.401, s32[]{:T(128)} %get-tuple-element.400, f32[256,16,64]{0,2,1:T(8,128)S(1)} %multiply_reduce_fusion.4, f32[256,256]{1,0:T(8,128)S(1)} %fusion.89, f32[16,256]{1,0:T(8,128)S(1)} %slice_bitcast_fusion.8, ...), kind=kOutput, calls=%fused_computation.30.clone.1 | convolution fusion | flops 140509184 | bytes 3524096 | tf_op jit(solution)/shard_map/while/body/eval_jaxpr/hts,shp->thp/dot_general | solution.py:83
  255.1 2.7 constant_dynamic-slice_fusion.15
  257.8 2.8 multiply_reduce_fusion.4
  261.8 3.7 %fusion.91 = f32[8,256,16,64]{1,3,2,0:T(8,128)} fusion(f32[8,256,16,64]{1,3,2,0:T(8,128)} %get-tuple-element.401, s32[]{:T(128)} %get-tuple-element.400, f32[256,16,64]{0,2,1:T(8,128)S(1)} %multiply_reduce_fusion.4, f32[256,256]{1,0:T(8,128)S(1)} %fusion.89, f32[16,256]{1,0:T(8,128)S(1)} %slice_bitcast_fusion.8, ...), kind=kOutput, calls=%fused_computation.30.clone.1 | convolution fusion | flops 140509184 | bytes 3524096 | tf_op jit(solution)/shard_map/while/body/eval_jaxpr/hts,shp->thp/dot_general | solution.py:83
  266.9 2.7 constant_dynamic-slice_fusion.15
  269.6 2.8 multiply_reduce_fusion.4
  273.7 3.6 %fusion.91 = f32[8,256,16,64]{1,3,2,0:T(8,128)} fusion(f32[8,256,16,64]{1,3,2,0:T(8,128)} %get-tuple-element.401, s32[]{:T(128)} %get-tuple-element.400, f32[256,16,64]{0,2,1:T(8,128)S(1)} %multiply_reduce_fusion.4, f32[256,256]{1,0:T(8,128)S(1)} %fusion.89, f32[16,256]{1,0:T(8,128)S(1)} %slice_bitcast_fusion.8, ...), kind=kOutput, calls=%fused_computation.30.clone.1 | convolution fusion | flops 140509184 | bytes 3524096 | tf_op jit(solution)/shard_map/while/body/eval_jaxpr/hts,shp->thp/dot_general | solution.py:83
  277.3 4.3 %multiply_reduce_fusion.1 = f32[8,256]{1,0:T(8,128)S(1)} fusion(f32[8,256,16,64]{1,3,2,0:T(8,128)} %get-tuple-element.105), kind=kLoop, calls=%fused_computation.62 | loop fusion | flops 4192256 | bytes 8396800 | tf_op jit(solution)/shard_map/reduce_sum | solution.py:165
  281.6 10.6 %psum.7 = f32[8,256]{1,0:T(8,128)S(1)} all-reduce(f32[8,256]{1,0:T(8,128)S(1)} %multiply_reduce_fusion.1), channel_id=1, replica_groups=mesh['seq'=64,'head'=4] {'head'}, use_global_device_ids=true, to_apply=%region_10.11 | all-reduce | flops 2048 | bytes 16384 | tf_op jit(solution)/shard_map/psum | solution.py:166
  292.2 6.3 %multiply_convert_fusion.14 = bf16[8,256,16,64]{1,3,2,0:T(8,128)(2,1)} fusion(f32[8,256,16,64]{1,3,2,0:T(8,128)} %get-tuple-element.105, f32[16,64]{1,0:T(8,128)S(1)} %mul.273, f32[8,256]{1,0:T(8,128)S(1)} %add_rsqrt_fusion), kind=kLoop, calls=%fused_computation.61 | loop fusion | flops 6291456 | bytes 12595200 | tf_op jit(solution)/shard_map/convert_element_type | solution.py:171
  298.5 10.9 %copy.84 = bf16[8,256,16,64]{3,2,1,0:T(8,128)(2,1)} copy(bf16[8,256,16,64]{1,3,2,0:T(8,128)(2,1)} %multiply_convert_fusion.14) | data formatting | bytes 8388608 | tf_op jit(solution)/shard_map/reshape | solution.py:171
  309.4 11.9 %reshape.274 = bf16[2048,1024]{1,0:T(8,128)(2,1)} reshape(bf16[8,256,16,64]{3,2,1,0:T(8,128)(2,1)} %copy.84) | data formatting | bytes 8388608 | tf_op jit(solution)/shard_map/reshape | solution.py:171
  (246 shorter events, 50.7 us)
Async XLA Ops:
  9.3 71.5 %copy-start = (f32[16,8,256]{0,1,2:T(8,128)}, f32[16,8,256]{0,1,2:T(8,128)S(1)}, u32[]{:S(2)}) copy-start(f32[16,8,256]{0,1,2:T(8,128)S(1)} %copy.55) | copy-start | bytes 393220
  73.9 4.7 %collective-permute-start = (f32[16,128,64]{1,2,0:T(8,128)S(1)}, f32[16,128,64]{1,2,0:T(8,128)S(1)}, u32[]{:S(2)}, u32[]{:S(2)}) collective-permute-start(f32[16,128,64]{1,2,0:T(8,128)S(1)} %multiply_reduce_fusion.2), channel_id=1, source_target_pairs={{0,4},{4,0},{8,12},{12,8},{16,20},{20,16},{24,28},{28,24},{32,36},... | collective-permute-start | bytes 1572872 | tf_op jit(solution)/shard_map/ppermute | solution.py:23
  77.3 1.3 collective-permute-start.1
  78.6 19.5 %copy-start.2 = (f32[16]{0:T(128)}, f32[16]{0:T(128)S(1)}, u32[]{:S(2)}) copy-start(f32[16]{0:T(128)S(1)} %collective-permute-done.1) | copy-start | bytes 196
  78.7 14.3 %collective-permute-start.2 = (f32[16,128,64]{1,2,0:T(8,128)S(1)}, f32[16,128,64]{1,2,0:T(8,128)S(1)}, u32[]{:S(2)}, u32[]{:S(2)}) collective-permute-start(f32[16,128,64]{1,2,0:T(8,128)S(1)} %add_select_fusion.4), channel_id=1, source_target_pairs={{0,8},{8,0},{4,12},{12,4},{16,24},{24,16},{20,28},{28,20},{32,40},... | collective-permute-start | bytes 1572872 | tf_op jit(solution)/shard_map/ppermute | solution.py:23
  81.5 15.1 %copy-start.5 = (f32[16]{0:T(128)}, f32[16]{0:T(128)S(1)}, u32[]{:S(2)}) copy-start(f32[16]{0:T(128)S(1)} %fusion.67) | copy-start | bytes 196
  81.5 11.5 %collective-permute-start.3 = (f32[16]{0:T(128)S(1)}, f32[16]{0:T(128)S(1)}, u32[]{:S(2)}, u32[]{:S(2)}) collective-permute-start(f32[16]{0:T(128)S(1)} %fusion.67), channel_id=1, source_target_pairs={{0,8},{8,0},{4,12},{12,4},{16,24},{24,16},{20,28},{28,20},{32,40},... | collective-permute-start | bytes 200 | tf_op jit(solution)/shard_map/ppermute | solution.py:23
  93.0 3.6 %copy-start.6 = (f32[16]{0:T(128)}, f32[16]{0:T(128)S(1)}, u32[]{:S(2)}) copy-start(f32[16]{0:T(128)S(1)} %collective-permute-done.3) | copy-start | bytes 196
  93.2 15.0 %collective-permute-start.4 = (f32[16,128,64]{1,2,0:T(8,128)S(1)}, f32[16,128,64]{1,2,0:T(8,128)}, u32[]{:S(2)}, u32[]{:S(2)}) collective-permute-start(f32[16,128,64]{1,2,0:T(8,128)S(1)} %add_select_fusion.3), channel_id=1, source_target_pairs={{0,16},{16,0},{4,20},{20,4},{8,24},{24,8},{12,28},{28,12},{32,48},... | collective-permute-start | bytes 1572872 | tf_op jit(solution)/shard_map/ppermute | solution.py:23
  99.5 8.6 %collective-permute-start.5 = (f32[16]{0:T(128)S(1)}, f32[16]{0:T(128)S(1)}, u32[]{:S(2)}, u32[]{:S(2)}) collective-permute-start(f32[16]{0:T(128)S(1)} %mul.246), channel_id=1, source_target_pairs={{0,16},{16,0},{4,20},{20,4},{8,24},{24,8},{12,28},{28,12},{32,48},... | collective-permute-start | bytes 200 | tf_op jit(solution)/shard_map/ppermute | solution.py:23
  109.4 20.1 %collective-permute-start.6 = (f32[16,128,64]{1,2,0:T(8,128)S(1)}, f32[16,128,64]{1,2,0:T(8,128)S(1)}, u32[]{:S(2)}, u32[]{:S(2)}) collective-permute-start(f32[16,128,64]{1,2,0:T(8,128)S(1)} %add_select_fusion.2), channel_id=1, source_target_pairs={{0,32},{32,0},{4,36},{36,4},{8,40},{40,8},{12,44},{44,12},{16,48},... | collective-permute-start | bytes 1572872 | tf_op jit(solution)/shard_map/ppermute | solution.py:23
  112.5 10.3 %copy-start.4 = (f32[1024]{0:T(1024)S(1)}, f32[1024]{0:T(1024)}, u32[]{:S(2)}) copy-start(f32[1024]{0:T(1024)} %param.18) | copy-start | bytes 12292
  112.5 29.0 %copy-start.3 = (f32[16]{0:T(128)S(1)}, f32[16]{0:T(128)}, u32[]{:S(2)}) copy-start(f32[16]{0:T(128)} %copy-done.2) | copy-start | bytes 196
  112.5 29.0 %copy-start.7 = (f32[16]{0:T(128)S(1)}, f32[16]{0:T(128)}, u32[]{:S(2)}) copy-start(f32[16]{0:T(128)} %copy-done.6) | copy-start | bytes 196
  122.6 60.6 %copy-start.8 = (s32[8]{0:T(128)S(1)}, s32[8]{0:T(128)}, u32[]{:S(2)}) copy-start(s32[8]{0:T(128)} %pad_add_fusion) | copy-start | bytes 100
  122.6 60.6 %copy-start.9 = (f32[16]{0:T(128)S(1)}, f32[16]{0:T(128)}, u32[]{:S(2)}) copy-start(f32[16]{0:T(128)} %param.17) | copy-start | bytes 196
  122.6 3.6 %collective-permute-start.7 = (f32[16]{0:T(128)S(1)}, f32[16]{0:T(128)S(1)}, u32[]{:S(2)}, u32[]{:S(2)}) collective-permute-start(f32[16]{0:T(128)S(1)} %mul.254), channel_id=1, source_target_pairs={{0,32},{32,0},{4,36},{36,4},{8,40},{40,8},{12,44},{44,12},{16,48},... | collective-permute-start | bytes 200 | tf_op jit(solution)/shard_map/ppermute | solution.py:23
  126.2 15.2 %collective-permute-start.9 = (f32[16]{0:T(128)S(1)}, f32[16]{0:T(128)S(1)}, u32[]{:S(2)}, u32[]{:S(2)}) collective-permute-start(f32[16]{0:T(128)S(1)} %mul.262), channel_id=1, source_target_pairs={{0,64},{64,0},{4,68},{68,4},{8,72},{72,8},{12,76},{76,12},{16,80},... | collective-permute-start | bytes 200 | tf_op jit(solution)/shard_map/ppermute | solution.py:23
  129.6 22.8 %collective-permute-start.8 = (f32[16,128,64]{1,2,0:T(8,128)S(1)}, f32[16,128,64]{1,2,0:T(8,128)S(1)}, u32[]{:S(2)}, u32[]{:S(2)}) collective-permute-start(f32[16,128,64]{1,2,0:T(8,128)S(1)} %add_select_fusion.1), channel_id=1, source_target_pairs={{0,64},{64,0},{4,68},{68,4},{8,72},{72,8},{12,76},{76,12},{16,80},... | collective-permute-start | bytes 1572872 | tf_op jit(solution)/shard_map/ppermute | solution.py:23
  152.7 29.2 %collective-permute-start.10 = (f32[16,128,64]{1,2,0:T(8,128)S(1)}, f32[16,128,64]{1,2,0:T(8,128)S(1)}, u32[]{:S(2)}, u32[]{:S(2)}) collective-permute-start(f32[16,128,64]{1,2,0:T(8,128)S(1)} %add_select_fusion), channel_id=1, source_target_pairs={{0,128},{128,0},{4,132},{132,4},{8,136},{136,8},{12,140},{140,12},... | collective-permute-start | bytes 1572872 | tf_op jit(solution)/shard_map/ppermute | solution.py:23
  182.0 1.1 copy-start.1
where the time goes:
time: 325 us; the launch traced here: 321 us
  matrix products  91 us (28%)
  local copies, waits for them, and re-layouts  87.3 us (27%)
  waiting for transfers between devices  66.9 us (21%)
  other arithmetic  46.9 us (14%)
  starting transfers between devices  16.9 us (5%)
  blocking collectives  10.6 us (3%)
    ppermute x11, waiting for transfers between devices, partner(): return lax.ppermute(block, axis, route)  66.9 us
    dot_general x8, matrix products, stretch_output(): jnp.einsum('hts,shp->thp', mask_weight, inputs_part, preferred_element_ty...  28.8 us
    dynamic_slice x40, local copies, waits for them, and re-layouts, per_device(): lax.map(one_stretch, (log_stretches, count_stretches, coef_stretches, pre...  26.8 us
    reshape x2, local copies, waits for them, and re-layouts, per_device(): scaled.astype(jnp.bfloat16).reshape(token_count, head_count * HEAD_DIM)  22.7 us
    dot_general x8, matrix products, stretch_output(): jnp.einsum('tn,lhnp->tlhp', out_part, stacked, preferred_element_type=jnp...  22.5 us
    dot_general x8, matrix products, stretch_state(): jnp.einsum('hsn,shp->hnp', scaled, inputs_part, preferred_element_type=jn...  21.2 us
    ppermute x11, starting transfers between devices, partner(): return lax.ppermute(block, axis, route)  16.9 us
    reshape x1, local copies, waits for them, and re-layouts, per_device(): input_blocks = inputs.reshape(stretch_count, BLOCK, head_count, HEAD_DIM)  11.9 us
  transfers between devices with their start and end apart: 11, of which 7 were waited for; matrix products, arithmetic and copies ran while one was open for 7% of the time, Pallas kernels for 0%

commit v1 on v0

v1 whole, which is shorter than its diff:
```python
import functools

import jax
import jax.numpy as jnp
from jax import lax
from jax.experimental import pallas as pl
from jax.experimental.pallas import tpu as pltpu
from jax.sharding import PartitionSpec as P

HEAD_TOTAL = 64
HEAD_DIM = 64
STATE = 128
LEVELS = 7
TOK_DEV = 2048
EPSILON = 1e-05

CHUNK = 256
CHUNKS = TOK_DEV // CHUNK
HEADS = 16
FEATURES = HEADS * HEAD_DIM
HALF = FEATURES // 2
PAIRS = HEADS // 2
WIDE = 2 * HEAD_DIM
SPAN_ROWS = 3 * HEADS
RESETS = 4
STEPS = ((2, 1), (6, 2), (8, 3), (16, 4), (48, 5))
PIECE = 2

F32 = jnp.float32
BF16 = jnp.bfloat16
PARAMS = dict(vmem_limit_bytes=32 * 1024 * 1024)


def dot(a, b):
    return lax.dot_general(a, b, (((1,), (0,)), ((), ())), preferred_element_type=F32)


def dot_nt(a, b):
    return lax.dot_general(a, b, (((1,), (1,)), ((), ())), preferred_element_type=F32)


def pair_rows(values, pair):
    width = values.shape[1]
    return jnp.concatenate(
        [
            jnp.broadcast_to(values[h : h + 1, :], (HEAD_DIM, width))
            for h in (2 * pair, 2 * pair + 1)
        ],
        axis=0,
    )


def pair_column(values, pair, width):
    return jnp.concatenate(
        [
            jnp.broadcast_to(values[h : h + 1, 0:1], (HEAD_DIM, width))
            for h in (2 * pair, 2 * pair + 1)
        ],
        axis=0,
    )


def write_spans(ref, first, span):
    high = span.astype(BF16)
    rest = span - high.astype(F32)
    middle = rest.astype(BF16)
    low = (rest - middle.astype(F32)).astype(BF16)
    ref[first : first + SPAN_ROWS, :] = jnp.concatenate([high, middle, low], axis=0)


def read_spans(ref, first):
    parts = ref[first : first + SPAN_ROWS, :].astype(F32)
    return parts[:HEADS] + parts[HEADS : 2 * HEADS] + parts[2 * HEADS :]


def state_kernel(
    place, resets, x_ref, b_ref, decay_ref, total_ref, pay_ref, start_ref, log_ref, far_ref, span_ref, state, logs
):
    c = pl.program_id(0)
    base = place[0] * TOK_DEV

    @pl.when(c == 0)
    def _():
        state[...] = jnp.zeros_like(state)
        rows = jnp.concatenate(
            [decay_ref[:, k * CHUNK : (k + 1) * CHUNK] for k in range(CHUNKS)], axis=0
        )
        square = (CHUNK, CHUNK)
        upto = lax.broadcasted_iota(jnp.int32, square, 0) <= lax.broadcasted_iota(
            jnp.int32, square, 1
        )
        ones = upto.astype(F32).astype(BF16)
        high = rows.astype(BF16)
        rest = rows - high.astype(F32)
        middle = rest.astype(BF16)
        low = (rest - middle.astype(F32)).astype(BF16)
        sums = dot(high, ones) + dot(middle, ones) + dot(low, ones)
        before = jnp.zeros((HEADS, 1), F32)
        for k in range(CHUNKS):
            part = sums[k * HEADS : (k + 1) * HEADS]
            logs[k] = part
            log_ref[:, k * CHUNK : (k + 1) * CHUNK] = part
            position = base + k * CHUNK + lax.broadcasted_iota(jnp.int32, (HEADS, CHUNK), 1)
            far = jnp.exp(before + part)
            for r in range(RESETS):
                cut = (resets[r] >= base) & (position >= resets[r])
                far = jnp.where(cut, 0.0, far)
            far_ref[:, k * CHUNK : (k + 1) * CHUNK] = far
            before = before + part[:, CHUNK - 1 : CHUNK]
            if k == CHUNKS - 1:
                span_ref[...] = jnp.broadcast_to(far[:, CHUNK - 1 : CHUNK], (HEADS, STATE))

    log = logs[c]
    end = log[:, CHUNK - 1 : CHUNK]
    first = base + c * CHUNK
    last = first + CHUNK - 1
    position = first + lax.broadcasted_iota(jnp.int32, (HEADS, CHUNK), 1)
    weight = jnp.exp(end - log)
    kept = jnp.exp(end)
    for r in range(RESETS):
        weight = jnp.where((position < resets[r]) & (resets[r] <= last), 0.0, weight)
        kept = jnp.where((resets[r] >= first) & (resets[r] <= last), 0.0, kept)
    middle = jnp.exp(0.5 * end)
    b = b_ref[...]
    for pair in range(PAIRS):
        rows = slice(pair * WIDE, (pair + 1) * WIDE)
        held = state[rows, :]
        start_ref[0, rows, :] = (held * pair_column(middle, pair, STATE)).astype(BF16)
        flipped = x_ref[:, rows].T
        scaled = (flipped.astype(F32) * pair_rows(weight, pair)).astype(BF16)
        state[rows, :] = held * pair_column(kept, pair, STATE) + dot(scaled, b)

    @pl.when(c == CHUNKS - 1)
    def _():
        total = state[...]
        total_ref[...] = total
        pay_ref[:FEATURES, :] = total.astype(BF16)
        write_spans(pay_ref, FEATURES, span_ref[...])


def whole(shape):
    return pl.BlockSpec(shape, lambda *_: (0,) * len(shape))


SMEM = pl.BlockSpec(memory_space=pltpu.SMEM)


def block_states(place, resets, inputs, state_in, log_decay):
    return pl.pallas_call(
        state_kernel,
        grid=(CHUNKS,),
        in_specs=[
            SMEM,
            SMEM,
            pl.BlockSpec((CHUNK, FEATURES), lambda c: (c, 0)),
            pl.BlockSpec((CHUNK, STATE), lambda c: (c, 0)),
            whole((HEADS, TOK_DEV)),
        ],
        out_specs=[
            whole((FEATURES, STATE)),
            whole((FEATURES + SPAN_ROWS, STATE)),
            pl.BlockSpec((1, FEATURES, STATE), lambda c: (c, 0, 0)),
            whole((HEADS, TOK_DEV)),
            whole((HEADS, TOK_DEV)),
            whole((HEADS, STATE)),
        ],
        out_shape=[
            jax.ShapeDtypeStruct((FEATURES, STATE), F32),
            jax.ShapeDtypeStruct((FEATURES + SPAN_ROWS, STATE), BF16),
            jax.ShapeDtypeStruct((CHUNKS, FEATURES, STATE), BF16),
            jax.ShapeDtypeStruct((HEADS, TOK_DEV), F32),
            jax.ShapeDtypeStruct((HEADS, TOK_DEV), F32),
            jax.ShapeDtypeStruct((HEADS, STATE), F32),
        ],
        scratch_shapes=[
            pltpu.VMEM((FEATURES, STATE), F32),
            pltpu.VMEM((CHUNKS, HEADS, CHUNK), F32),
        ],
        compiler_params=pltpu.CompilerParams(**PARAMS),
        name="block_states",
    )(place, resets, inputs, state_in, log_decay)


def join_kernel(shift, first, place, own_ref, span_ref, lead_ref, got_ref, *outs):
    sum_ref, new_span_ref, new_lead_ref, factor_ref, pay_ref = outs
    core = place[1]
    upper = place[2 + shift] == 1
    top = FEATURES if first else HALF
    span = span_ref[...]
    got_span = read_spans(got_ref, top)
    lead = lead_ref[...]
    factor_ref[...] = jnp.where(upper, lead, 0.0)
    new_lead_ref[...] = jnp.where(upper, lead * got_span, lead)
    both = span * got_span
    new_span_ref[...] = both
    span_here = jnp.where(core == 0, span[: HEADS // 2], span[HEADS // 2 :])
    got_here = jnp.where(core == 0, got_span[: HEADS // 2], got_span[HEADS // 2 :])
    own_factor = jnp.where(upper, 1.0, got_here)
    got_factor = jnp.where(upper, span_here, 1.0)
    offset = core * HALF if first else 0
    for h in range(HEADS // 2):
        rows = pl.ds(pl.multiple_of(offset + h * HEAD_DIM, HEAD_DIM), HEAD_DIM)
        new = own_ref[rows, :] * own_factor[h : h + 1] + got_ref[rows, :].astype(F32) * got_factor[
            h : h + 1
        ]
        here = slice(h * HEAD_DIM, (h + 1) * HEAD_DIM)
        sum_ref[here, :] = new
        pay_ref[here, :] = new.astype(BF16)
    write_spans(pay_ref, HALF, both)


def join(shift, first, place, own, span, lead, got):
    small = jax.ShapeDtypeStruct((HEADS, STATE), F32)
    vmem = pl.BlockSpec(memory_space=pltpu.VMEM)
    return pl.pallas_call(
        functools.partial(join_kernel, shift, first),
        in_specs=[SMEM] + [vmem] * 4,
        out_specs=[vmem] * 5,
        out_shape=[
            jax.ShapeDtypeStruct((HALF, STATE), F32),
            small,
            small,
            small,
            jax.ShapeDtypeStruct((HALF + SPAN_ROWS, STATE), BF16),
        ],
        compiler_params=pltpu.CompilerParams(**PARAMS),
        name="join" + str(shift),
    )(place, own, span, lead, got)


def inner_kernel(
    chunk0, place, resets, skip, x_ref, b_ref, c_ref, log_ref, weight_ref, far_ref, start_ref, got_ref, factor_ref, *rest
):
    y_ref = rest[-1]
    first = place[0] * TOK_DEV + (pl.program_id(0) + chunk0) * CHUNK
    log = log_ref[...]
    middle = 0.5 * log[:, CHUNK - 1 : CHUNK]
    after = weight_ref[0] * jnp.exp(log - middle)
    before = jnp.exp(middle - log)
    level = weight_ref[1] * far_ref[...] * factor_ref[:, 0:1]
    square = (CHUNK, CHUNK)
    source = first + lax.broadcasted_iota(jnp.int32, square, 0)
    target = first + lax.broadcasted_iota(jnp.int32, square, 1)
    scores = dot_nt(b_ref[...], c_ref[...])
    scores = jnp.where(source <= target, scores, 0.0)
    row = first + lax.broadcasted_iota(jnp.int32, (CHUNK, STATE), 0)
    near = c_ref[...].astype(F32)
    for r in range(RESETS):
        scores = jnp.where((source < resets[r]) & (resets[r] <= target), 0.0, scores)
        near = jnp.where((resets[r] >= first) & (row >= resets[r]), 0.0, near)
    scores = scores.astype(BF16)
    near = near.astype(BF16)
    c = c_ref[...]
    for pair in range(PAIRS):
        rows = slice(pair * WIDE, (pair + 1) * WIDE)
        x = x_ref[:, rows].T.astype(F32)
        scaled = (x * pair_rows(before, pair)).astype(BF16)
        inside = dot(scaled, scores) + dot_nt(start_ref[0, rows, :], near)
        y = inside * pair_rows(after, pair)
        y = y + dot_nt(got_ref[rows, :], c) * pair_rows(level, pair)
        direct = jnp.concatenate(
            [x[:HEAD_DIM] * skip[2 * pair], x[HEAD_DIM:] * skip[2 * pair + 1]], axis=0
        )
        y_ref[0, rows, :] = y + direct


def inner(chunk0, count, place, resets, skip, inputs, state_in, state_out, log, level_weight, far, starts, got, factor, y):
    at = lambda c: (c + chunk0, 0)
    along = lambda c: (0, c + chunk0)
    operands = [place, resets, skip, inputs, state_in, state_out, log, level_weight, far, starts, got, factor]
    in_specs = [
        SMEM,
        SMEM,
        SMEM,
        pl.BlockSpec((CHUNK, FEATURES), at),
        pl.BlockSpec((CHUNK, STATE), at),
        pl.BlockSpec((CHUNK, STATE), at),
        pl.BlockSpec((HEADS, CHUNK), along),
        pl.BlockSpec((2, HEADS, CHUNK), lambda c: (0, 0, c + chunk0)),
        pl.BlockSpec((HEADS, CHUNK), along),
        pl.BlockSpec((1, FEATURES, STATE), lambda c: (c + chunk0, 0, 0)),
        whole((FEATURES + SPAN_ROWS, STATE)),
        whole((HEADS, STATE)),
    ]
    aliases = {}
    if y is not None:
        aliases = {len(operands): 0}
        operands.append(y)
        in_specs.append(pl.BlockSpec(memory_space=pl.ANY))
    return pl.pallas_call(
        functools.partial(inner_kernel, chunk0),
        grid=(count,),
        in_specs=in_specs,
        out_specs=pl.BlockSpec((1, FEATURES, CHUNK), lambda c: (c + chunk0, 0, 0)),
        out_shape=jax.ShapeDtypeStruct((CHUNKS, FEATURES, CHUNK), F32),
        input_output_aliases=aliases,
        compiler_params=pltpu.CompilerParams(**PARAMS),
        cost_estimate=pl.CostEstimate(
            flops=count * 2 * CHUNK * FEATURES * 512, bytes_accessed=count * 2_000_000, transcendentals=0
        ),
        name="inner" + str(chunk0),
    )(*operands)


def level_kernel(levels, final, place, c_ref, weight_ref, far_ref, *rest):
    count = len(levels)
    mine, other, factors = rest[:count], rest[count : 2 * count], rest[2 * count : 3 * count]
    y_in = rest[3 * count]
    y_ref = rest[3 * count + 1]
    states = rest[-1]

    @pl.when(pl.program_id(0) == 0)
    def _():
        for n in range(count):
            a, b = mine[n][:HALF, :], other[n][:HALF, :]

            @pl.when(place[1] == 0)
            def _():
                states[n, :HALF, :] = a
                states[n, HALF:, :] = b

            @pl.when(place[1] == 1)
            def _():
                states[n, :HALF, :] = b
                states[n, HALF:, :] = a

    far = far_ref[...]
    coefs = [weight_ref[levels[n]] * far * factors[n][:, 0:1] for n in range(count)]
    c = c_ref[...]
    squares = jnp.zeros((8, CHUNK), F32)
    for pair in range(PAIRS):
        rows = slice(pair * WIDE, (pair + 1) * WIDE)
        y = y_in[0, rows, :]
        for n in range(count):
            y = y + dot_nt(states[n, rows, :], c) * pair_rows(coefs[n], pair)
        y_ref[0, rows, :] = y
        if final:
            part = y * y
            for k in range(WIDE // 8):
                squares = squares + part[8 * k : 8 * k + 8]
    if final:
        rest[3 * count + 2][0] = jnp.sum(squares, axis=0, keepdims=True)


def add_levels(levels, final, place, state_out, level_weight, far, mine, other, factors, y):
    count = len(levels)
    along = lambda c: (0, c)
    block = pl.BlockSpec((1, FEATURES, CHUNK), lambda c: (c, 0, 0))
    out_specs = [block]
    out_shape = [jax.ShapeDtypeStruct((CHUNKS, FEATURES, CHUNK), F32)]
    if final:
        out_specs.append(pl.BlockSpec((1, 1, CHUNK), lambda c: (c, 0, 0)))
        out_shape.append(jax.ShapeDtypeStruct((CHUNKS, 1, CHUNK), F32))
    return pl.pallas_call(
        functools.partial(level_kernel, levels, final),
        grid=(CHUNKS,),
        in_specs=[
            SMEM,
            pl.BlockSpec((CHUNK, STATE), lambda c: (c, 0)),
            pl.BlockSpec((LEVELS, HEADS, CHUNK), lambda c: (0, 0, c)),
            pl.BlockSpec((HEADS, CHUNK), along),
        ]
        + [whole((HALF + SPAN_ROWS, STATE))] * (2 * count)
        + [whole((HEADS, STATE))] * count
        + [block],
        out_specs=out_specs,
        out_shape=out_shape,
        input_output_aliases={4 + 3 * count: 0},
        scratch_shapes=[pltpu.VMEM((count, FEATURES, STATE), BF16)],
        compiler_params=pltpu.CompilerParams(**PARAMS),
        cost_estimate=pl.CostEstimate(
            flops=count * 2 * TOK_DEV * FEATURES * STATE * 2, bytes_accessed=18_000_000, transcendentals=0
        ),
        name="levels" + str(levels[0]),
    )(place, state_out, level_weight, far, *mine, *other, *factors, y)


def norm_kernel(y_ref, s0, s1, s2, s3, gain_ref, out_ref):
    squares = (s0[0] + s1[0]) + (s2[0] + s3[0])
    scale = lax.rsqrt(squares * (1.0 / (HEAD_TOTAL * HEAD_DIM)) + EPSILON)
    for pair in range(PAIRS):
        rows = slice(pair * WIDE, (pair + 1) * WIDE)
        gain = gain_ref[rows, :]
        y = y_ref[0, rows, :] * scale * jnp.concatenate([gain, gain], axis=1)
        out_ref[:, rows] = y.astype(BF16).T


def normalize(y, squares, gain):
    part = pl.BlockSpec((1, 1, CHUNK), lambda c: (c, 0, 0))
    return pl.pallas_call(
        norm_kernel,
        grid=(CHUNKS,),
        in_specs=[pl.BlockSpec((1, FEATURES, CHUNK), lambda c: (c, 0, 0))]
        + [part] * 4
        + [whole((FEATURES, STATE))],
        out_specs=pl.BlockSpec((CHUNK, FEATURES), lambda c: (c, 0)),
        out_shape=jax.ShapeDtypeStruct((TOK_DEV, FEATURES), BF16),
        compiler_params=pltpu.CompilerParams(**PARAMS),
        name="normalize",
    )(y, *squares, gain)


def swap(array, axis, distance, only_up=None):
    count = lax.axis_size(axis)
    route = [
        (low, low ^ distance)
        for low in range(count)
        if only_up is None or not low >> only_up & 1
    ]
    return lax.ppermute(array, axis, route)


def per_device(inputs, state_in, state_out, log_decay, level_weight, skip, norm_gain, resets):
    index = lax.axis_index("seq").astype(jnp.int32)
    place = jnp.stack([index, index & 1] + [index >> bit & 1 for bit in range(6)])
    gain = jnp.broadcast_to(norm_gain[:, None], (FEATURES, STATE))
    total, pay, starts, log, far, span = block_states(place, resets, inputs, state_in, log_decay)
    lead = jnp.ones((HEADS, STATE), F32)
    got = swap(pay, "seq", 1)
    one = got
    group, span, lead, one_factor, pay = join(0, True, place, total, span, lead, got)
    mine, other, factors = [], [], []
    for distance, bit in STEPS:
        got = swap(pay, "seq", distance, bit if bit == 5 else None)
        mine.append(got)
        other.append(swap(got, "seq", 1))
        if bit < 5:
            group, span, lead, factor, pay = join(bit, False, place, group, span, lead, got)
            factors.append(factor)
        else:
            factors.append(jnp.where(index >> bit & 1 == 1, lead, 0.0))
    y = None
    for chunk in range(0, CHUNKS, PIECE):
        y = inner(
            chunk, PIECE, place, resets, skip, inputs, state_in, state_out, log, level_weight, far, starts, one, one_factor, y
        )
    (y,) = add_levels((2, 3, 4), False, place, state_out, level_weight, far, mine[:3], other[:3], factors[:3], y)
    y, squares = add_levels((5, 6), True, place, state_out, level_weight, far, mine[3:], other[3:], factors[3:], y)
    shares = [squares] + [
        lax.ppermute(squares, "head", [(i, i ^ d) for i in range(4)]) for d in (1, 3, 2)
    ]
    return normalize(y, shares, gain)


def solution(mesh):
    placed = (
        P("seq", "head"),
        P("seq", None),
        P("seq", None),
        P("head", "seq"),
        P(None, "head", "seq"),
        P("head"),
        P("head"),
        P(),
    )
    return jax.shard_map(
        per_device, mesh=mesh, in_specs=placed, out_specs=P("seq", "head"), check_vma=False
    )
```

time: 325 us -> 81 us (0.25)
  the two profiles are of different devices: /device:TPU:16 before, /device:TPU:24 now
where the time goes in v1:
time: 81 us; the launch traced here: 80.6 us
  Pallas kernels  32.1 us (40%)
  starting transfers between devices  19 us (23%)
  waiting for transfers between devices  17.5 us (22%)
  local copies, waits for them, and re-layouts  11.8 us (15%)
    ppermute x11, starting transfers between devices, swap(): return lax.ppermute(array, axis, route)  14.7 us
    ppermute x11, waiting for transfers between devices, swap(): return lax.ppermute(array, axis, route)  12.9 us
    unnamed x24, local copies, waits for them, and re-layouts  11.6 us
    pallas_call x2, Pallas kernels, add_levels(): pl.pallas_call(functools.partial(level_kernel, levels, final), grid=(CHUN...  10.5 us
    pallas_call x4, Pallas kernels, inner(): pl.pallas_call(functools.partial(inner_kernel, chunk0), grid=(count,), in...  9.28 us
    ppermute x3, waiting for transfers between devices, per_device(): lax.ppermute(squares, 'head', [(i, i ^ d) for i in range(4)])  4.52 us
    pallas_call x1, Pallas kernels, normalize(): pl.pallas_call(norm_kernel, grid=(CHUNKS,), in_specs=[pl.BlockSpec((1, FE...  4.34 us
    ppermute x3, starting transfers between devices, per_device(): lax.ppermute(squares, 'head', [(i, i ^ d) for i in range(4)])  4.31 us
  transfers between devices with their start and end apart: 14, of which 7 were waited for; matrix products, arithmetic and copies ran while one was open for 0% of the time, Pallas kernels for 21%

profile of v1, /device:TPU:24, one launch (start us, length us, event | category | flops | bytes accessed | tf_op | source)
XLA Modules:
  0.0 80.6 jit_solution(9009622505443546520)
XLA Ops:
  0.0 0.1 stack.35.place
  0.1 0.0 copy-start
  0.1 2.2 %copy-done = bf16[2048,1024]{1,0:T(8,128)(2,1)S(1)} copy-done((bf16[2048,1024]{1,0:T(8,128)(2,1)S(1)}, bf16[2048,1024]{1,0:T(8,128)(2,1)}, u32[]{:S(2)}) %copy-start) | copy-done | bytes 4194328
  2.3 0.0 copy-start.5
  2.3 1.0 %copy-done.5 = bf16[2048,128]{1,0:T(8,128)(2,1)S(1)} copy-done((bf16[2048,128]{1,0:T(8,128)(2,1)S(1)}, bf16[2048,128]{1,0:T(8,128)(2,1)}, u32[]{:S(2)}) %copy-start.5) | copy-done | bytes 524312
  3.3 0.0 copy-start.7
  3.3 0.9 %copy-done.7 = f32[16,2048]{1,0:T(8,128)S(1)} copy-done((f32[16,2048]{1,0:T(8,128)S(1)}, f32[16,2048]{1,0:T(8,128)}, u32[]{:S(2)}) %copy-start.7) | copy-done | bytes 131096
  4.2 0.0 copy-start.8
  4.2 0.7 copy-done.8
  4.9 4.3 %block_states.1 = (f32[1024,128]{1,0:T(8,128)S(1)}, bf16[1072,128]{1,0:T(8,128)(2,1)S(1)}, bf16[8,1024,128]{2,1,0:T(8,128)(2,1)S(1)}, f32[16,2048]{1,0:T(8,128)S...) custom-call(s32[8]{0:T(128)S(1)} %stack.35.place, s32[4]{0:T(128)S(1)} %copy-done.8, bf16[2048,1024]{1,0:T(8,128)(2,1)S(1)} %copy-done, ...), custom_call_target="tpu_custom_call" | custom-call | tf_op jit(solution)/shard_map/block_states/pallas_call | solution.py:149
  9.2 0.1 collective-permute-start
  9.3 1.5 %collective-permute-done.got_ref = bf16[1072,128]{1,0:T(8,128)(2,1)S(1)} collective-permute-done((bf16[1072,128]{1,0:T(8,128)(2,1)S(1)}, bf16[1072,128]{1,0:T(8,128)(2,1)S(1)}, u32[]{:S(2)}, u32[]{:S(2)}) %collective-permute-start) | collective-permute-done | bytes 274464 | tf_op jit(solution)/shard_map/ppermute | solution.py:410
  10.8 0.6 join0.1
  11.4 0.8 %collective-permute-start.1 = (bf16[560,128]{1,0:T(8,128)(2,1)S(1)}, bf16[560,128]{1,0:T(8,128)(2,1)S(1)}, u32[]{:S(2)}, u32[]{:S(2)}) collective-permute-start(bf16[560,128]{1,0:T(8,128)(2,1)S(1)} %get-tuple-element.43), channel_id=1, source_target_pairs={{0,8},{4,12},{8,0},{12,4},{16,24},{20,28},{24,16},{28,20},{32,40},... | collective-permute-start | bytes 430088 | tf_op jit(solution)/shard_map/ppermute | solution.py:410
  12.2 5.1 %collective-permute-done.1.got_ref.rest_0_ = bf16[560,128]{1,0:T(8,128)(2,1)S(1)} collective-permute-done((bf16[560,128]{1,0:T(8,128)(2,1)S(1)}, bf16[560,128]{1,0:T(8,128)(2,1)S(1)}, u32[]{:S(2)}, u32[]{:S(2)}) %collective-permute-start.1) | collective-permute-done | bytes 143392 | tf_op jit(solution)/shard_map/ppermute | solution.py:410
  17.3 0.6 join1.1
  17.9 2.0 %collective-permute-start.2 = (bf16[560,128]{1,0:T(8,128)(2,1)S(1)}, bf16[560,128]{1,0:T(8,128)(2,1)S(1)}, u32[]{:S(2)}, u32[]{:S(2)}) collective-permute-start(bf16[560,128]{1,0:T(8,128)(2,1)S(1)} %get-tuple-element.47), channel_id=1, source_target_pairs={{0,24},{4,28},{8,16},{12,20},{16,8},{20,12},{24,0},{28,4},{32,56},... | collective-permute-start | bytes 430088 | tf_op jit(solution)/shard_map/ppermute | solution.py:410
  19.9 4.4 %collective-permute-done.2.got_ref.rest_1_ = bf16[560,128]{1,0:T(8,128)(2,1)S(1)} collective-permute-done((bf16[560,128]{1,0:T(8,128)(2,1)S(1)}, bf16[560,128]{1,0:T(8,128)(2,1)S(1)}, u32[]{:S(2)}, u32[]{:S(2)}) %collective-permute-start.2) | collective-permute-done | bytes 143392 | tf_op jit(solution)/shard_map/ppermute | solution.py:410
  24.3 0.6 join2.1
  24.9 2.0 %collective-permute-start.3 = (bf16[560,128]{1,0:T(8,128)(2,1)S(1)}, bf16[560,128]{1,0:T(8,128)(2,1)S(1)}, u32[]{:S(2)}, u32[]{:S(2)}) collective-permute-start(bf16[560,128]{1,0:T(8,128)(2,1)S(1)} %get-tuple-element.51), channel_id=1, source_target_pairs={{0,32},{4,36},{8,40},{12,44},{16,48},{20,52},{24,56},{28,60},{32,0... | collective-permute-start | bytes 430088 | tf_op jit(solution)/shard_map/ppermute | solution.py:410
  26.9 0.0 copy-start.1
  26.9 2.2 %copy-done.1 = bf16[2048,1024]{1,0:T(8,128)(2,1)S(1)} copy-done((bf16[2048,1024]{1,0:T(8,128)(2,1)S(1)}, bf16[2048,1024]{1,0:T(8,128)(2,1)}, u32[]{:S(2)}) %copy-start.1) | copy-done | bytes 4194328
  29.1 0.0 copy-start.3
  29.1 1.2 %copy-done.3 = f32[7,16,2048]{2,1,0:T(8,128)S(1)} copy-done((f32[7,16,2048]{2,1,0:T(8,128)S(1)}, f32[7,16,2048]{2,1,0:T(8,128)}, u32[]{:S(2)}) %copy-start.3) | copy-done | bytes 917528
  30.3 0.0 copy-start.4
  30.3 1.0 %copy-done.4 = bf16[2048,128]{1,0:T(8,128)(2,1)S(1)} copy-done((bf16[2048,128]{1,0:T(8,128)(2,1)S(1)}, bf16[2048,128]{1,0:T(8,128)(2,1)}, u32[]{:S(2)}) %copy-start.4) | copy-done | bytes 524312
  31.3 0.0 copy-start.6
  31.3 1.0 %copy-done.6 = bf16[2048,128]{1,0:T(8,128)(2,1)S(1)} copy-done((bf16[2048,128]{1,0:T(8,128)(2,1)S(1)}, bf16[2048,128]{1,0:T(8,128)(2,1)}, u32[]{:S(2)}) %copy-start.6) | copy-done | bytes 524312
  32.4 0.7 copy-done.9
  33.0 0.7 copy-done.10
  33.7 2.3 %inner0.1.rest_0_ = f32[8,1024,256]{2,1,0:T(8,128)S(1)} custom-call(s32[8]{0:T(128)S(1)} %stack.35.place, s32[4]{0:T(128)S(1)} %copy-done.9, f32[16]{0:T(128)S(1)} %copy-done.10, bf16[2048,1024]{1,0:T(8,128)(2,1)S(1)} %copy-done.1, bf16[2048,128]{1,0:T(8,128)(2,1)S(1)} %copy-done.6, bf16[2048,128]{1,0:T(8,128)(2,1)S(1)} %copy-done.4, ...), custom_call_target="tpu_custom_call" | custom-call | flops 536870912 | bytes 4000000 | tf_op jit(solution)/shard_map/inner0/pallas_call | solution.py:290
  36.0 0.1 collective-permute-start.8
  36.1 0.5 collective-permute-start.9
  36.6 0.0 collective-permute-done.3.got_ref.rest_2_
  36.6 0.6 join3.1
  37.2 3.4 %collective-permute-start.4 = (bf16[560,128]{1,0:T(8,128)(2,1)S(1)}, bf16[560,128]{1,0:T(8,128)(2,1)S(1)}, u32[]{:S(2)}, u32[]{:S(2)}) collective-permute-start(bf16[560,128]{1,0:T(8,128)(2,1)S(1)} %get-tuple-element.52), channel_id=1, source_target_pairs={{0,64},{4,68},{8,72},{12,76},{16,80},{20,84},{24,88},{28,92},{32,9... | collective-permute-start | bytes 430088 | tf_op jit(solution)/shard_map/ppermute | solution.py:410
  40.5 0.0 collective-permute-start.10
  40.5 0.0 copy-done.2
  40.5 2.3 %inner2.1.rest_0_ = f32[8,1024,256]{2,1,0:T(8,128)S(1)} custom-call(s32[8]{0:T(128)S(1)} %stack.35.place, s32[4]{0:T(128)S(1)} %copy-done.9, f32[16]{0:T(128)S(1)} %copy-done.10, bf16[2048,1024]{1,0:T(8,128)(2,1)S(1)} %copy-done.2, bf16[2048,128]{1,0:T(8,128)(2,1)S(1)} %copy-done.6, ...), custom_call_target="tpu_custom_call", output_to_operand_aliasing={{}: (12, {})} | custom-call | flops 536870912 | bytes 4000000 | tf_op jit(solution)/shard_map/inner2/pallas_call | solution.py:290
  42.9 2.3 %inner4.1.rest_0_ = f32[8,1024,256]{2,1,0:T(8,128)S(1)} custom-call(s32[8]{0:T(128)S(1)} %stack.35.place, s32[4]{0:T(128)S(1)} %copy-done.9, f32[16]{0:T(128)S(1)} %copy-done.10, bf16[2048,1024]{1,0:T(8,128)(2,1)S(1)} %copy-done.2, bf16[2048,128]{1,0:T(8,128)(2,1)S(1)} %copy-done.6, ...), custom_call_target="tpu_custom_call", output_to_operand_aliasing={{}: (12, {})} | custom-call | flops 536870912 | bytes 4000000 | tf_op jit(solution)/shard_map/inner4/pallas_call | solution.py:290
  45.2 2.3 %inner6.1.rest_9_ = f32[8,1024,256]{2,1,0:T(8,128)S(1)} custom-call(s32[8]{0:T(128)S(1)} %stack.35.place, s32[4]{0:T(128)S(1)} %copy-done.9, f32[16]{0:T(128)S(1)} %copy-done.10, bf16[2048,1024]{1,0:T(8,128)(2,1)S(1)} %copy-done.2, bf16[2048,128]{1,0:T(8,128)(2,1)S(1)} %copy-done.6, ...), custom_call_target="tpu_custom_call", output_to_operand_aliasing={{}: (12, {})} | custom-call | flops 536870912 | bytes 4000000 | tf_op jit(solution)/shard_map/inner6/pallas_call | solution.py:290
  47.5 0.0 collective-permute-done.4.got_ref.rest_0_
  47.6 1.3 %join4.1 = (f32[512,128]{1,0:T(8,128)}, f32[16,128]{1,0:T(8,128)}, f32[16,128]{1,0:T(8,128)S(1)}, f32[16,128]{1,0:T(8,128)S(1)}, bf16[560,128]{1,0:T(8,128)(2,1)S(1)}) custom-call(s32[8]{0:T(128)S(1)} %stack.35.place, f32[512,128]{1,0:T(8,128)S(1)} %get-tuple-element.53.own_ref, f32[16,128]{1,0:T(8,128)S(1)} %get-tuple-element.54.span_ref, ...), custom_call_target="tpu_custom_call" | custom-call | tf_op jit(solution)/shard_map/join4/pallas_call | solution.py:215
  48.9 5.5 %collective-permute-start.5 = (bf16[560,128]{1,0:T(8,128)(2,1)S(1)}, bf16[560,128]{1,0:T(8,128)(2,1)S(1)}, u32[]{:S(2)}, u32[]{:S(2)}) collective-permute-start(bf16[560,128]{1,0:T(8,128)(2,1)S(1)} %get-tuple-element.56), channel_id=1, source_target_pairs={{0,192},{4,196},{8,200},{12,204},{16,208},{20,212},{24,216},{28,22... | collective-permute-start | bytes 430088 | tf_op jit(solution)/shard_map/ppermute | solution.py:410
  54.3 0.3 collective-permute-start.6
  54.7 0.0 collective-permute-done.8.rest_3_
  54.7 0.0 collective-permute-done.9.rest_4_
  54.7 0.0 collective-permute-done.10.rest_5_
  54.7 5.8 %levels2.1.rest_6_ = f32[8,1024,256]{2,1,0:T(8,128)S(1)} custom-call(s32[8]{0:T(128)S(1)} %stack.35.place, bf16[2048,128]{1,0:T(8,128)(2,1)S(1)} %copy-done.4, f32[7,16,2048]{2,1,0:T(8,128)S(1)} %copy-done.3, f32[16,2048]{1,0:T(8,128)S(1)} %get-tuple-element.36.far_ref, ...), custom_call_target="tpu_custom_call", output_to_operand_aliasing={{}: (13, {})} | custom-call | flops 3221225472 | bytes 18000000 | tf_op jit(solution)/shard_map/levels2/pallas_call | solution.py:354
  60.4 0.0 copy-start.11
  60.4 0.6 collective-permute-done.5.rest_1_
  61.1 0.0 collective-permute-start.7
  61.1 0.0 collective-permute-done.6.rest_2_
  61.1 1.4 %collective-permute-done.7.rest_3_ = bf16[560,128]{1,0:T(8,128)(2,1)S(1)} collective-permute-done((bf16[560,128]{1,0:T(8,128)(2,1)S(1)}, bf16[560,128]{1,0:T(8,128)(2,1)S(1)}, u32[]{:S(2)}, u32[]{:S(2)}) %collective-permute-start.7) | collective-permute-done | bytes 143392 | tf_op jit(solution)/shard_map/ppermute | solution.py:410
  62.4 4.8 %levels5.1 = (f32[8,1024,256]{2,1,0:T(8,128)S(1)}, f32[8,1,256]{2,1,0:T(1,128)S(1)}) custom-call(s32[8]{0:T(128)S(1)} %stack.35.place, bf16[2048,128]{1,0:T(8,128)(2,1)S(1)} %copy-done.4, f32[7,16,2048]{2,1,0:T(8,128)S(1)} %copy-done.3, f32[16,2048]{1,0:T(8,128)S(1)} %get-tuple-element.36.far_ref, ...), custom_call_target="tpu_custom_call", output_to_operand_aliasing={{0}: (10, {})} | custom-call | flops 2147483648 | bytes 18000000 | tf_op jit(solution)/shard_map/levels5/pallas_call | solution.py:354
  67.2 1.5 %collective-permute-start.11 = (f32[8,1,256]{2,1,0:T(1,128)S(1)}, f32[8,1,256]{2,1,0:T(1,128)S(1)}, u32[]{:S(2)}, u32[]{:S(2)}) collective-permute-start(f32[8,1,256]{2,1,0:T(1,128)S(1)} %get-tuple-element.66.s0), channel_id=1, source_target_pairs={{0,1},{1,0},{2,3},{3,2},{4,5},{5,4},{6,7},{7,6},{8,9},{9,8},{10,11... | collective-permute-start | bytes 24584 | tf_op jit(solution)/shard_map/ppermute | solution.py:440
  68.7 2.2 %collective-permute-start.12 = (f32[8,1,256]{2,1,0:T(1,128)S(1)}, f32[8,1,256]{2,1,0:T(1,128)S(1)}, u32[]{:S(2)}, u32[]{:S(2)}) collective-permute-start(f32[8,1,256]{2,1,0:T(1,128)S(1)} %get-tuple-element.66.s0), channel_id=1, source_target_pairs={{0,3},{1,2},{2,1},{3,0},{4,7},{5,6},{6,5},{7,4},{8,11},{9,10},{10,... | collective-permute-start | bytes 24584 | tf_op jit(solution)/shard_map/ppermute | solution.py:440
  70.9 0.6 collective-permute-start.13
  71.5 0.0 collective-permute-done.11.s1
  71.5 2.0 %collective-permute-done.12.s2 = f32[8,1,256]{2,1,0:T(1,128)S(1)} collective-permute-done((f32[8,1,256]{2,1,0:T(1,128)S(1)}, f32[8,1,256]{2,1,0:T(1,128)S(1)}, u32[]{:S(2)}, u32[]{:S(2)}) %collective-permute-start.12) | collective-permute-done | bytes 8224 | tf_op jit(solution)/shard_map/ppermute | solution.py:440
  73.5 2.5 %collective-permute-done.13.s3 = f32[8,1,256]{2,1,0:T(1,128)S(1)} collective-permute-done((f32[8,1,256]{2,1,0:T(1,128)S(1)}, f32[8,1,256]{2,1,0:T(1,128)S(1)}, u32[]{:S(2)}, u32[]{:S(2)}) %collective-permute-start.13) | collective-permute-done | bytes 8224 | tf_op jit(solution)/shard_map/ppermute | solution.py:440
  76.1 0.0 copy-done.11
  76.1 0.2 broadcast_in_dim.15.gain_ref
  76.2 4.3 %normalize.1 = bf16[2048,1024]{1,0:T(8,128)(2,1)} custom-call(f32[8,1024,256]{2,1,0:T(8,128)S(1)} %get-tuple-element.65.y_ref, f32[8,1,256]{2,1,0:T(1,128)S(1)} %get-tuple-element.66.s0, f32[8,1,256]{2,1,0:T(1,128)S(1)} %collective-permute-done.11.s1, f32[8,1,256]{2,1,0:T(1,128)S(1)} %collective-permute-done.12.s2, ...), custom_call_target="tpu_custom_call" | custom-call | tf_op jit(solution)/shard_map/normalize/pallas_call | solution.py:390
  (5 shorter events, 0.0 us)
Async XLA Ops:
  0.1 2.2 %copy-start = (bf16[2048,1024]{1,0:T(8,128)(2,1)S(1)}, bf16[2048,1024]{1,0:T(8,128)(2,1)}, u32[]{:S(2)}) copy-start(bf16[2048,1024]{1,0:T(8,128)(2,1)} %x_ref.9) | copy-start | bytes 12582916
  2.3 1.0 %copy-start.5 = (bf16[2048,128]{1,0:T(8,128)(2,1)S(1)}, bf16[2048,128]{1,0:T(8,128)(2,1)}, u32[]{:S(2)}) copy-start(bf16[2048,128]{1,0:T(8,128)(2,1)} %b_ref.9) | copy-start | bytes 1572868
  3.3 0.9 %copy-start.7 = (f32[16,2048]{1,0:T(8,128)S(1)}, f32[16,2048]{1,0:T(8,128)}, u32[]{:S(2)}) copy-start(f32[16,2048]{1,0:T(8,128)} %decay_ref.1) | copy-start | bytes 393220
  4.2 0.7 copy-start.8
  9.2 1.6 %collective-permute-start = (bf16[1072,128]{1,0:T(8,128)(2,1)S(1)}, bf16[1072,128]{1,0:T(8,128)(2,1)S(1)}, u32[]{:S(2)}, u32[]{:S(2)}) collective-permute-start(bf16[1072,128]{1,0:T(8,128)(2,1)S(1)} %get-tuple-element.39), channel_id=1, source_target_pairs={{0,4},{4,0},{8,12},{12,8},{16,20},{20,16},{24,28},{28,24},{32,36},... | collective-permute-start | bytes 823304 | tf_op jit(solution)/shard_map/ppermute | solution.py:410
  11.4 5.9 %collective-permute-start.1 = (bf16[560,128]{1,0:T(8,128)(2,1)S(1)}, bf16[560,128]{1,0:T(8,128)(2,1)S(1)}, u32[]{:S(2)}, u32[]{:S(2)}) collective-permute-start(bf16[560,128]{1,0:T(8,128)(2,1)S(1)} %get-tuple-element.43), channel_id=1, source_target_pairs={{0,8},{4,12},{8,0},{12,4},{16,24},{20,28},{24,16},{28,20},{32,40},... | collective-permute-start | bytes 430088 | tf_op jit(solution)/shard_map/ppermute | solution.py:410
  17.9 6.4 %collective-permute-start.2 = (bf16[560,128]{1,0:T(8,128)(2,1)S(1)}, bf16[560,128]{1,0:T(8,128)(2,1)S(1)}, u32[]{:S(2)}, u32[]{:S(2)}) collective-permute-start(bf16[560,128]{1,0:T(8,128)(2,1)S(1)} %get-tuple-element.47), channel_id=1, source_target_pairs={{0,24},{4,28},{8,16},{12,20},{16,8},{20,12},{24,0},{28,4},{32,56},... | collective-permute-start | bytes 430088 | tf_op jit(solution)/shard_map/ppermute | solution.py:410
  24.9 11.7 %collective-permute-start.3 = (bf16[560,128]{1,0:T(8,128)(2,1)S(1)}, bf16[560,128]{1,0:T(8,128)(2,1)S(1)}, u32[]{:S(2)}, u32[]{:S(2)}) collective-permute-start(bf16[560,128]{1,0:T(8,128)(2,1)S(1)} %get-tuple-element.51), channel_id=1, source_target_pairs={{0,32},{4,36},{8,40},{12,44},{16,48},{20,52},{24,56},{28,60},{32,0... | collective-permute-start | bytes 430088 | tf_op jit(solution)/shard_map/ppermute | solution.py:410
  26.9 2.2 %copy-start.1 = (bf16[2048,1024]{1,0:T(8,128)(2,1)S(1)}, bf16[2048,1024]{1,0:T(8,128)(2,1)}, u32[]{:S(2)}) copy-start(bf16[2048,1024]{1,0:T(8,128)(2,1)} %x_ref.9) | copy-start | bytes 12582916
  29.1 1.2 %copy-start.3 = (f32[7,16,2048]{2,1,0:T(8,128)S(1)}, f32[7,16,2048]{2,1,0:T(8,128)}, u32[]{:S(2)}) copy-start(f32[7,16,2048]{2,1,0:T(8,128)} %weight_ref.11) | copy-start | bytes 2752516
  30.3 1.0 %copy-start.4 = (bf16[2048,128]{1,0:T(8,128)(2,1)S(1)}, bf16[2048,128]{1,0:T(8,128)(2,1)}, u32[]{:S(2)}) copy-start(bf16[2048,128]{1,0:T(8,128)(2,1)} %c_ref.11) | copy-start | bytes 1572868
  31.3 1.0 %copy-start.6 = (bf16[2048,128]{1,0:T(8,128)(2,1)S(1)}, bf16[2048,128]{1,0:T(8,128)(2,1)}, u32[]{:S(2)}) copy-start(bf16[2048,128]{1,0:T(8,128)(2,1)} %b_ref.9) | copy-start | bytes 1572868
  32.4 0.7 copy-start.9
  33.0 0.7 copy-start.10
  33.7 6.9 %copy-start.2 = (bf16[2048,1024]{1,0:T(8,128)(2,1)S(1)}, bf16[2048,1024]{1,0:T(8,128)(2,1)}, u32[]{:S(2)}) copy-start(bf16[2048,1024]{1,0:T(8,128)(2,1)} %x_ref.9) | copy-start | bytes 12582916
  36.0 18.7 %collective-permute-start.8 = (bf16[560,128]{1,0:T(8,128)(2,1)S(1)}, bf16[560,128]{1,0:T(8,128)(2,1)S(1)}, u32[]{:S(2)}, u32[]{:S(2)}) collective-permute-start(bf16[560,128]{1,0:T(8,128)(2,1)S(1)} %collective-permute-done.1.got_ref.rest_0_), channel_id=1, source_target_pairs={{0,4},{4,0},{8,12},{12,8},{16,20},{20,16},{24,28},{28,24},{32,36},... | collective-permute-start | bytes 430088 | tf_op jit(solution)/shard_map/ppermute | solution.py:410
  36.1 18.6 %collective-permute-start.9 = (bf16[560,128]{1,0:T(8,128)(2,1)S(1)}, bf16[560,128]{1,0:T(8,128)(2,1)S(1)}, u32[]{:S(2)}, u32[]{:S(2)}) collective-permute-start(bf16[560,128]{1,0:T(8,128)(2,1)S(1)} %collective-permute-done.2.got_ref.rest_1_), channel_id=1, source_target_pairs={{0,4},{4,0},{8,12},{12,8},{16,20},{20,16},{24,28},{28,24},{32,36},... | collective-permute-start | bytes 430088 | tf_op jit(solution)/shard_map/ppermute | solution.py:410
  37.2 10.4 %collective-permute-start.4 = (bf16[560,128]{1,0:T(8,128)(2,1)S(1)}, bf16[560,128]{1,0:T(8,128)(2,1)S(1)}, u32[]{:S(2)}, u32[]{:S(2)}) collective-permute-start(bf16[560,128]{1,0:T(8,128)(2,1)S(1)} %get-tuple-element.52), channel_id=1, source_target_pairs={{0,64},{4,68},{8,72},{12,76},{16,80},{20,84},{24,88},{28,92},{32,9... | collective-permute-start | bytes 430088 | tf_op jit(solution)/shard_map/ppermute | solution.py:410
  40.5 14.1 %collective-permute-start.10 = (bf16[560,128]{1,0:T(8,128)(2,1)S(1)}, bf16[560,128]{1,0:T(8,128)(2,1)S(1)}, u32[]{:S(2)}, u32[]{:S(2)}) collective-permute-start(bf16[560,128]{1,0:T(8,128)(2,1)S(1)} %collective-permute-done.3.got_ref.rest_2_), channel_id=1, source_target_pairs={{0,4},{4,0},{8,12},{12,8},{16,20},{20,16},{24,28},{28,24},{32,36},... | collective-permute-start | bytes 430088 | tf_op jit(solution)/shard_map/ppermute | solution.py:410
  48.9 12.2 %collective-permute-start.5 = (bf16[560,128]{1,0:T(8,128)(2,1)S(1)}, bf16[560,128]{1,0:T(8,128)(2,1)S(1)}, u32[]{:S(2)}, u32[]{:S(2)}) collective-permute-start(bf16[560,128]{1,0:T(8,128)(2,1)S(1)} %get-tuple-element.56), channel_id=1, source_target_pairs={{0,192},{4,196},{8,200},{12,204},{16,208},{20,212},{24,216},{28,22... | collective-permute-start | bytes 430088 | tf_op jit(solution)/shard_map/ppermute | solution.py:410
  54.3 6.7 %collective-permute-start.6 = (bf16[560,128]{1,0:T(8,128)(2,1)S(1)}, bf16[560,128]{1,0:T(8,128)(2,1)S(1)}, u32[]{:S(2)}, u32[]{:S(2)}) collective-permute-start(bf16[560,128]{1,0:T(8,128)(2,1)S(1)} %collective-permute-done.4.got_ref.rest_0_), channel_id=1, source_target_pairs={{0,4},{4,0},{8,12},{12,8},{16,20},{20,16},{24,28},{28,24},{32,36},... | collective-permute-start | bytes 430088 | tf_op jit(solution)/shard_map/ppermute | solution.py:410
  60.4 15.6 %copy-start.11 = (f32[1024]{0:T(1024)S(1)}, f32[1024]{0:T(1024)}, u32[]{:S(2)}) copy-start(f32[1024]{0:T(1024)} %param.14) | copy-start | bytes 12292
  61.1 1.4 %collective-permute-start.7 = (bf16[560,128]{1,0:T(8,128)(2,1)S(1)}, bf16[560,128]{1,0:T(8,128)(2,1)S(1)}, u32[]{:S(2)}, u32[]{:S(2)}) collective-permute-start(bf16[560,128]{1,0:T(8,128)(2,1)S(1)} %collective-permute-done.5.rest_1_), channel_id=1, source_target_pairs={{0,4},{4,0},{8,12},{12,8},{16,20},{20,16},{24,28},{28,24},{32,36},... | collective-permute-start | bytes 430088 | tf_op jit(solution)/shard_map/ppermute | solution.py:410
  67.2 4.3 %collective-permute-start.11 = (f32[8,1,256]{2,1,0:T(1,128)S(1)}, f32[8,1,256]{2,1,0:T(1,128)S(1)}, u32[]{:S(2)}, u32[]{:S(2)}) collective-permute-start(f32[8,1,256]{2,1,0:T(1,128)S(1)} %get-tuple-element.66.s0), channel_id=1, source_target_pairs={{0,1},{1,0},{2,3},{3,2},{4,5},{5,4},{6,7},{7,6},{8,9},{9,8},{10,11... | collective-permute-start | bytes 24584 | tf_op jit(solution)/shard_map/ppermute | solution.py:440
  68.7 4.9 %collective-permute-start.12 = (f32[8,1,256]{2,1,0:T(1,128)S(1)}, f32[8,1,256]{2,1,0:T(1,128)S(1)}, u32[]{:S(2)}, u32[]{:S(2)}) collective-permute-start(f32[8,1,256]{2,1,0:T(1,128)S(1)} %get-tuple-element.66.s0), channel_id=1, source_target_pairs={{0,3},{1,2},{2,1},{3,0},{4,7},{5,6},{6,5},{7,4},{8,11},{9,10},{10,... | collective-permute-start | bytes 24584 | tf_op jit(solution)/shard_map/ppermute | solution.py:440
  70.9 5.2 %collective-permute-start.13 = (f32[8,1,256]{2,1,0:T(1,128)S(1)}, f32[8,1,256]{2,1,0:T(1,128)S(1)}, u32[]{:S(2)}, u32[]{:S(2)}) collective-permute-start(f32[8,1,256]{2,1,0:T(1,128)S(1)} %get-tuple-element.66.s0), channel_id=1, source_target_pairs={{0,2},{1,3},{2,0},{3,1},{4,6},{5,7},{6,4},{7,5},{8,10},{9,11},{10,... | collective-permute-start | bytes 24584 | tf_op jit(solution)/shard_map/ppermute | solution.py:440

commit v2 on v0

v2 whole, which is shorter than its diff:
```python
import functools

import jax
import jax.numpy as jnp
from jax import lax
from jax.experimental import pallas as pl
from jax.experimental.pallas import tpu as pltpu
from jax.sharding import PartitionSpec as P

HEAD_TOTAL = 64
HEAD_DIM = 64
STATE = 128
LEVELS = 7
TOK_DEV = 2048
EPSILON = 1e-05

CHUNK = 256
CHUNKS = TOK_DEV // CHUNK
HEADS = 16
FEATURES = HEADS * HEAD_DIM
HALF = FEATURES // 2
HALF_HEADS = HEADS // 2
GROUP_HEADS = 8
WIDE = GROUP_HEADS * HEAD_DIM
GROUPS = HEADS // GROUP_HEADS
SPAN_ROWS = HEADS
RESETS = 4
PIECE = 2

F32 = jnp.float32
BF16 = jnp.bfloat16
PARAMS = dict(vmem_limit_bytes=16 * 1024 * 1024)
SMEM = pl.BlockSpec(memory_space=pltpu.SMEM)
VMEM = pl.BlockSpec(memory_space=pltpu.VMEM)
ANY = pl.BlockSpec(memory_space=pl.ANY)


def side(bit):
    return lax.axis_index("seq") >> bit & 1


def in_hbm(array):
    return pltpu.with_memory_space_constraint(array, pltpu.HBM)


def dot(a, b):
    return lax.dot_general(a, b, (((1,), (0,)), ((), ())), preferred_element_type=F32)


def dot_nt(a, b):
    return lax.dot_general(a, b, (((1,), (1,)), ((), ())), preferred_element_type=F32)


def head_rows(values, group):
    width = values.shape[1]
    heads = range(group * GROUP_HEADS, (group + 1) * GROUP_HEADS)
    return jnp.concatenate(
        [jnp.broadcast_to(values[h : h + 1, :], (HEAD_DIM, width)) for h in heads], axis=0
    )


def head_column(values, group, width):
    heads = range(group * GROUP_HEADS, (group + 1) * GROUP_HEADS)
    return jnp.concatenate(
        [jnp.broadcast_to(values[h : h + 1, 0:1], (HEAD_DIM, width)) for h in heads], axis=0
    )


def write_spans(ref, first, span):
    high = span.astype(BF16).astype(F32)
    middle = (span - high).astype(BF16).astype(F32)
    low = span - high - middle
    lane = lax.broadcasted_iota(jnp.int32, span.shape, 1)
    parts = jnp.where(lane < 32, high, jnp.where(lane < 64, middle, low))
    ref[first : first + SPAN_ROWS, :] = parts.astype(BF16)


def read_spans(ref, first):
    parts = ref[first : first + SPAN_ROWS, :].astype(F32)
    span = parts[:, 0:1] + parts[:, 32:33] + parts[:, 64:65]
    return jnp.broadcast_to(span, (HEADS, STATE))


def state_kernel(listed, x_any, b_any, c_any, decay_any, weight_any, *rest):
    total_ref, pay_ref, start_ref, log_ref, far_ref, span_ref, x_ref, b_ref, c_ref, weight_ref = rest[:10]
    x_in, decay_ref, state, sems, x_sems = rest[10:]
    base = lax.axis_index("seq") * TOK_DEV
    resets = [listed[r] for r in range(RESETS)]
    decay_copy = pltpu.make_async_copy(decay_any, decay_ref, sems.at[0])
    b_copy = pltpu.make_async_copy(b_any, b_ref, sems.at[1])
    later = [
        pltpu.make_async_copy(c_any, c_ref, sems.at[2]),
        pltpu.make_async_copy(weight_any, weight_ref, sems.at[3]),
    ]
    x_copies = []
    for k in range(CHUNKS):
        rows = slice(k * CHUNK, (k + 1) * CHUNK)
        x_copies.append(pltpu.make_async_copy(x_any.at[rows, :], x_in.at[k], x_sems.at[k]))
    for copy in [decay_copy, b_copy] + x_copies + later:
        copy.start()
    state[...] = jnp.zeros_like(state)
    square = (CHUNK, CHUNK)
    upto = lax.broadcasted_iota(jnp.int32, square, 0) <= lax.broadcasted_iota(
        jnp.int32, square, 1
    )
    ones = upto.astype(F32).astype(BF16)
    decay_copy.wait()
    rows = jnp.concatenate(
        [decay_ref[:, k * CHUNK : (k + 1) * CHUNK] for k in range(CHUNKS)], axis=0
    )
    high = rows.astype(BF16)
    rest_of = rows - high.astype(F32)
    middle = rest_of.astype(BF16)
    low = (rest_of - middle.astype(F32)).astype(BF16)
    sums = dot(high, ones) + dot(middle, ones) + dot(low, ones)
    before = jnp.zeros((HEADS, 1), F32)
    b_copy.wait()
    for k in range(CHUNKS):
        log = sums[k * HEADS : (k + 1) * HEADS]
        lanes = slice(k * CHUNK, (k + 1) * CHUNK)
        end = log[:, CHUNK - 1 : CHUNK]
        first = base + k * CHUNK
        last = first + CHUNK - 1
        position = first + lax.broadcasted_iota(jnp.int32, (HEADS, CHUNK), 1)
        weight = jnp.exp(end - log)
        kept = jnp.exp(end)
        far = jnp.exp(before + log)
        for reset in resets:
            weight = jnp.where((position < reset) & (reset <= last), 0.0, weight)
            kept = jnp.where((reset >= first) & (reset <= last), 0.0, kept)
            far = jnp.where((reset >= base) & (position >= reset), 0.0, far)
        log_ref[:, lanes] = log
        far_ref[:, lanes] = far
        before = before + end
        if k == CHUNKS - 1:
            span_ref[...] = jnp.broadcast_to(far[:, CHUNK - 1 : CHUNK], (HEADS, STATE))
        middle = jnp.exp(0.5 * end)
        b = b_ref[lanes, :]
        x_copies[k].wait()
        for group in range(GROUPS):
            rows = slice(group * WIDE, (group + 1) * WIDE)
            held = state[rows, :]
            start_ref[k, rows, :] = (held * head_column(middle, group, STATE)).astype(BF16)
            x = x_in[k, :, rows].T
            x_ref[k, rows, :] = x
            scaled = (x.astype(F32) * head_rows(weight, group)).astype(BF16)
            state[rows, :] = held * head_column(kept, group, STATE) + dot(scaled, b)
    total = state[...]
    total_ref[...] = total
    pay_ref[:FEATURES, :] = total.astype(BF16)
    write_spans(pay_ref, FEATURES, span_ref[...])
    for copy in later:
        copy.wait()


def block_states(resets, inputs, state_in, state_out, log_decay, level_weight):
    return pl.pallas_call(
        state_kernel,
        in_specs=[SMEM] + [ANY] * 5,
        out_specs=[VMEM] * 10,
        out_shape=[
            jax.ShapeDtypeStruct((FEATURES, STATE), F32),
            jax.ShapeDtypeStruct((FEATURES + SPAN_ROWS, STATE), BF16),
            jax.ShapeDtypeStruct((CHUNKS, FEATURES, STATE), BF16),
            jax.ShapeDtypeStruct((HEADS, TOK_DEV), F32),
            jax.ShapeDtypeStruct((HEADS, TOK_DEV), F32),
            jax.ShapeDtypeStruct((HEADS, STATE), F32),
            jax.ShapeDtypeStruct((CHUNKS, FEATURES, CHUNK), BF16),
            jax.ShapeDtypeStruct((TOK_DEV, STATE), BF16),
            jax.ShapeDtypeStruct((TOK_DEV, STATE), BF16),
            jax.ShapeDtypeStruct((LEVELS, HEADS, TOK_DEV), F32),
        ],
        scratch_shapes=[
            pltpu.VMEM((CHUNKS, CHUNK, FEATURES), BF16),
            pltpu.VMEM((HEADS, TOK_DEV), F32),
            pltpu.VMEM((FEATURES, STATE), F32),
            pltpu.SemaphoreType.DMA((4,)),
            pltpu.SemaphoreType.DMA((CHUNKS,)),
        ],
        compiler_params=pltpu.CompilerParams(**PARAMS),
        name="block_states",
    )(
        in_hbm(resets),
        in_hbm(inputs),
        in_hbm(state_in),
        in_hbm(state_out),
        in_hbm(log_decay),
        in_hbm(level_weight),
    )


def own_heads(span):
    return jnp.where(side(0) == 0, span[:HALF_HEADS], span[HALF_HEADS:])


def join_kernel(bit, own_ref, span_ref, *rest):
    *lead_ref, got_ref = rest[:-5]
    sum_ref, new_span_ref, new_lead_ref, factor_ref, pay_ref = rest[-5:]
    upper = side(bit) == 1
    first = bit == 0
    span = span_ref[...]
    lead = jnp.ones_like(span) if first else lead_ref[0][...]
    got_span = read_spans(got_ref, FEATURES if first else HALF)
    factor_ref[...] = jnp.where(upper, lead, 0.0)
    new_lead_ref[...] = jnp.where(upper, lead * got_span, lead)
    both = span * got_span
    new_span_ref[...] = both
    own_factor = jnp.where(upper, 1.0, own_heads(got_span))
    got_factor = jnp.where(upper, own_heads(span), 1.0)
    offset = side(0) * HALF if first else 0
    for h in range(HALF_HEADS):
        rows = pl.ds(pl.multiple_of(offset + h * HEAD_DIM, HEAD_DIM), HEAD_DIM)
        got = got_ref[rows, :].astype(F32)
        new = own_ref[rows, :] * own_factor[h : h + 1] + got * got_factor[h : h + 1]
        here = slice(h * HEAD_DIM, (h + 1) * HEAD_DIM)
        sum_ref[here, :] = new
        pay_ref[here, :] = new.astype(BF16)
    write_spans(pay_ref, HALF, both)


SMALL = jax.ShapeDtypeStruct((HEADS, STATE), F32)
HALF_SUM = jax.ShapeDtypeStruct((HALF, STATE), F32)
HALF_PAY = jax.ShapeDtypeStruct((HALF + SPAN_ROWS, STATE), BF16)


def join(bit, *operands):
    return pl.pallas_call(
        functools.partial(join_kernel, bit),
        in_specs=[VMEM] * len(operands),
        out_specs=[VMEM] * 5,
        out_shape=[HALF_SUM, SMALL, SMALL, SMALL, HALF_PAY],
        compiler_params=pltpu.CompilerParams(**PARAMS),
        name="join" + str(bit),
    )(*operands)


def join_chips_kernel(own_ref, span_ref, lead_ref, one_ref, two_ref, three_ref, *rest):
    sum_ref, new_span_ref, new_lead_ref, low_ref, high_ref, pay_ref, states_ref = rest[-7:]
    low_upper = side(1) == 1
    high_upper = side(2) == 1
    span, lead = span_ref[...], lead_ref[...]
    one, two, three = (read_spans(ref, HALF) for ref in (one_ref, two_ref, three_ref))
    low_ref[...] = jnp.where(low_upper, lead, 0.0)
    lead = jnp.where(low_upper, lead * one, lead)
    high_ref[...] = jnp.where(high_upper, lead, 0.0)
    near, away = span * one, two * three
    new_lead_ref[...] = jnp.where(high_upper, lead * away, lead)
    both = near * away
    new_span_ref[...] = both
    own_here = jnp.where(low_upper, 1.0, own_heads(one))
    one_here = jnp.where(low_upper, own_heads(span), 1.0)
    two_here = jnp.where(low_upper, 1.0, own_heads(three))
    three_here = jnp.where(low_upper, own_heads(two), 1.0)
    near_here = jnp.where(high_upper, 1.0, own_heads(away))
    away_here = jnp.where(high_upper, own_heads(near), 1.0)
    for h in range(HALF_HEADS):
        here = slice(h * HEAD_DIM, (h + 1) * HEAD_DIM)
        row = slice(h, h + 1)
        got = one_ref[here, :]
        here_sum = own_ref[here, :] * own_here[row] + got.astype(F32) * one_here[row]
        away_sum = two_ref[here, :].astype(F32) * two_here[row] + three_ref[here, :].astype(
            F32
        ) * three_here[row]
        new = here_sum * near_here[row] + away_sum * away_here[row]
        sum_ref[here, :] = new
        pay_ref[here, :] = new.astype(BF16)
        states_ref[here, :] = got
        states_ref[HALF + h * HEAD_DIM : HALF + (h + 1) * HEAD_DIM, :] = away_sum.astype(BF16)
    write_spans(pay_ref, HALF, both)


def join_chips(own, span, lead, got):
    return pl.pallas_call(
        join_chips_kernel,
        in_specs=[VMEM] * 6,
        out_specs=[VMEM] * 7,
        out_shape=[
            HALF_SUM,
            SMALL,
            SMALL,
            SMALL,
            SMALL,
            HALF_PAY,
            jax.ShapeDtypeStruct((FEATURES, STATE), BF16),
        ],
        compiler_params=pltpu.CompilerParams(**PARAMS),
        name="join_chips",
    )(own, span, lead, *got)


LATER = LEVELS - 2


def inner_kernel(chunks, listed, skip, x_ref, b_ref, c_ref, log_ref, weight_ref, far_ref, start_ref, got_ref, factor_ref, *rest):
    y_ref, flipped_ref, coef_ref = rest[-3:]
    square = (CHUNK, CHUNK)
    for chunk in chunks:
        first = lax.axis_index("seq") * TOK_DEV + chunk * CHUNK
        lanes = slice(chunk * CHUNK, (chunk + 1) * CHUNK)
        log = log_ref[:, lanes]
        far = far_ref[:, lanes]
        middle = 0.5 * log[:, CHUNK - 1 : CHUNK]
        after = weight_ref[0, :, lanes] * jnp.exp(log - middle)
        before = jnp.exp(middle - log)
        level = weight_ref[1, :, lanes] * far * factor_ref[:, 0:1]
        for n in range(LATER):
            coef_ref[n, :, lanes] = weight_ref[2 + n, :, lanes] * far
        source = first + lax.broadcasted_iota(jnp.int32, square, 0)
        target = first + lax.broadcasted_iota(jnp.int32, square, 1)
        c = c_ref[lanes, :].T
        flipped_ref[:, lanes] = c
        scores = dot(b_ref[lanes, :], c)
        scores = jnp.where(source <= target, scores, 0.0)
        reached = first + lax.broadcasted_iota(jnp.int32, (STATE, CHUNK), 1)
        near = c.astype(F32)
        for r in range(RESETS):
            reset = listed[r]
            scores = jnp.where((source < reset) & (reset <= target), 0.0, scores)
            near = jnp.where((reset >= first) & (reached >= reset), 0.0, near)
        scores = scores.astype(BF16)
        near = near.astype(BF16)
        for group in range(GROUPS):
            rows = slice(group * WIDE, (group + 1) * WIDE)
            x = x_ref[chunk, rows, :].astype(F32)
            scaled = (x * head_rows(before, group)).astype(BF16)
            inside = dot(scaled, scores) + dot(start_ref[chunk, rows, :], near)
            y = inside * head_rows(after, group)
            y = y + dot(got_ref[rows, :], c) * head_rows(level, group)
            direct = jnp.concatenate(
                [
                    x[h * HEAD_DIM : (h + 1) * HEAD_DIM] * skip[group * GROUP_HEADS + h]
                    for h in range(GROUP_HEADS)
                ],
                axis=0,
            )
            y_ref[chunk, rows, :] = y + direct


def inner(chunk0, operands, parts):
    resets, skip, *others = operands
    operands = [in_hbm(resets), in_hbm(skip)] + others
    in_specs = [SMEM, SMEM] + [VMEM] * len(others)
    aliases = {}
    if parts is not None:
        aliases = {len(operands) + n: n for n in range(3)}
        operands += parts
        in_specs += [VMEM] * 3
    return list(
        pl.pallas_call(
            functools.partial(inner_kernel, range(chunk0, chunk0 + PIECE)),
            in_specs=in_specs,
            out_specs=[VMEM] * 3,
            out_shape=[
                jax.ShapeDtypeStruct((CHUNKS, FEATURES, CHUNK), F32),
                jax.ShapeDtypeStruct((STATE, TOK_DEV), BF16),
                jax.ShapeDtypeStruct((LATER, HEADS, TOK_DEV), F32),
            ],
            input_output_aliases=aliases,
            compiler_params=pltpu.CompilerParams(**PARAMS),
            cost_estimate=pl.CostEstimate(
                flops=PIECE * 2 * CHUNK * FEATURES * 768, bytes_accessed=PIECE * 2_000_000, transcendentals=0
            ),
            name="inner" + str(chunk0),
        )(*operands)
    )


def level_kernel(levels, parts, final, flipped_ref, coef_ref, *rest):
    count = len(levels)
    mine, other = rest[:parts], rest[parts : 2 * parts]
    factors = rest[2 * parts : 2 * parts + count]
    y_ref, states = rest[-2 - final], rest[-1]
    lower = side(0) == 0
    factors = [factor[:, 0:1] for factor in factors]
    if final:
        factors = [jnp.where(side(LEVELS - 2) == 1, factor, 0.0) for factor in factors]
    for n in range(count):
        part, start = (0, n * HALF) if parts == 1 else (n, 0)
        a = mine[part][start : start + HALF, :].astype(F32)
        b = other[part][start : start + HALF, :].astype(F32)
        states[n, :HALF, :] = jnp.where(lower, a, b).astype(BF16)
        states[n, HALF:, :] = jnp.where(lower, b, a).astype(BF16)
    for chunk in range(CHUNKS):
        lanes = slice(chunk * CHUNK, (chunk + 1) * CHUNK)
        coefs = [coef_ref[level - 2, :, lanes] * factors[n] for n, level in enumerate(levels)]
        c = flipped_ref[:, lanes]
        squares = jnp.zeros((8, CHUNK), F32)
        for group in range(GROUPS):
            rows = slice(group * WIDE, (group + 1) * WIDE)
            y = y_ref[chunk, rows, :]
            for n in range(count):
                y = y + dot(states[n, rows, :], c) * head_rows(coefs[n], group)
            y_ref[chunk, rows, :] = y
            if final:
                part = y * y
                for k in range(WIDE // 8):
                    squares = squares + part[8 * k : 8 * k + 8]
        if final:
            rest[-2][chunk] = jnp.sum(squares, axis=0, keepdims=True)


def add_levels(levels, final, mine, other, factors, y, flipped, coef):
    count = len(levels)
    operands = [flipped, coef, *mine, *other, *factors]
    return pl.pallas_call(
        functools.partial(level_kernel, levels, len(mine), final),
        in_specs=[VMEM] * (len(operands) + 1),
        out_specs=[VMEM] * (1 + final),
        out_shape=[
            jax.ShapeDtypeStruct((CHUNKS, FEATURES, CHUNK), F32),
            jax.ShapeDtypeStruct((CHUNKS, 1, CHUNK), F32),
        ][: 1 + final],
        input_output_aliases={len(operands): 0},
        scratch_shapes=[pltpu.VMEM((count, FEATURES, STATE), BF16)],
        compiler_params=pltpu.CompilerParams(**PARAMS),
        cost_estimate=pl.CostEstimate(
            flops=count * 4 * TOK_DEV * FEATURES * STATE, bytes_accessed=4_000_000, transcendentals=0
        ),
        name="levels" + str(levels[0]),
    )(*operands, y)


def flip_kernel(y_ref, gain_ref, out_ref):
    for chunk in range(CHUNKS):
        for group in range(GROUPS):
            rows = slice(group * WIDE, (group + 1) * WIDE)
            y = y_ref[chunk, rows, :].T
            out_ref[chunk * CHUNK : (chunk + 1) * CHUNK, rows] = y * gain_ref[:, rows]


def flip(y, gain):
    return pl.pallas_call(
        flip_kernel,
        in_specs=[VMEM] * 2,
        out_specs=VMEM,
        out_shape=jax.ShapeDtypeStruct((TOK_DEV, FEATURES), F32),
        compiler_params=pltpu.CompilerParams(**PARAMS),
        cost_estimate=pl.CostEstimate(flops=0, bytes_accessed=16_000_000, transcendentals=0),
        name="flip",
    )(y, gain)


def norm_kernel(y_ref, s0, s1, s2, s3, out_any, buffers, sems):
    copies = []
    for chunk in range(CHUNKS):
        rows = slice(chunk * CHUNK, (chunk + 1) * CHUNK)
        squares = (s0[chunk] + s1[chunk]) + (s2[chunk] + s3[chunk])
        scale = lax.rsqrt(squares * (1.0 / (HEAD_TOTAL * HEAD_DIM)) + EPSILON)
        scale = jnp.broadcast_to(scale, (STATE, CHUNK)).T
        for column in range(FEATURES // STATE):
            columns = slice(column * STATE, (column + 1) * STATE)
            buffers[rows, columns] = (y_ref[rows, columns] * scale).astype(BF16)
        copies.append(
            pltpu.make_async_copy(buffers.at[rows, :], out_any.at[rows, :], sems.at[chunk])
        )
        copies[chunk].start()
    for copy in copies:
        copy.wait()


def normalize(y, squares):
    return pl.pallas_call(
        norm_kernel,
        in_specs=[VMEM] * 5,
        out_specs=ANY,
        out_shape=jax.ShapeDtypeStruct((TOK_DEV, FEATURES), BF16),
        scratch_shapes=[
            pltpu.VMEM((TOK_DEV, FEATURES), BF16),
            pltpu.SemaphoreType.DMA((CHUNKS,)),
        ],
        compiler_params=pltpu.CompilerParams(**PARAMS),
        name="normalize",
    )(y, *squares)


def swap(array, axis, distance, only_up=None):
    count = lax.axis_size(axis)
    route = [
        (low, low ^ distance)
        for low in range(count)
        if only_up is None or not low >> only_up & 1
    ]
    return lax.ppermute(array, axis, route)


def per_device(inputs, state_in, state_out, log_decay, level_weight, skip, norm_gain, resets):
    total, pay, starts, log, far, span, x, b, c, weights = block_states(
        resets, inputs, state_in, state_out, log_decay, level_weight
    )
    one = swap(pay, "seq", 1)
    half, span, lead, one_factor, pay = join(0, total, span, one)
    within = (resets, skip, x, b, c, log, weights, far, starts, one, one_factor)
    got = [swap(pay, "seq", distance) for distance in (2, 6, 4)]
    parts = inner(0, within, None)
    parts = inner(2, within, parts)
    got, parts = lax.optimization_barrier((got, parts))
    half, span, lead, two_factor, three_factor, pay, mine = join_chips(
        half, span, lead, (got[0], got[2], got[1])
    )
    four = swap(pay, "seq", 8)
    other = swap(mine, "seq", 1)
    parts = inner(4, within, parts)
    parts = inner(6, within, parts)
    four, parts = lax.optimization_barrier((four, parts))
    half, span, lead, four_factor, pay = join(3, half, span, lead, four)
    four, pay = lax.optimization_barrier((four, pay))
    y, flipped, coef = parts
    five = swap(pay, "seq", 16)
    four_other = swap(four, "seq", 1)
    (y,) = add_levels((2, 3), False, [mine], [other], [two_factor, three_factor], y, flipped, coef)
    five, y = lax.optimization_barrier((five, y))
    half, span, lead, five_factor, pay = join(4, half, span, lead, five)
    five, pay = lax.optimization_barrier((five, pay))
    six = swap(pay, "seq", 48, 5)
    five_other = swap(five, "seq", 1)
    (y,) = add_levels(
        (4, 5),
        False,
        [four, five],
        [four_other, five_other],
        [four_factor, five_factor],
        y,
        flipped,
        coef,
    )
    six, y = lax.optimization_barrier((six, y))
    six_other = swap(six, "seq", 1)
    y, squares = add_levels((6,), True, [six], [six_other], [lead], y, flipped, coef)
    shares = [squares] + [
        lax.ppermute(squares, "head", [(i, i ^ d) for i in range(4)]) for d in (1, 3, 2)
    ]
    return normalize(flip(y, norm_gain.reshape(1, FEATURES)), shares)


def solution(mesh):
    placed = (
        P("seq", "head"),
        P("seq", None),
        P("seq", None),
        P("head", "seq"),
        P(None, "head", "seq"),
        P("head"),
        P("head"),
        P(),
    )
    return jax.shard_map(
        per_device, mesh=mesh, in_specs=placed, out_specs=P("seq", "head"), check_vma=False
    )
```

time: 325 us -> 62 us (0.19)
  matrix products: 91 us -> 0 us
  local copies, waits for them, and re-layouts: 87.3 us -> 0.01 us
  waiting for transfers between devices: 66.9 us -> 15 us
  other arithmetic: 46.9 us -> 0 us
  Pallas kernels: 0 us -> 26.1 us
  blocking collectives: 10.6 us -> 0 us
    dot_general x33 -> x0, matrix products: 91 us -> none  [the longest x8 28.8 us: stretch_output(): jnp.einsum('hts,shp->thp', mask_weight, inputs_part, preferred_element_ty...]
    ppermute x11 -> x14, waiting for transfers between devices: 66.9 us -> 15 us  [the longest x11 12.7 us: swap(): return lax.ppermute(array, axis, route)]
    reshape x3 -> x0, local copies, waits for them, and re-layouts: 34.6 us -> none  [the longest x2 22.7 us: per_device(): scaled.astype(jnp.bfloat16).reshape(token_count, head_count * HEAD_DIM)]
    dynamic_slice x64 -> x0, local copies, waits for them, and re-layouts: 27.9 us -> none  [the longest x40 26.8 us: per_device(): lax.map(one_stretch, (log_stretches, count_stretches, coef_stretches, pre...]
    pallas_call x0 -> x14, Pallas kernels: none -> 26.1 us  [the longest x4 7.85 us: inner(): pl.pallas_call(functools.partial(inner_kernel, range(chunk0, chunk0 + PIE...]
    psum x1 -> x0, blocking collectives: 10.6 us -> none  [per_device(): whole_squares = lax.psum(squares, 'head')]
    while x1 -> x0, local copies, waits for them, and re-layouts: 10.3 us -> none  [per_device(): lax.map(one_stretch, (log_stretches, count_stretches, coef_stretches, pre...]
    eq x17 -> x0, other arithmetic: 10.2 us -> none  [the longest x8 4.73 us: stretch_state(): reset_count == reset_count[-1]]
  transfers between devices with their start and end apart: 11 -> 14, of which waited for: 7 -> 7; matrix products, arithmetic and copies ran while one was open for 7% -> 0% of each run, Pallas kernels for 0% -> 26%
where the time goes in v2:
time: 62 us; the launch traced here: 60.9 us
  Pallas kernels  26.1 us (42%)
  starting transfers between devices  19.4 us (31%)
  waiting for transfers between devices  15 us (24%)
    ppermute x11, starting transfers between devices, swap(): return lax.ppermute(array, axis, route)  15.1 us
    ppermute x11, waiting for transfers between devices, swap(): return lax.ppermute(array, axis, route)  12.7 us
    pallas_call x4, Pallas kernels, inner(): pl.pallas_call(functools.partial(inner_kernel, range(chunk0, chunk0 + PIE...  7.85 us
    pallas_call x3, Pallas kernels, add_levels(): pl.pallas_call(functools.partial(level_kernel, levels, len(mine), final),...  6.51 us
    pallas_call x1, Pallas kernels, block_states(): pl.pallas_call(state_kernel, in_specs=[SMEM] + [ANY] * 5, out_specs=[VMEM...  5.82 us
    ppermute x3, starting transfers between devices, per_device(): lax.ppermute(squares, 'head', [(i, i ^ d) for i in range(4)])  4.31 us
    ppermute x3, waiting for transfers between devices, per_device(): lax.ppermute(squares, 'head', [(i, i ^ d) for i in range(4)])  2.27 us
    pallas_call x1, Pallas kernels, normalize(): pl.pallas_call(norm_kernel, in_specs=[VMEM] * 5, out_specs=ANY, out_shape...  2.23 us
  transfers between devices with their start and end apart: 14, of which 7 were waited for; matrix products, arithmetic and copies ran while one was open for 0% of the time, Pallas kernels for 26%

profile of v2, /device:TPU:16, one launch (start us, length us, event | category | flops | bytes accessed | tf_op | source)
XLA Modules:
  0.0 60.9 jit_solution(6096577655063967445)
XLA Ops:
  0.0 5.8 %block_states.1 = (f32[1024,128]{1,0:T(8,128)S(1)}, bf16[1040,128]{1,0:T(8,128)(2,1)S(1)}, bf16[8,1024,128]{2,1,0:T(8,128)(2,1)S(1)}, f32[16,2048]{1,0:T(8,128)S...) custom-call(s32[4]{0:T(128)} %listed.9, ...), custom_call_target="tpu_custom_call" | custom-call | tf_op jit(solution)/shard_map/block_states/pallas_call | solution.py:157
  5.8 0.1 collective-permute-start
  5.9 1.5 %collective-permute-done.rest_0_.got_ref = bf16[1040,128]{1,0:T(8,128)(2,1)S(1)} collective-permute-done((bf16[1040,128]{1,0:T(8,128)(2,1)S(1)}, bf16[1040,128]{1,0:T(8,128)(2,1)S(1)}, u32[]{:S(2)}, u32[]{:S(2)}) %collective-permute-start) | collective-permute-done | bytes 266272 | tf_op jit(solution)/shard_map/ppermute | solution.py:483
  7.5 0.2 join0.1
  7.6 1.4 %collective-permute-start.1 = (bf16[528,128]{1,0:T(8,128)(2,1)S(1)}, bf16[528,128]{1,0:T(8,128)(2,1)S(1)}, u32[]{:S(2)}, u32[]{:S(2)}) collective-permute-start(bf16[528,128]{1,0:T(8,128)(2,1)S(1)} %get-tuple-element.73), channel_id=1, source_target_pairs={{0,8},{4,12},{8,0},{12,4},{16,24},{20,28},{24,16},{28,20},{32,40},... | collective-permute-start | bytes 405512 | tf_op jit(solution)/shard_map/ppermute | solution.py:483
  9.0 1.4 %collective-permute-start.2 = (bf16[528,128]{1,0:T(8,128)(2,1)S(1)}, bf16[528,128]{1,0:T(8,128)(2,1)S(1)}, u32[]{:S(2)}, u32[]{:S(2)}) collective-permute-start(bf16[528,128]{1,0:T(8,128)(2,1)S(1)} %get-tuple-element.73), channel_id=1, source_target_pairs={{0,24},{4,28},{8,16},{12,20},{16,8},{20,12},{24,0},{28,4},{32,56},... | collective-permute-start | bytes 405512 | tf_op jit(solution)/shard_map/ppermute | solution.py:483
  10.4 1.5 %collective-permute-start.3 = (bf16[528,128]{1,0:T(8,128)(2,1)S(1)}, bf16[528,128]{1,0:T(8,128)(2,1)S(1)}, u32[]{:S(2)}, u32[]{:S(2)}) collective-permute-start(bf16[528,128]{1,0:T(8,128)(2,1)S(1)} %get-tuple-element.73), channel_id=1, source_target_pairs={{0,16},{4,20},{8,24},{12,28},{16,0},{20,4},{24,8},{28,12},{32,48},... | collective-permute-start | bytes 405512 | tf_op jit(solution)/shard_map/ppermute | solution.py:483
  11.8 2.0 %inner0.1 = (f32[8,1024,256]{2,1,0:T(8,128)S(1)}, bf16[128,2048]{1,0:T(8,128)(2,1)S(1)}, f32[5,16,2048]{2,1,0:T(8,128)S(1)}) custom-call(s32[4]{0:T(128)} %listed.9, f32[16]{0:T(128)} %skip.7, bf16[8,1024,256]{2,1,0:T(8,128)(2,1)S(1)} %get-tuple-element.74.x_ref, bf16[2048,128]{1,0:T(8,128)(2,1)S(1)} %get-tuple-element.75.b_ref, ...), custom_call_target="tpu_custom_call" | custom-call | flops 805306368 | bytes 4000000 | tf_op jit(solution)/shard_map/inner0/pallas_call | solution.py:349
  13.8 2.0 %inner2.1 = (f32[8,1024,256]{2,1,0:T(8,128)S(1)}, bf16[128,2048]{1,0:T(8,128)(2,1)S(1)}, f32[5,16,2048]{2,1,0:T(8,128)S(1)}) custom-call(s32[4]{0:T(128)} %listed.9, f32[16]{0:T(128)} %skip.7, bf16[8,1024,256]{2,1,0:T(8,128)(2,1)S(1)} %get-tuple-element.74.x_ref, ...), custom_call_target="tpu_custom_call", output_to_operand_aliasing={{0}: (11, {}), {1}: (12, {}), {2}: (13, {})} | custom-call | flops 805306368 | bytes 4000000 | tf_op jit(solution)/shard_map/inner2/pallas_call | solution.py:349
  15.8 0.0 collective-permute-done.1.one_ref
  15.8 1.5 %collective-permute-done.2.three_ref = bf16[528,128]{1,0:T(8,128)(2,1)S(1)} collective-permute-done((bf16[528,128]{1,0:T(8,128)(2,1)S(1)}, bf16[528,128]{1,0:T(8,128)(2,1)S(1)}, u32[]{:S(2)}, u32[]{:S(2)}) %collective-permute-start.2) | collective-permute-done | bytes 135200 | tf_op jit(solution)/shard_map/ppermute | solution.py:483
  17.3 0.0 collective-permute-done.3.two_ref
  17.3 0.3 join_chips.1
  17.5 0.1 collective-permute-start.6
  17.6 2.0 %collective-permute-start.4 = (bf16[528,128]{1,0:T(8,128)(2,1)S(1)}, bf16[528,128]{1,0:T(8,128)(2,1)S(1)}, u32[]{:S(2)}, u32[]{:S(2)}) collective-permute-start(bf16[528,128]{1,0:T(8,128)(2,1)S(1)} %get-tuple-element.91), channel_id=1, source_target_pairs={{0,32},{4,36},{8,40},{12,44},{16,48},{20,52},{24,56},{28,60},{32,0... | collective-permute-start | bytes 405512 | tf_op jit(solution)/shard_map/ppermute | solution.py:483
  19.6 2.0 %inner4.1 = (f32[8,1024,256]{2,1,0:T(8,128)S(1)}, bf16[128,2048]{1,0:T(8,128)(2,1)S(1)}, f32[5,16,2048]{2,1,0:T(8,128)S(1)}) custom-call(s32[4]{0:T(128)} %listed.9, f32[16]{0:T(128)} %skip.7, bf16[8,1024,256]{2,1,0:T(8,128)(2,1)S(1)} %get-tuple-element.74.x_ref, ...), custom_call_target="tpu_custom_call", output_to_operand_aliasing={{0}: (11, {}), {1}: (12, {}), {2}: (13, {})} | custom-call | flops 805306368 | bytes 4000000 | tf_op jit(solution)/shard_map/inner4/pallas_call | solution.py:349
  21.6 2.0 %inner6.1 = (f32[8,1024,256]{2,1,0:T(8,128)S(1)}, bf16[128,2048]{1,0:T(8,128)(2,1)S(1)}, f32[5,16,2048]{2,1,0:T(8,128)S(1)}) custom-call(s32[4]{0:T(128)} %listed.9, f32[16]{0:T(128)} %skip.7, bf16[8,1024,256]{2,1,0:T(8,128)(2,1)S(1)} %get-tuple-element.74.x_ref, ...), custom_call_target="tpu_custom_call", output_to_operand_aliasing={{0}: (11, {}), {1}: (12, {}), {2}: (13, {})} | custom-call | flops 805306368 | bytes 4000000 | tf_op jit(solution)/shard_map/inner6/pallas_call | solution.py:349
  23.6 0.2 collective-permute-done.4.rest_1_.rest_0_
  23.8 0.2 join3.1
  24.0 3.5 %collective-permute-start.5 = (bf16[528,128]{1,0:T(8,128)(2,1)S(1)}, bf16[528,128]{1,0:T(8,128)(2,1)S(1)}, u32[]{:S(2)}, u32[]{:S(2)}) collective-permute-start(bf16[528,128]{1,0:T(8,128)(2,1)S(1)} %get-tuple-element.108), channel_id=1, source_target_pairs={{0,64},{4,68},{8,72},{12,76},{16,80},{20,84},{24,88},{28,92},{32,9... | collective-permute-start | bytes 405512 | tf_op jit(solution)/shard_map/ppermute | solution.py:483
  27.5 0.0 collective-permute-start.8
  27.5 0.0 collective-permute-done.6.rest_1_
  27.5 2.4 %levels2.1.rest_6_ = f32[8,1024,256]{2,1,0:T(8,128)S(1)} custom-call(bf16[128,2048]{1,0:T(8,128)(2,1)S(1)} %get-tuple-element.101.flipped_ref, f32[5,16,2048]{2,1,0:T(8,128)S(1)} %get-tuple-element.102.coef_ref, bf16[1024,128]{1,0:T(8,128)(2,1)S(1)} %get-tuple-element.109.rest_0_, ...), custom_call_target="tpu_custom_call", output_to_operand_aliasing={{}: (6, {})} | custom-call | flops 2147483648 | bytes 4000000 | tf_op jit(solution)/shard_map/levels2/pallas_call | solution.py:405
  29.9 4.2 %collective-permute-done.5.rest_1_ = bf16[528,128]{1,0:T(8,128)(2,1)S(1)} collective-permute-done((bf16[528,128]{1,0:T(8,128)(2,1)S(1)}, bf16[528,128]{1,0:T(8,128)(2,1)S(1)}, u32[]{:S(2)}, u32[]{:S(2)}) %collective-permute-start.5) | collective-permute-done | bytes 135200 | tf_op jit(solution)/shard_map/ppermute | solution.py:483
  34.1 0.9 %join4.1 = (f32[512,128]{1,0:T(8,128)}, f32[16,128]{1,0:T(8,128)}, f32[16,128]{1,0:T(8,128)S(1)}, f32[16,128]{1,0:T(8,128)S(1)}, bf16[528,128]{1,0:T(8,128)(2,1)S(1)}) custom-call(f32[512,128]{1,0:T(8,128)S(1)} %get-tuple-element.114.own_ref, f32[16,128]{1,0:T(8,128)S(1)} %get-tuple-element.115.span_ref, f32[16,128]{1,0:T(8,128)S(1)} %get-tuple-element.116.rest_0_, ...), custom_call_target="tpu_custom_call" | custom-call | tf_op jit(solution)/shard_map/join4/pallas_call | solution.py:227
  35.0 0.0 collective-permute-start.9
  35.0 5.2 %collective-permute-start.7 = (bf16[528,128]{1,0:T(8,128)(2,1)S(1)}, bf16[528,128]{1,0:T(8,128)(2,1)S(1)}, u32[]{:S(2)}, u32[]{:S(2)}) collective-permute-start(bf16[528,128]{1,0:T(8,128)(2,1)S(1)} %get-tuple-element.118), channel_id=1, source_target_pairs={{0,192},{4,196},{8,200},{12,204},{16,208},{20,212},{24,216},{28,22... | collective-permute-start | bytes 405512 | tf_op jit(solution)/shard_map/ppermute | solution.py:483
  40.2 0.0 collective-permute-done.8.rest_2_
  40.2 0.0 collective-permute-done.9.rest_3_
  40.2 2.4 %levels4.1.rest_3_ = f32[8,1024,256]{2,1,0:T(8,128)S(1)} custom-call(bf16[128,2048]{1,0:T(8,128)(2,1)S(1)} %get-tuple-element.101.flipped_ref, f32[5,16,2048]{2,1,0:T(8,128)S(1)} %get-tuple-element.102.coef_ref, bf16[528,128]{1,0:T(8,128)(2,1)S(1)} %collective-permute-done.4.rest_1_.rest_0_, ...), custom_call_target="tpu_custom_call", output_to_operand_aliasing={{}: (8, {})} | custom-call | flops 2147483648 | bytes 4000000 | tf_op jit(solution)/shard_map/levels4/pallas_call | solution.py:405
  42.6 0.0 copy-start
  42.6 4.0 %collective-permute-done.7.rest_0_ = bf16[528,128]{1,0:T(8,128)(2,1)S(1)} collective-permute-done((bf16[528,128]{1,0:T(8,128)(2,1)S(1)}, bf16[528,128]{1,0:T(8,128)(2,1)S(1)}, u32[]{:S(2)}, u32[]{:S(2)}) %collective-permute-start.7) | collective-permute-done | bytes 135200 | tf_op jit(solution)/shard_map/ppermute | solution.py:483
  46.6 0.0 collective-permute-start.10
  46.6 1.4 %collective-permute-done.10.rest_1_ = bf16[528,128]{1,0:T(8,128)(2,1)S(1)} collective-permute-done((bf16[528,128]{1,0:T(8,128)(2,1)S(1)}, bf16[528,128]{1,0:T(8,128)(2,1)S(1)}, u32[]{:S(2)}, u32[]{:S(2)}) %collective-permute-start.10) | collective-permute-done | bytes 135200 | tf_op jit(solution)/shard_map/ppermute | solution.py:483
  48.0 1.7 %levels6.1 = (f32[8,1024,256]{2,1,0:T(8,128)S(1)}, f32[8,1,256]{2,1,0:T(1,128)S(1)}) custom-call(bf16[128,2048]{1,0:T(8,128)(2,1)S(1)} %get-tuple-element.101.flipped_ref, f32[5,16,2048]{2,1,0:T(8,128)S(1)} %get-tuple-element.102.coef_ref, bf16[528,128]{1,0:T(8,128)(2,1)S(1)} %collective-permute-done.7.rest_0_, ...), custom_call_target="tpu_custom_call", output_to_operand_aliasing={{0}: (5, {})} | custom-call | flops 1073741824 | bytes 4000000 | tf_op jit(solution)/shard_map/levels6/pallas_call | solution.py:405
  49.6 1.6 %collective-permute-start.11 = (f32[8,1,256]{2,1,0:T(1,128)S(1)}, f32[8,1,256]{2,1,0:T(1,128)S(1)}, u32[]{:S(2)}, u32[]{:S(2)}) collective-permute-start(f32[8,1,256]{2,1,0:T(1,128)S(1)} %get-tuple-element.128.s0), channel_id=1, source_target_pairs={{0,1},{1,0},{2,3},{3,2},{4,5},{5,4},{6,7},{7,6},{8,9},{9,8},{10,11... | collective-permute-start | bytes 24584 | tf_op jit(solution)/shard_map/ppermute | solution.py:530
  51.2 2.1 %collective-permute-start.12 = (f32[8,1,256]{2,1,0:T(1,128)S(1)}, f32[8,1,256]{2,1,0:T(1,128)S(1)}, u32[]{:S(2)}, u32[]{:S(2)}) collective-permute-start(f32[8,1,256]{2,1,0:T(1,128)S(1)} %get-tuple-element.128.s0), channel_id=1, source_target_pairs={{0,3},{1,2},{2,1},{3,0},{4,7},{5,6},{6,5},{7,4},{8,11},{9,10},{10,... | collective-permute-start | bytes 24584 | tf_op jit(solution)/shard_map/ppermute | solution.py:530
  53.3 0.6 %collective-permute-start.13 = (f32[8,1,256]{2,1,0:T(1,128)S(1)}, f32[8,1,256]{2,1,0:T(1,128)S(1)}, u32[]{:S(2)}, u32[]{:S(2)}) collective-permute-start(f32[8,1,256]{2,1,0:T(1,128)S(1)} %get-tuple-element.128.s0), channel_id=1, source_target_pairs={{0,2},{1,3},{2,0},{3,1},{4,6},{5,7},{6,4},{7,5},{8,10},{9,11},{10,... | collective-permute-start | bytes 24584 | tf_op jit(solution)/shard_map/ppermute | solution.py:530
  54.0 0.0 copy-done
  54.0 2.2 %flip.1.y_ref = f32[2048,1024]{1,0:T(8,128)S(1)} custom-call(f32[8,1024,256]{2,1,0:T(8,128)S(1)} %get-tuple-element.127.y_ref, f32[1,1024]{1,0:T(1,128)S(1)} %bitcast.1), custom_call_target="tpu_custom_call" | custom-call | bytes 16000000 | tf_op jit(solution)/shard_map/flip/pallas_call | solution.py:432
  56.2 0.0 collective-permute-done.11.s1
  56.2 0.0 collective-permute-done.12.s2
  56.2 2.3 %collective-permute-done.13.s3 = f32[8,1,256]{2,1,0:T(1,128)S(1)} collective-permute-done((f32[8,1,256]{2,1,0:T(1,128)S(1)}, f32[8,1,256]{2,1,0:T(1,128)S(1)}, u32[]{:S(2)}, u32[]{:S(2)}) %collective-permute-start.13) | collective-permute-done | bytes 8224 | tf_op jit(solution)/shard_map/ppermute | solution.py:530
  58.5 2.2 %normalize.1 = bf16[2048,1024]{1,0:T(8,128)(2,1)} custom-call(f32[2048,1024]{1,0:T(8,128)S(1)} %flip.1.y_ref, f32[8,1,256]{2,1,0:T(1,128)S(1)} %get-tuple-element.128.s0, f32[8,1,256]{2,1,0:T(1,128)S(1)} %collective-permute-done.11.s1, f32[8,1,256]{2,1,0:T(1,128)S(1)} %collective-permute-done.12.s2, f32[8,1,256]{2,1,0:T(1,128)S(1)} %collective-permute-done.13.s3), custom_call_target="tpu_custom_call" | custom-call | tf_op jit(solution)/shard_map/normalize/pallas_call | solution.py:462
Async XLA Ops:
  5.8 1.6 %collective-permute-start = (bf16[1040,128]{1,0:T(8,128)(2,1)S(1)}, bf16[1040,128]{1,0:T(8,128)(2,1)S(1)}, u32[]{:S(2)}, u32[]{:S(2)}) collective-permute-start(bf16[1040,128]{1,0:T(8,128)(2,1)S(1)} %get-tuple-element.69), channel_id=1, source_target_pairs={{0,4},{4,0},{8,12},{12,8},{16,20},{20,16},{24,28},{28,24},{32,36},... | collective-permute-start | bytes 798728 | tf_op jit(solution)/shard_map/ppermute | solution.py:483
  7.6 8.1 %collective-permute-start.1 = (bf16[528,128]{1,0:T(8,128)(2,1)S(1)}, bf16[528,128]{1,0:T(8,128)(2,1)S(1)}, u32[]{:S(2)}, u32[]{:S(2)}) collective-permute-start(bf16[528,128]{1,0:T(8,128)(2,1)S(1)} %get-tuple-element.73), channel_id=1, source_target_pairs={{0,8},{4,12},{8,0},{12,4},{16,24},{20,28},{24,16},{28,20},{32,40},... | collective-permute-start | bytes 405512 | tf_op jit(solution)/shard_map/ppermute | solution.py:483
  9.0 8.2 %collective-permute-start.2 = (bf16[528,128]{1,0:T(8,128)(2,1)S(1)}, bf16[528,128]{1,0:T(8,128)(2,1)S(1)}, u32[]{:S(2)}, u32[]{:S(2)}) collective-permute-start(bf16[528,128]{1,0:T(8,128)(2,1)S(1)} %get-tuple-element.73), channel_id=1, source_target_pairs={{0,24},{4,28},{8,16},{12,20},{16,8},{20,12},{24,0},{28,4},{32,56},... | collective-permute-start | bytes 405512 | tf_op jit(solution)/shard_map/ppermute | solution.py:483
  10.4 6.9 %collective-permute-start.3 = (bf16[528,128]{1,0:T(8,128)(2,1)S(1)}, bf16[528,128]{1,0:T(8,128)(2,1)S(1)}, u32[]{:S(2)}, u32[]{:S(2)}) collective-permute-start(bf16[528,128]{1,0:T(8,128)(2,1)S(1)} %get-tuple-element.73), channel_id=1, source_target_pairs={{0,16},{4,20},{8,24},{12,28},{16,0},{20,4},{24,8},{28,12},{32,48},... | collective-permute-start | bytes 405512 | tf_op jit(solution)/shard_map/ppermute | solution.py:483
  17.5 10.0 %collective-permute-start.6 = (bf16[1024,128]{1,0:T(8,128)(2,1)S(1)}, bf16[1024,128]{1,0:T(8,128)(2,1)S(1)}, u32[]{:S(2)}, u32[]{:S(2)}) collective-permute-start(bf16[1024,128]{1,0:T(8,128)(2,1)S(1)} %get-tuple-element.109.rest_0_), channel_id=1, source_target_pairs={{0,4},{4,0},{8,12},{12,8},{16,20},{20,16},{24,28},{28,24},{32,36},... | collective-permute-start | bytes 786440 | tf_op jit(solution)/shard_map/ppermute | solution.py:483
  17.6 6.2 %collective-permute-start.4 = (bf16[528,128]{1,0:T(8,128)(2,1)S(1)}, bf16[528,128]{1,0:T(8,128)(2,1)S(1)}, u32[]{:S(2)}, u32[]{:S(2)}) collective-permute-start(bf16[528,128]{1,0:T(8,128)(2,1)S(1)} %get-tuple-element.91), channel_id=1, source_target_pairs={{0,32},{4,36},{8,40},{12,44},{16,48},{20,52},{24,56},{28,60},{32,0... | collective-permute-start | bytes 405512 | tf_op jit(solution)/shard_map/ppermute | solution.py:483
  24.0 10.1 %collective-permute-start.5 = (bf16[528,128]{1,0:T(8,128)(2,1)S(1)}, bf16[528,128]{1,0:T(8,128)(2,1)S(1)}, u32[]{:S(2)}, u32[]{:S(2)}) collective-permute-start(bf16[528,128]{1,0:T(8,128)(2,1)S(1)} %get-tuple-element.108), channel_id=1, source_target_pairs={{0,64},{4,68},{8,72},{12,76},{16,80},{20,84},{24,88},{28,92},{32,9... | collective-permute-start | bytes 405512 | tf_op jit(solution)/shard_map/ppermute | solution.py:483
  27.5 12.7 %collective-permute-start.8 = (bf16[528,128]{1,0:T(8,128)(2,1)S(1)}, bf16[528,128]{1,0:T(8,128)(2,1)S(1)}, u32[]{:S(2)}, u32[]{:S(2)}) collective-permute-start(bf16[528,128]{1,0:T(8,128)(2,1)S(1)} %collective-permute-done.4.rest_1_.rest_0_), channel_id=1, source_target_pairs={{0,4},{4,0},{8,12},{12,8},{16,20},{20,16},{24,28},{28,24},{32,36},... | collective-permute-start | bytes 405512 | tf_op jit(solution)/shard_map/ppermute | solution.py:483
  35.0 5.2 %collective-permute-start.9 = (bf16[528,128]{1,0:T(8,128)(2,1)S(1)}, bf16[528,128]{1,0:T(8,128)(2,1)S(1)}, u32[]{:S(2)}, u32[]{:S(2)}) collective-permute-start(bf16[528,128]{1,0:T(8,128)(2,1)S(1)} %collective-permute-done.5.rest_1_), channel_id=1, source_target_pairs={{0,4},{4,0},{8,12},{12,8},{16,20},{20,16},{24,28},{28,24},{32,36},... | collective-permute-start | bytes 405512 | tf_op jit(solution)/shard_map/ppermute | solution.py:483
  35.0 11.6 %collective-permute-start.7 = (bf16[528,128]{1,0:T(8,128)(2,1)S(1)}, bf16[528,128]{1,0:T(8,128)(2,1)S(1)}, u32[]{:S(2)}, u32[]{:S(2)}) collective-permute-start(bf16[528,128]{1,0:T(8,128)(2,1)S(1)} %get-tuple-element.118), channel_id=1, source_target_pairs={{0,192},{4,196},{8,200},{12,204},{16,208},{20,212},{24,216},{28,22... | collective-permute-start | bytes 405512 | tf_op jit(solution)/shard_map/ppermute | solution.py:483
  42.6 11.4 %copy-start = (f32[1024]{0:T(1024)S(1)}, f32[1024]{0:T(1024)}, u32[]{:S(2)}) copy-start(f32[1024]{0:T(1024)} %param.14) | copy-start | bytes 12292
  46.6 1.4 %collective-permute-start.10 = (bf16[528,128]{1,0:T(8,128)(2,1)S(1)}, bf16[528,128]{1,0:T(8,128)(2,1)S(1)}, u32[]{:S(2)}, u32[]{:S(2)}) collective-permute-start(bf16[528,128]{1,0:T(8,128)(2,1)S(1)} %collective-permute-done.7.rest_0_), channel_id=1, source_target_pairs={{0,4},{4,0},{8,12},{12,8},{16,20},{20,16},{24,28},{28,24},{32,36},... | collective-permute-start | bytes 405512 | tf_op jit(solution)/shard_map/ppermute | solution.py:483
  49.6 6.5 %collective-permute-start.11 = (f32[8,1,256]{2,1,0:T(1,128)S(1)}, f32[8,1,256]{2,1,0:T(1,128)S(1)}, u32[]{:S(2)}, u32[]{:S(2)}) collective-permute-start(f32[8,1,256]{2,1,0:T(1,128)S(1)} %get-tuple-element.128.s0), channel_id=1, source_target_pairs={{0,1},{1,0},{2,3},{3,2},{4,5},{5,4},{6,7},{7,6},{8,9},{9,8},{10,11... | collective-permute-start | bytes 24584 | tf_op jit(solution)/shard_map/ppermute | solution.py:530
  51.2 5.0 %collective-permute-start.12 = (f32[8,1,256]{2,1,0:T(1,128)S(1)}, f32[8,1,256]{2,1,0:T(1,128)S(1)}, u32[]{:S(2)}, u32[]{:S(2)}) collective-permute-start(f32[8,1,256]{2,1,0:T(1,128)S(1)} %get-tuple-element.128.s0), channel_id=1, source_target_pairs={{0,3},{1,2},{2,1},{3,0},{4,7},{5,6},{6,5},{7,4},{8,11},{9,10},{10,... | collective-permute-start | bytes 24584 | tf_op jit(solution)/shard_map/ppermute | solution.py:530
  53.3 5.2 %collective-permute-start.13 = (f32[8,1,256]{2,1,0:T(1,128)S(1)}, f32[8,1,256]{2,1,0:T(1,128)S(1)}, u32[]{:S(2)}, u32[]{:S(2)}) collective-permute-start(f32[8,1,256]{2,1,0:T(1,128)S(1)} %get-tuple-element.128.s0), channel_id=1, source_target_pairs={{0,2},{1,3},{2,0},{3,1},{4,6},{5,7},{6,4},{7,5},{8,10},{9,11},{10,... | collective-permute-start | bytes 24584 | tf_op jit(solution)/shard_map/ppermute | solution.py:530

commit v3 on v2

--- a/solution.py
+++ b/solution.py
@@ -20,6 +20,9 @@
 FEATURES = HEADS * HEAD_DIM
 HALF = FEATURES // 2
 HALF_HEADS = HEADS // 2
+CHIPS = 2
+SHARD = HALF // CHIPS
+SHARD_HEADS = HALF_HEADS // CHIPS
 GROUP_HEADS = 8
 WIDE = GROUP_HEADS * HEAD_DIM
 GROUPS = HEADS // GROUP_HEADS
@@ -193,23 +196,28 @@
     return jnp.where(side(0) == 0, span[:HALF_HEADS], span[HALF_HEADS:])
 
 
-def join_kernel(bit, own_ref, span_ref, *rest):
-    *lead_ref, got_ref = rest[:-5]
-    sum_ref, new_span_ref, new_lead_ref, factor_ref, pay_ref = rest[-5:]
-    upper = side(bit) == 1
-    first = bit == 0
+def chip():
+    return side(1)
+
+
+def shard_head(span, head):
+    row = side(0) * HALF_HEADS + chip() * SHARD_HEADS + head
+    here = lax.broadcasted_iota(jnp.int32, span.shape, 0) == row
+    return jnp.sum(jnp.where(here, span, 0.0), axis=0, keepdims=True)
+
+
+def join_cores_kernel(own_ref, span_ref, got_ref, sum_ref, new_span_ref, new_lead_ref, factor_ref, pay_ref):
+    upper = side(0) == 1
     span = span_ref[...]
-    lead = jnp.ones_like(span) if first else lead_ref[0][...]
-    got_span = read_spans(got_ref, FEATURES if first else HALF)
-    factor_ref[...] = jnp.where(upper, lead, 0.0)
-    new_lead_ref[...] = jnp.where(upper, lead * got_span, lead)
+    got_span = read_spans(got_ref, FEATURES)
+    factor_ref[...] = jnp.broadcast_to(jnp.where(upper, 1.0, 0.0), span.shape)
+    new_lead_ref[...] = jnp.where(upper, got_span, 1.0)
     both = span * got_span
     new_span_ref[...] = both
     own_factor = jnp.where(upper, 1.0, own_heads(got_span))
     got_factor = jnp.where(upper, own_heads(span), 1.0)
-    offset = side(0) * HALF if first else 0
     for h in range(HALF_HEADS):
-        rows = pl.ds(pl.multiple_of(offset + h * HEAD_DIM, HEAD_DIM), HEAD_DIM)
+        rows = pl.ds(pl.multiple_of(side(0) * HALF + h * HEAD_DIM, HEAD_DIM), HEAD_DIM)
         got = got_ref[rows, :].astype(F32)
         new = own_ref[rows, :] * own_factor[h : h + 1] + got * got_factor[h : h + 1]
         here = slice(h * HEAD_DIM, (h + 1) * HEAD_DIM)
@@ -218,24 +226,80 @@
     write_spans(pay_ref, HALF, both)
 
 
+def join_kernel(bit, own_ref, span_ref, lead_ref, got_ref, *rest):
+    *below, sum_ref, new_span_ref, new_lead_ref, factor_ref, pay_ref = rest[: 5 + len(rest) // 6]
+    if below:
+        rest[-1][:SHARD, :] = below[0][:SHARD, :]
+        rest[-1][SHARD:, :] = got_ref[:SHARD, :]
+    upper = side(bit) == 1
+    span, lead = span_ref[...], lead_ref[...]
+    got_span = read_spans(got_ref, SHARD)
+    factor_ref[...] = jnp.where(upper, lead, 0.0)
+    new_lead_ref[...] = jnp.where(upper, lead * got_span, lead)
+    both = span * got_span
+    new_span_ref[...] = both
+    for h in range(SHARD_HEADS):
+        here = slice(h * HEAD_DIM, (h + 1) * HEAD_DIM)
+        own_factor = jnp.where(upper, 1.0, shard_head(got_span, h))
+        got_factor = jnp.where(upper, shard_head(span, h), 1.0)
+        new = own_ref[here, :] * own_factor + got_ref[here, :].astype(F32) * got_factor
+        sum_ref[here, :] = new
+        pay_ref[here, :] = new.astype(BF16)
+    write_spans(pay_ref, SHARD, both)
+
+
 SMALL = jax.ShapeDtypeStruct((HEADS, STATE), F32)
 HALF_SUM = jax.ShapeDtypeStruct((HALF, STATE), F32)
 HALF_PAY = jax.ShapeDtypeStruct((HALF + SPAN_ROWS, STATE), BF16)
-
-
-def join(bit, *operands):
-    return pl.pallas_call(
-        functools.partial(join_kernel, bit),
+SHARD_SUM = jax.ShapeDtypeStruct((SHARD, STATE), F32)
+SHARD_PAIR = jax.ShapeDtypeStruct((2 * SHARD, STATE), BF16)
+SHARD_PAY = jax.ShapeDtypeStruct((SHARD + SPAN_ROWS, STATE), BF16)
+
+
+def join_cores(*operands):
+    return pl.pallas_call(
+        join_cores_kernel,
         in_specs=[VMEM] * len(operands),
         out_specs=[VMEM] * 5,
         out_shape=[HALF_SUM, SMALL, SMALL, SMALL, HALF_PAY],
         compiler_params=pltpu.CompilerParams(**PARAMS),
+        name="join_cores",
+    )(*operands)
+
+
+def join(bit, *operands):
+    return pl.pallas_call(
+        functools.partial(join_kernel, bit),
+        in_specs=[VMEM] * len(operands),
+        out_specs=[VMEM] * (5 + len(operands) // 5),
+        out_shape=[SHARD_SUM, SMALL, SMALL, SMALL, SHARD_PAY, SHARD_PAIR][: 5 + len(operands) // 5],
+        compiler_params=pltpu.CompilerParams(**PARAMS),
         name="join" + str(bit),
     )(*operands)
 
 
+def gather_kernel(parts, *refs):
+    out_ref = refs[-1]
+    for distance in range(CHIPS):
+        row = (chip() ^ distance) * SHARD
+        for n in range(parts):
+            rows = pl.ds(pl.multiple_of(row + n * HALF, SHARD), SHARD)
+            out_ref[rows, :] = refs[distance][n * SHARD : (n + 1) * SHARD, :]
+
+
+def gather(parts, own, got):
+    return pl.pallas_call(
+        functools.partial(gather_kernel, parts),
+        in_specs=[VMEM] * CHIPS,
+        out_specs=VMEM,
+        out_shape=jax.ShapeDtypeStruct((parts * HALF, STATE), BF16),
+        compiler_params=pltpu.CompilerParams(**PARAMS),
+        name="gather" + str(parts),
+    )(own, *got)
+
+
 def join_chips_kernel(own_ref, span_ref, lead_ref, one_ref, two_ref, three_ref, *rest):
-    sum_ref, new_span_ref, new_lead_ref, low_ref, high_ref, pay_ref, states_ref = rest[-7:]
+    sum_ref, new_span_ref, new_lead_ref, low_ref, high_ref, pay_ref, states_ref, sums = rest
     low_upper = side(1) == 1
     high_upper = side(2) == 1
     span, lead = span_ref[...], lead_ref[...]
@@ -262,11 +326,13 @@
             F32
         ) * three_here[row]
         new = here_sum * near_here[row] + away_sum * away_here[row]
-        sum_ref[here, :] = new
-        pay_ref[here, :] = new.astype(BF16)
+        sums[here, :] = new
         states_ref[here, :] = got
         states_ref[HALF + h * HEAD_DIM : HALF + (h + 1) * HEAD_DIM, :] = away_sum.astype(BF16)
-    write_spans(pay_ref, HALF, both)
+    shard = sums[pl.ds(pl.multiple_of(chip() * SHARD, SHARD), SHARD), :]
+    sum_ref[...] = shard
+    pay_ref[:SHARD, :] = shard.astype(BF16)
+    write_spans(pay_ref, SHARD, both)
 
 
 def join_chips(own, span, lead, got):
@@ -275,14 +341,15 @@
         in_specs=[VMEM] * 6,
         out_specs=[VMEM] * 7,
         out_shape=[
-            HALF_SUM,
+            SHARD_SUM,
             SMALL,
             SMALL,
             SMALL,
             SMALL,
-            HALF_PAY,
+            SHARD_PAY,
             jax.ShapeDtypeStruct((FEATURES, STATE), BF16),
         ],
+        scratch_shapes=[pltpu.VMEM((HALF, STATE), F32)],
         compiler_params=pltpu.CompilerParams(**PARAMS),
         name="join_chips",
     )(own, span, lead, *got)
@@ -488,44 +555,40 @@
         resets, inputs, state_in, state_out, log_decay, level_weight
     )
     one = swap(pay, "seq", 1)
-    half, span, lead, one_factor, pay = join(0, total, span, one)
+    half, span, lead, one_factor, pay = join_cores(total, span, one)
     within = (resets, skip, x, b, c, log, weights, far, starts, one, one_factor)
     got = [swap(pay, "seq", distance) for distance in (2, 6, 4)]
     parts = inner(0, within, None)
     parts = inner(2, within, parts)
     got, parts = lax.optimization_barrier((got, parts))
-    half, span, lead, two_factor, three_factor, pay, mine = join_chips(
+    shard, span, lead, two_factor, three_factor, pay, mine = join_chips(
         half, span, lead, (got[0], got[2], got[1])
     )
     four = swap(pay, "seq", 8)
+    mine, pay = lax.optimization_barrier((mine, pay))
     other = swap(mine, "seq", 1)
     parts = inner(4, within, parts)
+    four, parts = lax.optimization_barrier((four, parts))
+    shard, span, lead, four_factor, pay = join(3, shard, span, lead, four)
+    five = swap(pay, "seq", 16)
+    pay, parts = lax.optimization_barrier((pay, parts))
     parts = inner(6, within, parts)
-    four, parts = lax.optimization_barrier((four, parts))
-    half, span, lead, four_factor, pay = join(3, half, span, lead, four)
-    four, pay = lax.optimization_barrier((four, pay))
+    five, parts = lax.optimization_barrier((five, parts))
     y, flipped, coef = parts
-    five = swap(pay, "seq", 16)
-    four_other = swap(four, "seq", 1)
+    shard, span, lead, five_factor, pay, both = join(4, shard, span, lead, five, four)
+    six = swap(pay, "seq", 48, 5)
+    both, y = lax.optimization_barrier((both, y))
+    both_got = swap(both, "seq", 2)
     (y,) = add_levels((2, 3), False, [mine], [other], [two_factor, three_factor], y, flipped, coef)
-    five, y = lax.optimization_barrier((five, y))
-    half, span, lead, five_factor, pay = join(4, half, span, lead, five)
-    five, pay = lax.optimization_barrier((five, pay))
-    six = swap(pay, "seq", 48, 5)
-    five_other = swap(five, "seq", 1)
-    (y,) = add_levels(
-        (4, 5),
-        False,
-        [four, five],
-        [four_other, five_other],
-        [four_factor, five_factor],
-        y,
-        flipped,
-        coef,
-    )
-    six, y = lax.optimization_barrier((six, y))
-    six_other = swap(six, "seq", 1)
-    y, squares = add_levels((6,), True, [six], [six_other], [lead], y, flipped, coef)
+    both_got, six, y = lax.optimization_barrier((both_got, six, y))
+    six_got = swap(six, "seq", 2)
+    mine = gather(2, both, [both_got])
+    other = swap(mine, "seq", 1)
+    (y,) = add_levels((4, 5), False, [mine], [other], [four_factor, five_factor], y, flipped, coef)
+    six_got, y = lax.optimization_barrier((six_got, y))
+    mine = gather(1, six, [six_got])
+    other = swap(mine, "seq", 1)
+    y, squares = add_levels((6,), True, [mine], [other], [lead], y, flipped, coef)
     shares = [squares] + [
         lax.ppermute(squares, "head", [(i, i ^ d) for i in range(4)]) for d in (1, 3, 2)
     ]

time: 62 us -> 60.7 us (0.979); the launches traced: 60.9 us -> 60.6 us
  waiting for transfers between devices: 15 us -> 11.2 us
  starting transfers between devices: 19.4 us -> 22.8 us
    ppermute x11 -> x12, waiting for transfers between devices: 12.7 us -> 8.96 us  [swap(): return lax.ppermute(array, axis, route)]
    ppermute x11 -> x12, starting transfers between devices: 15.1 us -> 18.5 us  [swap(): return lax.ppermute(array, axis, route)]
    pallas_call x3 -> x2, Pallas kernels: 1.24 us -> 0.99 us  [join(): pl.pallas_call(functools.partial(join_kernel, bit), in_specs=[VMEM] * len...]
  transfers between devices with their start and end apart: 14 -> 15, of which waited for: 7 -> 8; matrix products, arithmetic and copies ran while one was open for 0% -> 0% of each run, Pallas kernels for 26% -> 26%
where the time goes in v3:
time: 60.7 us; the launch traced here: 60.6 us
  Pallas kernels  26.1 us (43%)
  starting transfers between devices  22.8 us (38%)
  waiting for transfers between devices  11.2 us (18%)
    ppermute x12, starting transfers between devices, swap(): return lax.ppermute(array, axis, route)  18.5 us
    ppermute x12, waiting for transfers between devices, swap(): return lax.ppermute(array, axis, route)  8.96 us
    pallas_call x4, Pallas kernels, inner(): pl.pallas_call(functools.partial(inner_kernel, range(chunk0, chunk0 + PIE...  7.86 us
    pallas_call x3, Pallas kernels, add_levels(): pl.pallas_call(functools.partial(level_kernel, levels, len(mine), final),...  6.51 us
    pallas_call x1, Pallas kernels, block_states(): pl.pallas_call(state_kernel, in_specs=[SMEM] + [ANY] * 5, out_specs=[VMEM...  5.83 us
    ppermute x3, starting transfers between devices, per_device(): lax.ppermute(squares, 'head', [(i, i ^ d) for i in range(4)])  4.31 us
    ppermute x3, waiting for transfers between devices, per_device(): lax.ppermute(squares, 'head', [(i, i ^ d) for i in range(4)])  2.27 us
    pallas_call x1, Pallas kernels, normalize(): pl.pallas_call(norm_kernel, in_specs=[VMEM] * 5, out_specs=ANY, out_shape...  2.23 us
  transfers between devices with their start and end apart: 15, of which 8 were waited for; matrix products, arithmetic and copies ran while one was open for 0% of the time, Pallas kernels for 26%

profile of v3, /device:TPU:16, one launch (start us, length us, event | category | flops | bytes accessed | tf_op | source)
XLA Modules:
  0.0 60.6 jit_solution(14526940806686471550)
XLA Ops:
  0.0 5.8 %block_states.1 = (f32[1024,128]{1,0:T(8,128)S(1)}, bf16[1040,128]{1,0:T(8,128)(2,1)S(1)}, bf16[8,1024,128]{2,1,0:T(8,128)(2,1)S(1)}, f32[16,2048]{1,0:T(8,128)S...) custom-call(s32[4]{0:T(128)} %listed.9, ...), custom_call_target="tpu_custom_call" | custom-call | tf_op jit(solution)/shard_map/block_states/pallas_call | solution.py:160
  5.8 0.1 collective-permute-start
  5.9 1.5 %collective-permute-done.got_ref = bf16[1040,128]{1,0:T(8,128)(2,1)S(1)} collective-permute-done((bf16[1040,128]{1,0:T(8,128)(2,1)S(1)}, bf16[1040,128]{1,0:T(8,128)(2,1)S(1)}, u32[]{:S(2)}, u32[]{:S(2)}) %collective-permute-start) | collective-permute-done | bytes 266272 | tf_op jit(solution)/shard_map/ppermute | solution.py:550
  7.5 0.2 join_cores.1
  7.6 1.4 %collective-permute-start.1 = (bf16[528,128]{1,0:T(8,128)(2,1)S(1)}, bf16[528,128]{1,0:T(8,128)(2,1)S(1)}, u32[]{:S(2)}, u32[]{:S(2)}) collective-permute-start(bf16[528,128]{1,0:T(8,128)(2,1)S(1)} %get-tuple-element.81), channel_id=1, source_target_pairs={{0,8},{4,12},{8,0},{12,4},{16,24},{20,28},{24,16},{28,20},{32,40},... | collective-permute-start | bytes 405512 | tf_op jit(solution)/shard_map/ppermute | solution.py:550
  9.0 1.4 %collective-permute-start.2 = (bf16[528,128]{1,0:T(8,128)(2,1)S(1)}, bf16[528,128]{1,0:T(8,128)(2,1)S(1)}, u32[]{:S(2)}, u32[]{:S(2)}) collective-permute-start(bf16[528,128]{1,0:T(8,128)(2,1)S(1)} %get-tuple-element.81), channel_id=1, source_target_pairs={{0,24},{4,28},{8,16},{12,20},{16,8},{20,12},{24,0},{28,4},{32,56},... | collective-permute-start | bytes 405512 | tf_op jit(solution)/shard_map/ppermute | solution.py:550
  10.4 1.5 %collective-permute-start.3 = (bf16[528,128]{1,0:T(8,128)(2,1)S(1)}, bf16[528,128]{1,0:T(8,128)(2,1)S(1)}, u32[]{:S(2)}, u32[]{:S(2)}) collective-permute-start(bf16[528,128]{1,0:T(8,128)(2,1)S(1)} %get-tuple-element.81), channel_id=1, source_target_pairs={{0,16},{4,20},{8,24},{12,28},{16,0},{20,4},{24,8},{28,12},{32,48},... | collective-permute-start | bytes 405512 | tf_op jit(solution)/shard_map/ppermute | solution.py:550
  11.8 2.0 %inner0.1 = (f32[8,1024,256]{2,1,0:T(8,128)S(1)}, bf16[128,2048]{1,0:T(8,128)(2,1)S(1)}, f32[5,16,2048]{2,1,0:T(8,128)S(1)}) custom-call(s32[4]{0:T(128)} %listed.9, f32[16]{0:T(128)} %skip.7, bf16[8,1024,256]{2,1,0:T(8,128)(2,1)S(1)} %get-tuple-element.82.x_ref, bf16[2048,128]{1,0:T(8,128)(2,1)S(1)} %get-tuple-element.83.b_ref, ...), custom_call_target="tpu_custom_call" | custom-call | flops 805306368 | bytes 4000000 | tf_op jit(solution)/shard_map/inner0/pallas_call | solution.py:416
  13.8 2.0 %inner2.1 = (f32[8,1024,256]{2,1,0:T(8,128)S(1)}, bf16[128,2048]{1,0:T(8,128)(2,1)S(1)}, f32[5,16,2048]{2,1,0:T(8,128)S(1)}) custom-call(s32[4]{0:T(128)} %listed.9, f32[16]{0:T(128)} %skip.7, bf16[8,1024,256]{2,1,0:T(8,128)(2,1)S(1)} %get-tuple-element.82.x_ref, ...), custom_call_target="tpu_custom_call", output_to_operand_aliasing={{0}: (11, {}), {1}: (12, {}), {2}: (13, {})} | custom-call | flops 805306368 | bytes 4000000 | tf_op jit(solution)/shard_map/inner2/pallas_call | solution.py:416
  15.8 0.0 collective-permute-done.1.one_ref
  15.8 1.5 %collective-permute-done.2.three_ref = bf16[528,128]{1,0:T(8,128)(2,1)S(1)} collective-permute-done((bf16[528,128]{1,0:T(8,128)(2,1)S(1)}, bf16[528,128]{1,0:T(8,128)(2,1)S(1)}, u32[]{:S(2)}, u32[]{:S(2)}) %collective-permute-start.2) | collective-permute-done | bytes 135200 | tf_op jit(solution)/shard_map/ppermute | solution.py:550
  17.3 0.0 collective-permute-done.3.two_ref
  17.3 0.3 join_chips.1
  17.5 0.1 collective-permute-start.8
  17.6 2.0 %collective-permute-start.4 = (bf16[272,128]{1,0:T(8,128)(2,1)S(1)}, bf16[272,128]{1,0:T(8,128)(2,1)S(1)}, u32[]{:S(2)}, u32[]{:S(2)}) collective-permute-start(bf16[272,128]{1,0:T(8,128)(2,1)S(1)} %get-tuple-element.102), channel_id=1, source_target_pairs={{0,32},{4,36},{8,40},{12,44},{16,48},{20,52},{24,56},{28,60},{32,0... | collective-permute-start | bytes 208904 | tf_op jit(solution)/shard_map/ppermute | solution.py:550
  19.6 2.0 %inner4.1 = (f32[8,1024,256]{2,1,0:T(8,128)S(1)}, bf16[128,2048]{1,0:T(8,128)(2,1)S(1)}, f32[5,16,2048]{2,1,0:T(8,128)S(1)}) custom-call(s32[4]{0:T(128)} %listed.9, f32[16]{0:T(128)} %skip.7, bf16[8,1024,256]{2,1,0:T(8,128)(2,1)S(1)} %get-tuple-element.82.x_ref, ...), custom_call_target="tpu_custom_call", output_to_operand_aliasing={{0}: (11, {}), {1}: (12, {}), {2}: (13, {})} | custom-call | flops 805306368 | bytes 4000000 | tf_op jit(solution)/shard_map/inner4/pallas_call | solution.py:416
  21.6 0.8 %collective-permute-done.4.got_ref.rest_0_ = bf16[272,128]{1,0:T(8,128)(2,1)S(1)} collective-permute-done((bf16[272,128]{1,0:T(8,128)(2,1)S(1)}, bf16[272,128]{1,0:T(8,128)(2,1)S(1)}, u32[]{:S(2)}, u32[]{:S(2)}) %collective-permute-start.4) | collective-permute-done | bytes 69664 | tf_op jit(solution)/shard_map/ppermute | solution.py:550
  22.4 0.2 join3.1
  22.6 3.5 %collective-permute-start.5 = (bf16[272,128]{1,0:T(8,128)(2,1)S(1)}, bf16[272,128]{1,0:T(8,128)(2,1)S(1)}, u32[]{:S(2)}, u32[]{:S(2)}) collective-permute-start(bf16[272,128]{1,0:T(8,128)(2,1)S(1)} %get-tuple-element.110), channel_id=1, source_target_pairs={{0,64},{4,68},{8,72},{12,76},{16,80},{20,84},{24,88},{28,92},{32,9... | collective-permute-start | bytes 208904 | tf_op jit(solution)/shard_map/ppermute | solution.py:550
  26.1 2.0 %inner6.1 = (f32[8,1024,256]{2,1,0:T(8,128)S(1)}, bf16[128,2048]{1,0:T(8,128)(2,1)S(1)}, f32[5,16,2048]{2,1,0:T(8,128)S(1)}) custom-call(s32[4]{0:T(128)} %listed.9, f32[16]{0:T(128)} %skip.7, bf16[8,1024,256]{2,1,0:T(8,128)(2,1)S(1)} %get-tuple-element.82.x_ref, ...), custom_call_target="tpu_custom_call", output_to_operand_aliasing={{0}: (11, {}), {1}: (12, {}), {2}: (13, {})} | custom-call | flops 805306368 | bytes 4000000 | tf_op jit(solution)/shard_map/inner6/pallas_call | solution.py:416
  28.1 1.8 %collective-permute-done.5.got_ref = bf16[272,128]{1,0:T(8,128)(2,1)S(1)} collective-permute-done((bf16[272,128]{1,0:T(8,128)(2,1)S(1)}, bf16[272,128]{1,0:T(8,128)(2,1)S(1)}, u32[]{:S(2)}, u32[]{:S(2)}) %collective-permute-start.5) | collective-permute-done | bytes 69664 | tf_op jit(solution)/shard_map/ppermute | solution.py:550
  29.9 0.8 %join4.1 = (f32[256,128]{1,0:T(8,128)}, f32[16,128]{1,0:T(8,128)}, f32[16,128]{1,0:T(8,128)S(1)}, f32[16,128]{1,0:T(8,128)S(1)}, bf16[272,128]{1,0:T(8,128)(2,1)S(1)}, /*index=5*/bf16[512,128]{1,0:T(8,128)(2,1)S(1)}) custom-call(f32[256,128]{1,0:T(8,128)S(1)} %get-tuple-element.122.own_ref, f32[16,128]{1,0:T(8,128)S(1)} %get-tuple-element.123.span_ref, ...), custom_call_target="tpu_custom_call" | custom-call | tf_op jit(solution)/shard_map/join4/pallas_call | solution.py:271
  30.7 2.0 %collective-permute-start.6 = (bf16[512,128]{1,0:T(8,128)(2,1)S(1)}, bf16[512,128]{1,0:T(8,128)(2,1)S(1)}, u32[]{:S(2)}, u32[]{:S(2)}) collective-permute-start(bf16[512,128]{1,0:T(8,128)(2,1)S(1)} %get-tuple-element.128.refs_0_), channel_id=1, source_target_pairs={{0,8},{4,12},{8,0},{12,4},{16,24},{20,28},{24,16},{28,20},{32,40},... | collective-permute-start | bytes 393224 | tf_op jit(solution)/shard_map/ppermute | solution.py:550
  32.7 6.3 %collective-permute-start.7 = (bf16[272,128]{1,0:T(8,128)(2,1)S(1)}, bf16[272,128]{1,0:T(8,128)(2,1)S(1)}, u32[]{:S(2)}, u32[]{:S(2)}) collective-permute-start(bf16[272,128]{1,0:T(8,128)(2,1)S(1)} %get-tuple-element.129), channel_id=1, source_target_pairs={{0,192},{4,196},{8,200},{12,204},{16,208},{20,212},{24,216},{28,22... | collective-permute-start | bytes 208904 | tf_op jit(solution)/shard_map/ppermute | solution.py:550
  39.0 0.0 collective-permute-done.8.rest_1_
  39.0 2.4 %levels2.1.rest_4_ = f32[8,1024,256]{2,1,0:T(8,128)S(1)} custom-call(bf16[128,2048]{1,0:T(8,128)(2,1)S(1)} %get-tuple-element.120.flipped_ref, f32[5,16,2048]{2,1,0:T(8,128)S(1)} %get-tuple-element.121.coef_ref, bf16[1024,128]{1,0:T(8,128)(2,1)S(1)} %get-tuple-element.131.rest_0_, ...), custom_call_target="tpu_custom_call", output_to_operand_aliasing={{}: (6, {})} | custom-call | flops 2147483648 | bytes 4000000 | tf_op jit(solution)/shard_map/levels2/pallas_call | solution.py:472
  41.4 0.0 collective-permute-done.7.refs_0_
  41.4 0.0 collective-permute-done.6.refs_1_
  41.5 0.1 collective-permute-start.10
  41.6 0.2 collective-permute-start.9
  41.7 1.4 %collective-permute-done.10.rest_1_ = bf16[1024,128]{1,0:T(8,128)(2,1)S(1)} collective-permute-done((bf16[1024,128]{1,0:T(8,128)(2,1)S(1)}, bf16[1024,128]{1,0:T(8,128)(2,1)S(1)}, u32[]{:S(2)}, u32[]{:S(2)}) %collective-permute-start.10) | collective-permute-done | bytes 262176 | tf_op jit(solution)/shard_map/ppermute | solution.py:550
  43.1 2.4 %levels4.1.rest_3_ = f32[8,1024,256]{2,1,0:T(8,128)S(1)} custom-call(bf16[128,2048]{1,0:T(8,128)(2,1)S(1)} %get-tuple-element.120.flipped_ref, f32[5,16,2048]{2,1,0:T(8,128)S(1)} %get-tuple-element.121.coef_ref, bf16[1024,128]{1,0:T(8,128)(2,1)S(1)} %gather2.1.rest_0_, ...), custom_call_target="tpu_custom_call", output_to_operand_aliasing={{}: (6, {})} | custom-call | flops 2147483648 | bytes 4000000 | tf_op jit(solution)/shard_map/levels4/pallas_call | solution.py:472
  45.5 0.0 copy-start
  45.5 0.7 %collective-permute-done.9.refs_1_ = bf16[272,128]{1,0:T(8,128)(2,1)S(1)} collective-permute-done((bf16[272,128]{1,0:T(8,128)(2,1)S(1)}, bf16[272,128]{1,0:T(8,128)(2,1)S(1)}, u32[]{:S(2)}, u32[]{:S(2)}) %collective-permute-start.9) | collective-permute-done | bytes 69664 | tf_op jit(solution)/shard_map/ppermute | solution.py:550
  46.2 0.1 collective-permute-start.11
  46.3 1.3 %collective-permute-done.11.rest_1_ = bf16[512,128]{1,0:T(8,128)(2,1)S(1)} collective-permute-done((bf16[512,128]{1,0:T(8,128)(2,1)S(1)}, bf16[512,128]{1,0:T(8,128)(2,1)S(1)}, u32[]{:S(2)}, u32[]{:S(2)}) %collective-permute-start.11) | collective-permute-done | bytes 131104 | tf_op jit(solution)/shard_map/ppermute | solution.py:550
  47.6 1.7 %levels6.1 = (f32[8,1024,256]{2,1,0:T(8,128)S(1)}, f32[8,1,256]{2,1,0:T(1,128)S(1)}) custom-call(bf16[128,2048]{1,0:T(8,128)(2,1)S(1)} %get-tuple-element.120.flipped_ref, f32[5,16,2048]{2,1,0:T(8,128)S(1)} %get-tuple-element.121.coef_ref, bf16[512,128]{1,0:T(8,128)(2,1)S(1)} %gather1.1.rest_0_, ...), custom_call_target="tpu_custom_call", output_to_operand_aliasing={{0}: (5, {})} | custom-call | flops 1073741824 | bytes 4000000 | tf_op jit(solution)/shard_map/levels6/pallas_call | solution.py:472
  49.3 1.6 %collective-permute-start.12 = (f32[8,1,256]{2,1,0:T(1,128)S(1)}, f32[8,1,256]{2,1,0:T(1,128)S(1)}, u32[]{:S(2)}, u32[]{:S(2)}) collective-permute-start(f32[8,1,256]{2,1,0:T(1,128)S(1)} %get-tuple-element.144.s0), channel_id=1, source_target_pairs={{0,1},{1,0},{2,3},{3,2},{4,5},{5,4},{6,7},{7,6},{8,9},{9,8},{10,11... | collective-permute-start | bytes 24584 | tf_op jit(solution)/shard_map/ppermute | solution.py:593
  50.9 2.1 %collective-permute-start.13 = (f32[8,1,256]{2,1,0:T(1,128)S(1)}, f32[8,1,256]{2,1,0:T(1,128)S(1)}, u32[]{:S(2)}, u32[]{:S(2)}) collective-permute-start(f32[8,1,256]{2,1,0:T(1,128)S(1)} %get-tuple-element.144.s0), channel_id=1, source_target_pairs={{0,3},{1,2},{2,1},{3,0},{4,7},{5,6},{6,5},{7,4},{8,11},{9,10},{10,... | collective-permute-start | bytes 24584 | tf_op jit(solution)/shard_map/ppermute | solution.py:593
  53.0 0.6 %collective-permute-start.14 = (f32[8,1,256]{2,1,0:T(1,128)S(1)}, f32[8,1,256]{2,1,0:T(1,128)S(1)}, u32[]{:S(2)}, u32[]{:S(2)}) collective-permute-start(f32[8,1,256]{2,1,0:T(1,128)S(1)} %get-tuple-element.144.s0), channel_id=1, source_target_pairs={{0,2},{1,3},{2,0},{3,1},{4,6},{5,7},{6,4},{7,5},{8,10},{9,11},{10,... | collective-permute-start | bytes 24584 | tf_op jit(solution)/shard_map/ppermute | solution.py:593
  53.6 0.0 copy-done
  53.6 2.2 %flip.1.y_ref = f32[2048,1024]{1,0:T(8,128)S(1)} custom-call(f32[8,1024,256]{2,1,0:T(8,128)S(1)} %get-tuple-element.143.y_ref, f32[1,1024]{1,0:T(1,128)S(1)} %bitcast.1), custom_call_target="tpu_custom_call" | custom-call | bytes 16000000 | tf_op jit(solution)/shard_map/flip/pallas_call | solution.py:499
  55.9 0.0 collective-permute-done.12.s1
  55.9 0.0 collective-permute-done.13.s2
  55.9 2.3 %collective-permute-done.14.s3 = f32[8,1,256]{2,1,0:T(1,128)S(1)} collective-permute-done((f32[8,1,256]{2,1,0:T(1,128)S(1)}, f32[8,1,256]{2,1,0:T(1,128)S(1)}, u32[]{:S(2)}, u32[]{:S(2)}) %collective-permute-start.14) | collective-permute-done | bytes 8224 | tf_op jit(solution)/shard_map/ppermute | solution.py:593
  58.1 2.2 %normalize.1 = bf16[2048,1024]{1,0:T(8,128)(2,1)} custom-call(f32[2048,1024]{1,0:T(8,128)S(1)} %flip.1.y_ref, f32[8,1,256]{2,1,0:T(1,128)S(1)} %get-tuple-element.144.s0, f32[8,1,256]{2,1,0:T(1,128)S(1)} %collective-permute-done.12.s1, f32[8,1,256]{2,1,0:T(1,128)S(1)} %collective-permute-done.13.s2, f32[8,1,256]{2,1,0:T(1,128)S(1)} %collective-permute-done.14.s3), custom_call_target="tpu_custom_call" | custom-call | tf_op jit(solution)/shard_map/normalize/pallas_call | solution.py:529
  (2 shorter events, 0.0 us)
Async XLA Ops:
  5.8 1.6 %collective-permute-start = (bf16[1040,128]{1,0:T(8,128)(2,1)S(1)}, bf16[1040,128]{1,0:T(8,128)(2,1)S(1)}, u32[]{:S(2)}, u32[]{:S(2)}) collective-permute-start(bf16[1040,128]{1,0:T(8,128)(2,1)S(1)} %get-tuple-element.77), channel_id=1, source_target_pairs={{0,4},{4,0},{8,12},{12,8},{16,20},{20,16},{24,28},{28,24},{32,36},... | collective-permute-start | bytes 798728 | tf_op jit(solution)/shard_map/ppermute | solution.py:550
  7.6 8.1 %collective-permute-start.1 = (bf16[528,128]{1,0:T(8,128)(2,1)S(1)}, bf16[528,128]{1,0:T(8,128)(2,1)S(1)}, u32[]{:S(2)}, u32[]{:S(2)}) collective-permute-start(bf16[528,128]{1,0:T(8,128)(2,1)S(1)} %get-tuple-element.81), channel_id=1, source_target_pairs={{0,8},{4,12},{8,0},{12,4},{16,24},{20,28},{24,16},{28,20},{32,40},... | collective-permute-start | bytes 405512 | tf_op jit(solution)/shard_map/ppermute | solution.py:550
  9.0 8.2 %collective-permute-start.2 = (bf16[528,128]{1,0:T(8,128)(2,1)S(1)}, bf16[528,128]{1,0:T(8,128)(2,1)S(1)}, u32[]{:S(2)}, u32[]{:S(2)}) collective-permute-start(bf16[528,128]{1,0:T(8,128)(2,1)S(1)} %get-tuple-element.81), channel_id=1, source_target_pairs={{0,24},{4,28},{8,16},{12,20},{16,8},{20,12},{24,0},{28,4},{32,56},... | collective-permute-start | bytes 405512 | tf_op jit(solution)/shard_map/ppermute | solution.py:550
  10.4 6.9 %collective-permute-start.3 = (bf16[528,128]{1,0:T(8,128)(2,1)S(1)}, bf16[528,128]{1,0:T(8,128)(2,1)S(1)}, u32[]{:S(2)}, u32[]{:S(2)}) collective-permute-start(bf16[528,128]{1,0:T(8,128)(2,1)S(1)} %get-tuple-element.81), channel_id=1, source_target_pairs={{0,16},{4,20},{8,24},{12,28},{16,0},{20,4},{24,8},{28,12},{32,48},... | collective-permute-start | bytes 405512 | tf_op jit(solution)/shard_map/ppermute | solution.py:550
  17.5 21.4 %collective-permute-start.8 = (bf16[1024,128]{1,0:T(8,128)(2,1)S(1)}, bf16[1024,128]{1,0:T(8,128)(2,1)S(1)}, u32[]{:S(2)}, u32[]{:S(2)}) collective-permute-start(bf16[1024,128]{1,0:T(8,128)(2,1)S(1)} %get-tuple-element.131.rest_0_), channel_id=1, source_target_pairs={{0,4},{4,0},{8,12},{12,8},{16,20},{20,16},{24,28},{28,24},{32,36},... | collective-permute-start | bytes 786440 | tf_op jit(solution)/shard_map/ppermute | solution.py:550
  17.6 4.8 %collective-permute-start.4 = (bf16[272,128]{1,0:T(8,128)(2,1)S(1)}, bf16[272,128]{1,0:T(8,128)(2,1)S(1)}, u32[]{:S(2)}, u32[]{:S(2)}) collective-permute-start(bf16[272,128]{1,0:T(8,128)(2,1)S(1)} %get-tuple-element.102), channel_id=1, source_target_pairs={{0,32},{4,36},{8,40},{12,44},{16,48},{20,52},{24,56},{28,60},{32,0... | collective-permute-start | bytes 208904 | tf_op jit(solution)/shard_map/ppermute | solution.py:550
  22.6 7.3 %collective-permute-start.5 = (bf16[272,128]{1,0:T(8,128)(2,1)S(1)}, bf16[272,128]{1,0:T(8,128)(2,1)S(1)}, u32[]{:S(2)}, u32[]{:S(2)}) collective-permute-start(bf16[272,128]{1,0:T(8,128)(2,1)S(1)} %get-tuple-element.110), channel_id=1, source_target_pairs={{0,64},{4,68},{8,72},{12,76},{16,80},{20,84},{24,88},{28,92},{32,9... | collective-permute-start | bytes 208904 | tf_op jit(solution)/shard_map/ppermute | solution.py:550
  30.7 10.7 %collective-permute-start.6 = (bf16[512,128]{1,0:T(8,128)(2,1)S(1)}, bf16[512,128]{1,0:T(8,128)(2,1)S(1)}, u32[]{:S(2)}, u32[]{:S(2)}) collective-permute-start(bf16[512,128]{1,0:T(8,128)(2,1)S(1)} %get-tuple-element.128.refs_0_), channel_id=1, source_target_pairs={{0,8},{4,12},{8,0},{12,4},{16,24},{20,28},{24,16},{28,20},{32,40},... | collective-permute-start | bytes 393224 | tf_op jit(solution)/shard_map/ppermute | solution.py:550
  32.7 8.7 %collective-permute-start.7 = (bf16[272,128]{1,0:T(8,128)(2,1)S(1)}, bf16[272,128]{1,0:T(8,128)(2,1)S(1)}, u32[]{:S(2)}, u32[]{:S(2)}) collective-permute-start(bf16[272,128]{1,0:T(8,128)(2,1)S(1)} %get-tuple-element.129), channel_id=1, source_target_pairs={{0,192},{4,196},{8,200},{12,204},{16,208},{20,212},{24,216},{28,22... | collective-permute-start | bytes 208904 | tf_op jit(solution)/shard_map/ppermute | solution.py:550
  41.5 1.6 %collective-permute-start.10 = (bf16[1024,128]{1,0:T(8,128)(2,1)S(1)}, bf16[1024,128]{1,0:T(8,128)(2,1)S(1)}, u32[]{:S(2)}, u32[]{:S(2)}) collective-permute-start(bf16[1024,128]{1,0:T(8,128)(2,1)S(1)} %gather2.1.rest_0_), channel_id=1, source_target_pairs={{0,4},{4,0},{8,12},{12,8},{16,20},{20,16},{24,28},{28,24},{32,36},... | collective-permute-start | bytes 786440 | tf_op jit(solution)/shard_map/ppermute | solution.py:550
  41.6 4.6 %collective-permute-start.9 = (bf16[272,128]{1,0:T(8,128)(2,1)S(1)}, bf16[272,128]{1,0:T(8,128)(2,1)S(1)}, u32[]{:S(2)}, u32[]{:S(2)}) collective-permute-start(bf16[272,128]{1,0:T(8,128)(2,1)S(1)} %collective-permute-done.7.refs_0_), channel_id=1, source_target_pairs={{0,8},{4,12},{8,0},{12,4},{16,24},{20,28},{24,16},{28,20},{32,40},... | collective-permute-start | bytes 208904 | tf_op jit(solution)/shard_map/ppermute | solution.py:550
  45.5 8.1 %copy-start = (f32[1024]{0:T(1024)S(1)}, f32[1024]{0:T(1024)}, u32[]{:S(2)}) copy-start(f32[1024]{0:T(1024)} %param.14) | copy-start | bytes 12292
  46.2 1.4 %collective-permute-start.11 = (bf16[512,128]{1,0:T(8,128)(2,1)S(1)}, bf16[512,128]{1,0:T(8,128)(2,1)S(1)}, u32[]{:S(2)}, u32[]{:S(2)}) collective-permute-start(bf16[512,128]{1,0:T(8,128)(2,1)S(1)} %gather1.1.rest_0_), channel_id=1, source_target_pairs={{0,4},{4,0},{8,12},{12,8},{16,20},{20,16},{24,28},{28,24},{32,36},... | collective-permute-start | bytes 393224 | tf_op jit(solution)/shard_map/ppermute | solution.py:550
  49.3 6.5 %collective-permute-start.12 = (f32[8,1,256]{2,1,0:T(1,128)S(1)}, f32[8,1,256]{2,1,0:T(1,128)S(1)}, u32[]{:S(2)}, u32[]{:S(2)}) collective-permute-start(f32[8,1,256]{2,1,0:T(1,128)S(1)} %get-tuple-element.144.s0), channel_id=1, source_target_pairs={{0,1},{1,0},{2,3},{3,2},{4,5},{5,4},{6,7},{7,6},{8,9},{9,8},{10,11... | collective-permute-start | bytes 24584 | tf_op jit(solution)/shard_map/ppermute | solution.py:593
  50.9 5.0 %collective-permute-start.13 = (f32[8,1,256]{2,1,0:T(1,128)S(1)}, f32[8,1,256]{2,1,0:T(1,128)S(1)}, u32[]{:S(2)}, u32[]{:S(2)}) collective-permute-start(f32[8,1,256]{2,1,0:T(1,128)S(1)} %get-tuple-element.144.s0), channel_id=1, source_target_pairs={{0,3},{1,2},{2,1},{3,0},{4,7},{5,6},{6,5},{7,4},{8,11},{9,10},{10,... | collective-permute-start | bytes 24584 | tf_op jit(solution)/shard_map/ppermute | solution.py:593
  53.0 5.2 %collective-permute-start.14 = (f32[8,1,256]{2,1,0:T(1,128)S(1)}, f32[8,1,256]{2,1,0:T(1,128)S(1)}, u32[]{:S(2)}, u32[]{:S(2)}) collective-permute-start(f32[8,1,256]{2,1,0:T(1,128)S(1)} %get-tuple-element.144.s0), channel_id=1, source_target_pairs={{0,2},{1,3},{2,0},{3,1},{4,6},{5,7},{6,4},{7,5},{8,10},{9,11},{10,... | collective-permute-start | bytes 24584 | tf_op jit(solution)/shard_map/ppermute | solution.py:593

commit v4 on v3

--- a/solution.py
+++ b/solution.py
@@ -227,23 +227,27 @@
 
 
 def join_kernel(bit, own_ref, span_ref, lead_ref, got_ref, *rest):
-    *below, sum_ref, new_span_ref, new_lead_ref, factor_ref, pay_ref = rest[: 5 + len(rest) // 6]
-    if below:
-        rest[-1][:SHARD, :] = below[0][:SHARD, :]
-        rest[-1][SHARD:, :] = got_ref[:SHARD, :]
+    last = bit == 4
+    if last:
+        below, both_ref = rest[0], rest[1]
+        both_ref[:SHARD, :] = below[:SHARD, :]
+        both_ref[SHARD:, :] = got_ref[:SHARD, :]
+    new_lead_ref, factor_ref, pay_ref = rest[-3:]
     upper = side(bit) == 1
     span, lead = span_ref[...], lead_ref[...]
     got_span = read_spans(got_ref, SHARD)
     factor_ref[...] = jnp.where(upper, lead, 0.0)
     new_lead_ref[...] = jnp.where(upper, lead * got_span, lead)
     both = span * got_span
-    new_span_ref[...] = both
+    if not last:
+        rest[1][...] = both
     for h in range(SHARD_HEADS):
         here = slice(h * HEAD_DIM, (h + 1) * HEAD_DIM)
         own_factor = jnp.where(upper, 1.0, shard_head(got_span, h))
         got_factor = jnp.where(upper, shard_head(span, h), 1.0)
         new = own_ref[here, :] * own_factor + got_ref[here, :].astype(F32) * got_factor
-        sum_ref[here, :] = new
+        if not last:
+            rest[0][here, :] = new
         pay_ref[here, :] = new.astype(BF16)
     write_spans(pay_ref, SHARD, both)
 
@@ -271,8 +275,8 @@
     return pl.pallas_call(
         functools.partial(join_kernel, bit),
         in_specs=[VMEM] * len(operands),
-        out_specs=[VMEM] * (5 + len(operands) // 5),
-        out_shape=[SHARD_SUM, SMALL, SMALL, SMALL, SHARD_PAY, SHARD_PAIR][: 5 + len(operands) // 5],
+        out_specs=[VMEM] * (4 if bit == 4 else 5),
+        out_shape=([SHARD_PAIR] if bit == 4 else [SHARD_SUM, SMALL]) + [SMALL, SMALL, SHARD_PAY],
         compiler_params=pltpu.CompilerParams(**PARAMS),
         name="join" + str(bit),
     )(*operands)
@@ -575,8 +579,8 @@
     parts = inner(6, within, parts)
     five, parts = lax.optimization_barrier((five, parts))
     y, flipped, coef = parts
-    shard, span, lead, five_factor, pay, both = join(4, shard, span, lead, five, four)
-    six = swap(pay, "seq", 48, 5)
+    both, lead, five_factor, pay = join(4, shard, span, lead, five, four)
+    six = swap(pay, "seq", 48)
     both, y = lax.optimization_barrier((both, y))
     both_got = swap(both, "seq", 2)
     (y,) = add_levels((2, 3), False, [mine], [other], [two_factor, three_factor], y, flipped, coef)

time: 60.7 us -> 58.4 us (0.962)
  starting transfers between devices: 22.8 us -> 21 us
    ppermute x12, starting transfers between devices: 18.5 us -> 16.7 us  [swap(): return lax.ppermute(array, axis, route)]
    pallas_call x2, Pallas kernels: 0.99 us -> 0.33 us  [join(): pl.pallas_call(functools.partial(join_kernel, bit), in_specs=[VMEM] * len...]
where the time goes in v4:
time: 58.4 us; the launch traced here: 58.1 us
  Pallas kernels  25.5 us (44%)
  starting transfers between devices  21 us (36%)
  waiting for transfers between devices  11.2 us (19%)
    ppermute x12, starting transfers between devices, swap(): return lax.ppermute(array, axis, route)  16.7 us
    ppermute x12, waiting for transfers between devices, swap(): return lax.ppermute(array, axis, route)  8.93 us
    pallas_call x4, Pallas kernels, inner(): pl.pallas_call(functools.partial(inner_kernel, range(chunk0, chunk0 + PIE...  7.86 us
    pallas_call x3, Pallas kernels, add_levels(): pl.pallas_call(functools.partial(level_kernel, levels, len(mine), final),...  6.5 us
    pallas_call x1, Pallas kernels, block_states(): pl.pallas_call(state_kernel, in_specs=[SMEM] + [ANY] * 5, out_specs=[VMEM...  5.83 us
    ppermute x3, starting transfers between devices, per_device(): lax.ppermute(squares, 'head', [(i, i ^ d) for i in range(4)])  4.32 us
    ppermute x3, waiting for transfers between devices, per_device(): lax.ppermute(squares, 'head', [(i, i ^ d) for i in range(4)])  2.27 us
    pallas_call x1, Pallas kernels, normalize(): pl.pallas_call(norm_kernel, in_specs=[VMEM] * 5, out_specs=ANY, out_shape...  2.23 us
  transfers between devices with their start and end apart: 15, of which 8 were waited for; matrix products, arithmetic and copies ran while one was open for 0% of the time, Pallas kernels for 26%

profile of v4, /device:TPU:16, one launch (start us, length us, event | category | flops | bytes accessed | tf_op | source)
XLA Modules:
  0.0 58.1 jit_solution(7342012255892762523)
XLA Ops:
  0.0 5.8 %block_states.1 = (f32[1024,128]{1,0:T(8,128)S(1)}, bf16[1040,128]{1,0:T(8,128)(2,1)S(1)}, bf16[8,1024,128]{2,1,0:T(8,128)(2,1)S(1)}, f32[16,2048]{1,0:T(8,128)S...) custom-call(s32[4]{0:T(128)} %listed.9, ...), custom_call_target="tpu_custom_call" | custom-call | tf_op jit(solution)/shard_map/block_states/pallas_call | solution.py:160
  5.8 0.1 collective-permute-start
  5.9 1.5 %collective-permute-done.got_ref = bf16[1040,128]{1,0:T(8,128)(2,1)S(1)} collective-permute-done((bf16[1040,128]{1,0:T(8,128)(2,1)S(1)}, bf16[1040,128]{1,0:T(8,128)(2,1)S(1)}, u32[]{:S(2)}, u32[]{:S(2)}) %collective-permute-start) | collective-permute-done | bytes 266272 | tf_op jit(solution)/shard_map/ppermute | solution.py:554
  7.5 0.2 join_cores.1
  7.6 1.4 %collective-permute-start.1 = (bf16[528,128]{1,0:T(8,128)(2,1)S(1)}, bf16[528,128]{1,0:T(8,128)(2,1)S(1)}, u32[]{:S(2)}, u32[]{:S(2)}) collective-permute-start(bf16[528,128]{1,0:T(8,128)(2,1)S(1)} %get-tuple-element.81), channel_id=1, source_target_pairs={{0,8},{4,12},{8,0},{12,4},{16,24},{20,28},{24,16},{28,20},{32,40},... | collective-permute-start | bytes 405512 | tf_op jit(solution)/shard_map/ppermute | solution.py:554
  9.0 1.4 %collective-permute-start.2 = (bf16[528,128]{1,0:T(8,128)(2,1)S(1)}, bf16[528,128]{1,0:T(8,128)(2,1)S(1)}, u32[]{:S(2)}, u32[]{:S(2)}) collective-permute-start(bf16[528,128]{1,0:T(8,128)(2,1)S(1)} %get-tuple-element.81), channel_id=1, source_target_pairs={{0,24},{4,28},{8,16},{12,20},{16,8},{20,12},{24,0},{28,4},{32,56},... | collective-permute-start | bytes 405512 | tf_op jit(solution)/shard_map/ppermute | solution.py:554
  10.4 1.5 %collective-permute-start.3 = (bf16[528,128]{1,0:T(8,128)(2,1)S(1)}, bf16[528,128]{1,0:T(8,128)(2,1)S(1)}, u32[]{:S(2)}, u32[]{:S(2)}) collective-permute-start(bf16[528,128]{1,0:T(8,128)(2,1)S(1)} %get-tuple-element.81), channel_id=1, source_target_pairs={{0,16},{4,20},{8,24},{12,28},{16,0},{20,4},{24,8},{28,12},{32,48},... | collective-permute-start | bytes 405512 | tf_op jit(solution)/shard_map/ppermute | solution.py:554
  11.8 2.0 %inner0.1 = (f32[8,1024,256]{2,1,0:T(8,128)S(1)}, bf16[128,2048]{1,0:T(8,128)(2,1)S(1)}, f32[5,16,2048]{2,1,0:T(8,128)S(1)}) custom-call(s32[4]{0:T(128)} %listed.9, f32[16]{0:T(128)} %skip.7, bf16[8,1024,256]{2,1,0:T(8,128)(2,1)S(1)} %get-tuple-element.82.x_ref, bf16[2048,128]{1,0:T(8,128)(2,1)S(1)} %get-tuple-element.83.b_ref, ...), custom_call_target="tpu_custom_call" | custom-call | flops 805306368 | bytes 4000000 | tf_op jit(solution)/shard_map/inner0/pallas_call | solution.py:420
  13.8 2.0 %inner2.1 = (f32[8,1024,256]{2,1,0:T(8,128)S(1)}, bf16[128,2048]{1,0:T(8,128)(2,1)S(1)}, f32[5,16,2048]{2,1,0:T(8,128)S(1)}) custom-call(s32[4]{0:T(128)} %listed.9, f32[16]{0:T(128)} %skip.7, bf16[8,1024,256]{2,1,0:T(8,128)(2,1)S(1)} %get-tuple-element.82.x_ref, ...), custom_call_target="tpu_custom_call", output_to_operand_aliasing={{0}: (11, {}), {1}: (12, {}), {2}: (13, {})} | custom-call | flops 805306368 | bytes 4000000 | tf_op jit(solution)/shard_map/inner2/pallas_call | solution.py:420
  15.8 0.0 collective-permute-done.1.one_ref
  15.8 1.5 %collective-permute-done.2.three_ref = bf16[528,128]{1,0:T(8,128)(2,1)S(1)} collective-permute-done((bf16[528,128]{1,0:T(8,128)(2,1)S(1)}, bf16[528,128]{1,0:T(8,128)(2,1)S(1)}, u32[]{:S(2)}, u32[]{:S(2)}) %collective-permute-start.2) | collective-permute-done | bytes 135200 | tf_op jit(solution)/shard_map/ppermute | solution.py:554
  17.3 0.0 collective-permute-done.3.two_ref
  17.3 0.3 join_chips.1
  17.5 0.1 collective-permute-start.8
  17.6 2.0 %collective-permute-start.4 = (bf16[272,128]{1,0:T(8,128)(2,1)S(1)}, bf16[272,128]{1,0:T(8,128)(2,1)S(1)}, u32[]{:S(2)}, u32[]{:S(2)}) collective-permute-start(bf16[272,128]{1,0:T(8,128)(2,1)S(1)} %get-tuple-element.102), channel_id=1, source_target_pairs={{0,32},{4,36},{8,40},{12,44},{16,48},{20,52},{24,56},{28,60},{32,0... | collective-permute-start | bytes 208904 | tf_op jit(solution)/shard_map/ppermute | solution.py:554
  19.6 2.0 %inner4.1 = (f32[8,1024,256]{2,1,0:T(8,128)S(1)}, bf16[128,2048]{1,0:T(8,128)(2,1)S(1)}, f32[5,16,2048]{2,1,0:T(8,128)S(1)}) custom-call(s32[4]{0:T(128)} %listed.9, f32[16]{0:T(128)} %skip.7, bf16[8,1024,256]{2,1,0:T(8,128)(2,1)S(1)} %get-tuple-element.82.x_ref, ...), custom_call_target="tpu_custom_call", output_to_operand_aliasing={{0}: (11, {}), {1}: (12, {}), {2}: (13, {})} | custom-call | flops 805306368 | bytes 4000000 | tf_op jit(solution)/shard_map/inner4/pallas_call | solution.py:420
  21.6 0.8 %collective-permute-done.4.got_ref.rest_0_ = bf16[272,128]{1,0:T(8,128)(2,1)S(1)} collective-permute-done((bf16[272,128]{1,0:T(8,128)(2,1)S(1)}, bf16[272,128]{1,0:T(8,128)(2,1)S(1)}, u32[]{:S(2)}, u32[]{:S(2)}) %collective-permute-start.4) | collective-permute-done | bytes 69664 | tf_op jit(solution)/shard_map/ppermute | solution.py:554
  22.4 0.2 join3.1
  22.6 3.5 %collective-permute-start.5 = (bf16[272,128]{1,0:T(8,128)(2,1)S(1)}, bf16[272,128]{1,0:T(8,128)(2,1)S(1)}, u32[]{:S(2)}, u32[]{:S(2)}) collective-permute-start(bf16[272,128]{1,0:T(8,128)(2,1)S(1)} %get-tuple-element.110), channel_id=1, source_target_pairs={{0,64},{4,68},{8,72},{12,76},{16,80},{20,84},{24,88},{28,92},{32,9... | collective-permute-start | bytes 208904 | tf_op jit(solution)/shard_map/ppermute | solution.py:554
  26.1 2.0 %inner6.1 = (f32[8,1024,256]{2,1,0:T(8,128)S(1)}, bf16[128,2048]{1,0:T(8,128)(2,1)S(1)}, f32[5,16,2048]{2,1,0:T(8,128)S(1)}) custom-call(s32[4]{0:T(128)} %listed.9, f32[16]{0:T(128)} %skip.7, bf16[8,1024,256]{2,1,0:T(8,128)(2,1)S(1)} %get-tuple-element.82.x_ref, ...), custom_call_target="tpu_custom_call", output_to_operand_aliasing={{0}: (11, {}), {1}: (12, {}), {2}: (13, {})} | custom-call | flops 805306368 | bytes 4000000 | tf_op jit(solution)/shard_map/inner6/pallas_call | solution.py:420
  28.1 1.8 %collective-permute-done.5.got_ref = bf16[272,128]{1,0:T(8,128)(2,1)S(1)} collective-permute-done((bf16[272,128]{1,0:T(8,128)(2,1)S(1)}, bf16[272,128]{1,0:T(8,128)(2,1)S(1)}, u32[]{:S(2)}, u32[]{:S(2)}) %collective-permute-start.5) | collective-permute-done | bytes 69664 | tf_op jit(solution)/shard_map/ppermute | solution.py:554
  29.9 0.2 join4.1
  30.1 2.0 %collective-permute-start.6 = (bf16[512,128]{1,0:T(8,128)(2,1)S(1)}, bf16[512,128]{1,0:T(8,128)(2,1)S(1)}, u32[]{:S(2)}, u32[]{:S(2)}) collective-permute-start(bf16[512,128]{1,0:T(8,128)(2,1)S(1)} %get-tuple-element.128.refs_0_), channel_id=1, source_target_pairs={{0,8},{4,12},{8,0},{12,4},{16,24},{20,28},{24,16},{28,20},{32,40},... | collective-permute-start | bytes 393224 | tf_op jit(solution)/shard_map/ppermute | solution.py:554
  32.1 4.4 %collective-permute-start.7 = (bf16[272,128]{1,0:T(8,128)(2,1)S(1)}, bf16[272,128]{1,0:T(8,128)(2,1)S(1)}, u32[]{:S(2)}, u32[]{:S(2)}) collective-permute-start(bf16[272,128]{1,0:T(8,128)(2,1)S(1)} %get-tuple-element.129), channel_id=1, source_target_pairs={{0,192},{4,196},{8,200},{12,204},{16,208},{20,212},{24,216},{28,22... | collective-permute-start | bytes 208904 | tf_op jit(solution)/shard_map/ppermute | solution.py:554
  36.5 0.0 collective-permute-done.8.rest_1_
  36.5 2.4 %levels2.1.rest_4_ = f32[8,1024,256]{2,1,0:T(8,128)S(1)} custom-call(bf16[128,2048]{1,0:T(8,128)(2,1)S(1)} %get-tuple-element.120.flipped_ref, f32[5,16,2048]{2,1,0:T(8,128)S(1)} %get-tuple-element.121.coef_ref, bf16[1024,128]{1,0:T(8,128)(2,1)S(1)} %get-tuple-element.131.rest_0_, ...), custom_call_target="tpu_custom_call", output_to_operand_aliasing={{}: (6, {})} | custom-call | flops 2147483648 | bytes 4000000 | tf_op jit(solution)/shard_map/levels2/pallas_call | solution.py:476
  38.9 0.0 collective-permute-done.7.refs_0_
  38.9 0.0 collective-permute-done.6.refs_1_
  39.0 0.1 collective-permute-start.10
  39.1 0.2 collective-permute-start.9
  39.3 1.3 %collective-permute-done.10.rest_1_ = bf16[1024,128]{1,0:T(8,128)(2,1)S(1)} collective-permute-done((bf16[1024,128]{1,0:T(8,128)(2,1)S(1)}, bf16[1024,128]{1,0:T(8,128)(2,1)S(1)}, u32[]{:S(2)}, u32[]{:S(2)}) %collective-permute-start.10) | collective-permute-done | bytes 262176 | tf_op jit(solution)/shard_map/ppermute | solution.py:554
  40.6 2.4 %levels4.1.rest_3_ = f32[8,1024,256]{2,1,0:T(8,128)S(1)} custom-call(bf16[128,2048]{1,0:T(8,128)(2,1)S(1)} %get-tuple-element.120.flipped_ref, f32[5,16,2048]{2,1,0:T(8,128)S(1)} %get-tuple-element.121.coef_ref, bf16[1024,128]{1,0:T(8,128)(2,1)S(1)} %gather2.1.rest_0_, ...), custom_call_target="tpu_custom_call", output_to_operand_aliasing={{}: (6, {})} | custom-call | flops 2147483648 | bytes 4000000 | tf_op jit(solution)/shard_map/levels4/pallas_call | solution.py:476
  43.0 0.0 copy-start
  43.0 0.7 %collective-permute-done.9.refs_1_ = bf16[272,128]{1,0:T(8,128)(2,1)S(1)} collective-permute-done((bf16[272,128]{1,0:T(8,128)(2,1)S(1)}, bf16[272,128]{1,0:T(8,128)(2,1)S(1)}, u32[]{:S(2)}, u32[]{:S(2)}) %collective-permute-start.9) | collective-permute-done | bytes 69664 | tf_op jit(solution)/shard_map/ppermute | solution.py:554
  43.7 0.1 collective-permute-start.11
  43.8 1.3 %collective-permute-done.11.rest_1_ = bf16[512,128]{1,0:T(8,128)(2,1)S(1)} collective-permute-done((bf16[512,128]{1,0:T(8,128)(2,1)S(1)}, bf16[512,128]{1,0:T(8,128)(2,1)S(1)}, u32[]{:S(2)}, u32[]{:S(2)}) %collective-permute-start.11) | collective-permute-done | bytes 131104 | tf_op jit(solution)/shard_map/ppermute | solution.py:554
  45.1 1.7 %levels6.1 = (f32[8,1024,256]{2,1,0:T(8,128)S(1)}, f32[8,1,256]{2,1,0:T(1,128)S(1)}) custom-call(bf16[128,2048]{1,0:T(8,128)(2,1)S(1)} %get-tuple-element.120.flipped_ref, f32[5,16,2048]{2,1,0:T(8,128)S(1)} %get-tuple-element.121.coef_ref, bf16[512,128]{1,0:T(8,128)(2,1)S(1)} %gather1.1.rest_0_, ...), custom_call_target="tpu_custom_call", output_to_operand_aliasing={{0}: (5, {})} | custom-call | flops 1073741824 | bytes 4000000 | tf_op jit(solution)/shard_map/levels6/pallas_call | solution.py:476
  46.8 1.6 %collective-permute-start.12 = (f32[8,1,256]{2,1,0:T(1,128)S(1)}, f32[8,1,256]{2,1,0:T(1,128)S(1)}, u32[]{:S(2)}, u32[]{:S(2)}) collective-permute-start(f32[8,1,256]{2,1,0:T(1,128)S(1)} %get-tuple-element.144.s0), channel_id=1, source_target_pairs={{0,1},{1,0},{2,3},{3,2},{4,5},{5,4},{6,7},{7,6},{8,9},{9,8},{10,11... | collective-permute-start | bytes 24584 | tf_op jit(solution)/shard_map/ppermute | solution.py:597
  48.4 2.1 %collective-permute-start.13 = (f32[8,1,256]{2,1,0:T(1,128)S(1)}, f32[8,1,256]{2,1,0:T(1,128)S(1)}, u32[]{:S(2)}, u32[]{:S(2)}) collective-permute-start(f32[8,1,256]{2,1,0:T(1,128)S(1)} %get-tuple-element.144.s0), channel_id=1, source_target_pairs={{0,3},{1,2},{2,1},{3,0},{4,7},{5,6},{6,5},{7,4},{8,11},{9,10},{10,... | collective-permute-start | bytes 24584 | tf_op jit(solution)/shard_map/ppermute | solution.py:597
  50.5 0.6 %collective-permute-start.14 = (f32[8,1,256]{2,1,0:T(1,128)S(1)}, f32[8,1,256]{2,1,0:T(1,128)S(1)}, u32[]{:S(2)}, u32[]{:S(2)}) collective-permute-start(f32[8,1,256]{2,1,0:T(1,128)S(1)} %get-tuple-element.144.s0), channel_id=1, source_target_pairs={{0,2},{1,3},{2,0},{3,1},{4,6},{5,7},{6,4},{7,5},{8,10},{9,11},{10,... | collective-permute-start | bytes 24584 | tf_op jit(solution)/shard_map/ppermute | solution.py:597
  51.1 0.0 copy-done
  51.2 2.2 %flip.1.y_ref = f32[2048,1024]{1,0:T(8,128)S(1)} custom-call(f32[8,1024,256]{2,1,0:T(8,128)S(1)} %get-tuple-element.143.y_ref, f32[1,1024]{1,0:T(1,128)S(1)} %bitcast.1), custom_call_target="tpu_custom_call" | custom-call | bytes 16000000 | tf_op jit(solution)/shard_map/flip/pallas_call | solution.py:503
  53.4 0.0 collective-permute-done.12.s1
  53.4 0.0 collective-permute-done.13.s2
  53.4 2.3 %collective-permute-done.14.s3 = f32[8,1,256]{2,1,0:T(1,128)S(1)} collective-permute-done((f32[8,1,256]{2,1,0:T(1,128)S(1)}, f32[8,1,256]{2,1,0:T(1,128)S(1)}, u32[]{:S(2)}, u32[]{:S(2)}) %collective-permute-start.14) | collective-permute-done | bytes 8224 | tf_op jit(solution)/shard_map/ppermute | solution.py:597
  55.7 2.2 %normalize.1 = bf16[2048,1024]{1,0:T(8,128)(2,1)} custom-call(f32[2048,1024]{1,0:T(8,128)S(1)} %flip.1.y_ref, f32[8,1,256]{2,1,0:T(1,128)S(1)} %get-tuple-element.144.s0, f32[8,1,256]{2,1,0:T(1,128)S(1)} %collective-permute-done.12.s1, f32[8,1,256]{2,1,0:T(1,128)S(1)} %collective-permute-done.13.s2, f32[8,1,256]{2,1,0:T(1,128)S(1)} %collective-permute-done.14.s3), custom_call_target="tpu_custom_call" | custom-call | tf_op jit(solution)/shard_map/normalize/pallas_call | solution.py:533
  (2 shorter events, 0.0 us)
Async XLA Ops:
  5.8 1.6 %collective-permute-start = (bf16[1040,128]{1,0:T(8,128)(2,1)S(1)}, bf16[1040,128]{1,0:T(8,128)(2,1)S(1)}, u32[]{:S(2)}, u32[]{:S(2)}) collective-permute-start(bf16[1040,128]{1,0:T(8,128)(2,1)S(1)} %get-tuple-element.77), channel_id=1, source_target_pairs={{0,4},{4,0},{8,12},{12,8},{16,20},{20,16},{24,28},{28,24},{32,36},... | collective-permute-start | bytes 798728 | tf_op jit(solution)/shard_map/ppermute | solution.py:554
  7.6 8.1 %collective-permute-start.1 = (bf16[528,128]{1,0:T(8,128)(2,1)S(1)}, bf16[528,128]{1,0:T(8,128)(2,1)S(1)}, u32[]{:S(2)}, u32[]{:S(2)}) collective-permute-start(bf16[528,128]{1,0:T(8,128)(2,1)S(1)} %get-tuple-element.81), channel_id=1, source_target_pairs={{0,8},{4,12},{8,0},{12,4},{16,24},{20,28},{24,16},{28,20},{32,40},... | collective-permute-start | bytes 405512 | tf_op jit(solution)/shard_map/ppermute | solution.py:554
  9.0 8.2 %collective-permute-start.2 = (bf16[528,128]{1,0:T(8,128)(2,1)S(1)}, bf16[528,128]{1,0:T(8,128)(2,1)S(1)}, u32[]{:S(2)}, u32[]{:S(2)}) collective-permute-start(bf16[528,128]{1,0:T(8,128)(2,1)S(1)} %get-tuple-element.81), channel_id=1, source_target_pairs={{0,24},{4,28},{8,16},{12,20},{16,8},{20,12},{24,0},{28,4},{32,56},... | collective-permute-start | bytes 405512 | tf_op jit(solution)/shard_map/ppermute | solution.py:554
  10.4 6.9 %collective-permute-start.3 = (bf16[528,128]{1,0:T(8,128)(2,1)S(1)}, bf16[528,128]{1,0:T(8,128)(2,1)S(1)}, u32[]{:S(2)}, u32[]{:S(2)}) collective-permute-start(bf16[528,128]{1,0:T(8,128)(2,1)S(1)} %get-tuple-element.81), channel_id=1, source_target_pairs={{0,16},{4,20},{8,24},{12,28},{16,0},{20,4},{24,8},{28,12},{32,48},... | collective-permute-start | bytes 405512 | tf_op jit(solution)/shard_map/ppermute | solution.py:554
  17.5 19.0 %collective-permute-start.8 = (bf16[1024,128]{1,0:T(8,128)(2,1)S(1)}, bf16[1024,128]{1,0:T(8,128)(2,1)S(1)}, u32[]{:S(2)}, u32[]{:S(2)}) collective-permute-start(bf16[1024,128]{1,0:T(8,128)(2,1)S(1)} %get-tuple-element.131.rest_0_), channel_id=1, source_target_pairs={{0,4},{4,0},{8,12},{12,8},{16,20},{20,16},{24,28},{28,24},{32,36},... | collective-permute-start | bytes 786440 | tf_op jit(solution)/shard_map/ppermute | solution.py:554
  17.6 4.8 %collective-permute-start.4 = (bf16[272,128]{1,0:T(8,128)(2,1)S(1)}, bf16[272,128]{1,0:T(8,128)(2,1)S(1)}, u32[]{:S(2)}, u32[]{:S(2)}) collective-permute-start(bf16[272,128]{1,0:T(8,128)(2,1)S(1)} %get-tuple-element.102), channel_id=1, source_target_pairs={{0,32},{4,36},{8,40},{12,44},{16,48},{20,52},{24,56},{28,60},{32,0... | collective-permute-start | bytes 208904 | tf_op jit(solution)/shard_map/ppermute | solution.py:554
  22.6 7.3 %collective-permute-start.5 = (bf16[272,128]{1,0:T(8,128)(2,1)S(1)}, bf16[272,128]{1,0:T(8,128)(2,1)S(1)}, u32[]{:S(2)}, u32[]{:S(2)}) collective-permute-start(bf16[272,128]{1,0:T(8,128)(2,1)S(1)} %get-tuple-element.110), channel_id=1, source_target_pairs={{0,64},{4,68},{8,72},{12,76},{16,80},{20,84},{24,88},{28,92},{32,9... | collective-permute-start | bytes 208904 | tf_op jit(solution)/shard_map/ppermute | solution.py:554
  30.1 8.9 %collective-permute-start.6 = (bf16[512,128]{1,0:T(8,128)(2,1)S(1)}, bf16[512,128]{1,0:T(8,128)(2,1)S(1)}, u32[]{:S(2)}, u32[]{:S(2)}) collective-permute-start(bf16[512,128]{1,0:T(8,128)(2,1)S(1)} %get-tuple-element.128.refs_0_), channel_id=1, source_target_pairs={{0,8},{4,12},{8,0},{12,4},{16,24},{20,28},{24,16},{28,20},{32,40},... | collective-permute-start | bytes 393224 | tf_op jit(solution)/shard_map/ppermute | solution.py:554
  32.1 6.8 %collective-permute-start.7 = (bf16[272,128]{1,0:T(8,128)(2,1)S(1)}, bf16[272,128]{1,0:T(8,128)(2,1)S(1)}, u32[]{:S(2)}, u32[]{:S(2)}) collective-permute-start(bf16[272,128]{1,0:T(8,128)(2,1)S(1)} %get-tuple-element.129), channel_id=1, source_target_pairs={{0,192},{4,196},{8,200},{12,204},{16,208},{20,212},{24,216},{28,22... | collective-permute-start | bytes 208904 | tf_op jit(solution)/shard_map/ppermute | solution.py:554
  39.0 1.6 %collective-permute-start.10 = (bf16[1024,128]{1,0:T(8,128)(2,1)S(1)}, bf16[1024,128]{1,0:T(8,128)(2,1)S(1)}, u32[]{:S(2)}, u32[]{:S(2)}) collective-permute-start(bf16[1024,128]{1,0:T(8,128)(2,1)S(1)} %gather2.1.rest_0_), channel_id=1, source_target_pairs={{0,4},{4,0},{8,12},{12,8},{16,20},{20,16},{24,28},{28,24},{32,36},... | collective-permute-start | bytes 786440 | tf_op jit(solution)/shard_map/ppermute | solution.py:554
  39.1 4.6 %collective-permute-start.9 = (bf16[272,128]{1,0:T(8,128)(2,1)S(1)}, bf16[272,128]{1,0:T(8,128)(2,1)S(1)}, u32[]{:S(2)}, u32[]{:S(2)}) collective-permute-start(bf16[272,128]{1,0:T(8,128)(2,1)S(1)} %collective-permute-done.7.refs_0_), channel_id=1, source_target_pairs={{0,8},{4,12},{8,0},{12,4},{16,24},{20,28},{24,16},{28,20},{32,40},... | collective-permute-start | bytes 208904 | tf_op jit(solution)/shard_map/ppermute | solution.py:554
  43.0 8.1 %copy-start = (f32[1024]{0:T(1024)S(1)}, f32[1024]{0:T(1024)}, u32[]{:S(2)}) copy-start(f32[1024]{0:T(1024)} %param.14) | copy-start | bytes 12292
  43.7 1.4 %collective-permute-start.11 = (bf16[512,128]{1,0:T(8,128)(2,1)S(1)}, bf16[512,128]{1,0:T(8,128)(2,1)S(1)}, u32[]{:S(2)}, u32[]{:S(2)}) collective-permute-start(bf16[512,128]{1,0:T(8,128)(2,1)S(1)} %gather1.1.rest_0_), channel_id=1, source_target_pairs={{0,4},{4,0},{8,12},{12,8},{16,20},{20,16},{24,28},{28,24},{32,36},... | collective-permute-start | bytes 393224 | tf_op jit(solution)/shard_map/ppermute | solution.py:554
  46.8 6.5 %collective-permute-start.12 = (f32[8,1,256]{2,1,0:T(1,128)S(1)}, f32[8,1,256]{2,1,0:T(1,128)S(1)}, u32[]{:S(2)}, u32[]{:S(2)}) collective-permute-start(f32[8,1,256]{2,1,0:T(1,128)S(1)} %get-tuple-element.144.s0), channel_id=1, source_target_pairs={{0,1},{1,0},{2,3},{3,2},{4,5},{5,4},{6,7},{7,6},{8,9},{9,8},{10,11... | collective-permute-start | bytes 24584 | tf_op jit(solution)/shard_map/ppermute | solution.py:597
  48.4 5.0 %collective-permute-start.13 = (f32[8,1,256]{2,1,0:T(1,128)S(1)}, f32[8,1,256]{2,1,0:T(1,128)S(1)}, u32[]{:S(2)}, u32[]{:S(2)}) collective-permute-start(f32[8,1,256]{2,1,0:T(1,128)S(1)} %get-tuple-element.144.s0), channel_id=1, source_target_pairs={{0,3},{1,2},{2,1},{3,0},{4,7},{5,6},{6,5},{7,4},{8,11},{9,10},{10,... | collective-permute-start | bytes 24584 | tf_op jit(solution)/shard_map/ppermute | solution.py:597
  50.5 5.2 %collective-permute-start.14 = (f32[8,1,256]{2,1,0:T(1,128)S(1)}, f32[8,1,256]{2,1,0:T(1,128)S(1)}, u32[]{:S(2)}, u32[]{:S(2)}) collective-permute-start(f32[8,1,256]{2,1,0:T(1,128)S(1)} %get-tuple-element.144.s0), channel_id=1, source_target_pairs={{0,2},{1,3},{2,0},{3,1},{4,6},{5,7},{6,4},{7,5},{8,10},{9,11},{10,... | collective-permute-start | bytes 24584 | tf_op jit(solution)/shard_map/ppermute | solution.py:597

commit v5 on v4

--- a/solution.py
+++ b/solution.py
@@ -24,6 +24,7 @@
 SHARD = HALF // CHIPS
 SHARD_HEADS = HALF_HEADS // CHIPS
 GROUP_HEADS = 8
+AHEAD = 3
 WIDE = GROUP_HEADS * HEAD_DIM
 GROUPS = HEADS // GROUP_HEADS
 SPAN_ROWS = HEADS
@@ -99,7 +100,7 @@
     for k in range(CHUNKS):
         rows = slice(k * CHUNK, (k + 1) * CHUNK)
         x_copies.append(pltpu.make_async_copy(x_any.at[rows, :], x_in.at[k], x_sems.at[k]))
-    for copy in [decay_copy, b_copy] + x_copies + later:
+    for copy in [decay_copy, b_copy] + x_copies[:AHEAD]:
         copy.start()
     state[...] = jnp.zeros_like(state)
     square = (CHUNK, CHUNK)
@@ -140,6 +141,11 @@
         middle = jnp.exp(0.5 * end)
         b = b_ref[lanes, :]
         x_copies[k].wait()
+        if k + AHEAD < CHUNKS:
+            x_copies[k + AHEAD].start()
+        if k + AHEAD == CHUNKS - 1:
+            for copy in later:
+                copy.start()
         for group in range(GROUPS):
             rows = slice(group * WIDE, (group + 1) * WIDE)
             held = state[rows, :]
@@ -577,13 +583,13 @@
     five = swap(pay, "seq", 16)
     pay, parts = lax.optimization_barrier((pay, parts))
     parts = inner(6, within, parts)
-    five, parts = lax.optimization_barrier((five, parts))
     y, flipped, coef = parts
+    (y,) = add_levels((2, 3), False, [mine], [other], [two_factor, three_factor], y, flipped, coef)
+    five, y = lax.optimization_barrier((five, y))
     both, lead, five_factor, pay = join(4, shard, span, lead, five, four)
     six = swap(pay, "seq", 48)
     both, y = lax.optimization_barrier((both, y))
     both_got = swap(both, "seq", 2)
-    (y,) = add_levels((2, 3), False, [mine], [other], [two_factor, three_factor], y, flipped, coef)
     both_got, six, y = lax.optimization_barrier((both_got, six, y))
     six_got = swap(six, "seq", 2)
     mine = gather(2, both, [both_got])

time: 58.4 us -> 58.5 us (level)
  no operation moved by 1% of the time
where the time goes in v5:
time: 58.5 us; the launch traced here: 58.1 us
  Pallas kernels  25 us (43%)
  starting transfers between devices  21 us (36%)
  waiting for transfers between devices  11.7 us (20%)
    ppermute x12, starting transfers between devices, swap(): return lax.ppermute(array, axis, route)  16.7 us
    ppermute x12, waiting for transfers between devices, swap(): return lax.ppermute(array, axis, route)  9.4 us
    pallas_call x4, Pallas kernels, inner(): pl.pallas_call(functools.partial(inner_kernel, range(chunk0, chunk0 + PIE...  7.86 us
    pallas_call x3, Pallas kernels, add_levels(): pl.pallas_call(functools.partial(level_kernel, levels, len(mine), final),...  6.5 us
    pallas_call x1, Pallas kernels, block_states(): pl.pallas_call(state_kernel, in_specs=[SMEM] + [ANY] * 5, out_specs=[VMEM...  5.41 us
    ppermute x3, starting transfers between devices, per_device(): lax.ppermute(squares, 'head', [(i, i ^ d) for i in range(4)])  4.31 us
    ppermute x3, waiting for transfers between devices, per_device(): lax.ppermute(squares, 'head', [(i, i ^ d) for i in range(4)])  2.27 us
    pallas_call x1, Pallas kernels, normalize(): pl.pallas_call(norm_kernel, in_specs=[VMEM] * 5, out_specs=ANY, out_shape...  2.23 us
  transfers between devices with their start and end apart: 15, of which 8 were waited for; matrix products, arithmetic and copies ran while one was open for 0% of the time, Pallas kernels for 26%

profile of v5, /device:TPU:16, one launch (start us, length us, event | category | flops | bytes accessed | tf_op | source)
XLA Modules:
  0.0 58.1 jit_solution(1701537098076322956)
XLA Ops:
  0.0 5.4 %block_states.1 = (f32[1024,128]{1,0:T(8,128)S(1)}, bf16[1040,128]{1,0:T(8,128)(2,1)S(1)}, bf16[8,1024,128]{2,1,0:T(8,128)(2,1)S(1)}, f32[16,2048]{1,0:T(8,128)S...) custom-call(s32[4]{0:T(128)} %listed.9, ...), custom_call_target="tpu_custom_call" | custom-call | tf_op jit(solution)/shard_map/block_states/pallas_call | solution.py:166
  5.4 0.1 collective-permute-start
  5.5 1.5 %collective-permute-done.got_ref = bf16[1040,128]{1,0:T(8,128)(2,1)S(1)} collective-permute-done((bf16[1040,128]{1,0:T(8,128)(2,1)S(1)}, bf16[1040,128]{1,0:T(8,128)(2,1)S(1)}, u32[]{:S(2)}, u32[]{:S(2)}) %collective-permute-start) | collective-permute-done | bytes 266272 | tf_op jit(solution)/shard_map/ppermute | solution.py:560
  7.0 0.2 join_cores.1
  7.2 1.4 %collective-permute-start.1 = (bf16[528,128]{1,0:T(8,128)(2,1)S(1)}, bf16[528,128]{1,0:T(8,128)(2,1)S(1)}, u32[]{:S(2)}, u32[]{:S(2)}) collective-permute-start(bf16[528,128]{1,0:T(8,128)(2,1)S(1)} %get-tuple-element.87), channel_id=1, source_target_pairs={{0,8},{4,12},{8,0},{12,4},{16,24},{20,28},{24,16},{28,20},{32,40},... | collective-permute-start | bytes 405512 | tf_op jit(solution)/shard_map/ppermute | solution.py:560
  8.6 1.4 %collective-permute-start.2 = (bf16[528,128]{1,0:T(8,128)(2,1)S(1)}, bf16[528,128]{1,0:T(8,128)(2,1)S(1)}, u32[]{:S(2)}, u32[]{:S(2)}) collective-permute-start(bf16[528,128]{1,0:T(8,128)(2,1)S(1)} %get-tuple-element.87), channel_id=1, source_target_pairs={{0,24},{4,28},{8,16},{12,20},{16,8},{20,12},{24,0},{28,4},{32,56},... | collective-permute-start | bytes 405512 | tf_op jit(solution)/shard_map/ppermute | solution.py:560
  10.0 1.5 %collective-permute-start.3 = (bf16[528,128]{1,0:T(8,128)(2,1)S(1)}, bf16[528,128]{1,0:T(8,128)(2,1)S(1)}, u32[]{:S(2)}, u32[]{:S(2)}) collective-permute-start(bf16[528,128]{1,0:T(8,128)(2,1)S(1)} %get-tuple-element.87), channel_id=1, source_target_pairs={{0,16},{4,20},{8,24},{12,28},{16,0},{20,4},{24,8},{28,12},{32,48},... | collective-permute-start | bytes 405512 | tf_op jit(solution)/shard_map/ppermute | solution.py:560
  11.4 2.0 %inner0.1 = (f32[8,1024,256]{2,1,0:T(8,128)S(1)}, bf16[128,2048]{1,0:T(8,128)(2,1)S(1)}, f32[5,16,2048]{2,1,0:T(8,128)S(1)}) custom-call(s32[4]{0:T(128)} %listed.9, f32[16]{0:T(128)} %skip.7, bf16[8,1024,256]{2,1,0:T(8,128)(2,1)S(1)} %get-tuple-element.73.x_ref, bf16[2048,128]{1,0:T(8,128)(2,1)S(1)} %get-tuple-element.74.b_ref, ...), custom_call_target="tpu_custom_call" | custom-call | flops 805306368 | bytes 4000000 | tf_op jit(solution)/shard_map/inner0/pallas_call | solution.py:426
  13.4 2.0 %inner2.1 = (f32[8,1024,256]{2,1,0:T(8,128)S(1)}, bf16[128,2048]{1,0:T(8,128)(2,1)S(1)}, f32[5,16,2048]{2,1,0:T(8,128)S(1)}) custom-call(s32[4]{0:T(128)} %listed.9, f32[16]{0:T(128)} %skip.7, bf16[8,1024,256]{2,1,0:T(8,128)(2,1)S(1)} %get-tuple-element.73.x_ref, ...), custom_call_target="tpu_custom_call", output_to_operand_aliasing={{0}: (11, {}), {1}: (12, {}), {2}: (13, {})} | custom-call | flops 805306368 | bytes 4000000 | tf_op jit(solution)/shard_map/inner2/pallas_call | solution.py:426
  15.4 0.0 collective-permute-done.1.one_ref
  15.4 1.5 %collective-permute-done.2.three_ref = bf16[528,128]{1,0:T(8,128)(2,1)S(1)} collective-permute-done((bf16[528,128]{1,0:T(8,128)(2,1)S(1)}, bf16[528,128]{1,0:T(8,128)(2,1)S(1)}, u32[]{:S(2)}, u32[]{:S(2)}) %collective-permute-start.2) | collective-permute-done | bytes 135200 | tf_op jit(solution)/shard_map/ppermute | solution.py:560
  16.8 0.0 collective-permute-done.3.two_ref
  16.8 0.3 join_chips.1
  17.1 0.1 collective-permute-start.6
  17.2 2.0 %collective-permute-start.4 = (bf16[272,128]{1,0:T(8,128)(2,1)S(1)}, bf16[272,128]{1,0:T(8,128)(2,1)S(1)}, u32[]{:S(2)}, u32[]{:S(2)}) collective-permute-start(bf16[272,128]{1,0:T(8,128)(2,1)S(1)} %get-tuple-element.100), channel_id=1, source_target_pairs={{0,32},{4,36},{8,40},{12,44},{16,48},{20,52},{24,56},{28,60},{32,0... | collective-permute-start | bytes 208904 | tf_op jit(solution)/shard_map/ppermute | solution.py:560
  19.2 2.0 %inner4.1 = (f32[8,1024,256]{2,1,0:T(8,128)S(1)}, bf16[128,2048]{1,0:T(8,128)(2,1)S(1)}, f32[5,16,2048]{2,1,0:T(8,128)S(1)}) custom-call(s32[4]{0:T(128)} %listed.9, f32[16]{0:T(128)} %skip.7, bf16[8,1024,256]{2,1,0:T(8,128)(2,1)S(1)} %get-tuple-element.73.x_ref, ...), custom_call_target="tpu_custom_call", output_to_operand_aliasing={{0}: (11, {}), {1}: (12, {}), {2}: (13, {})} | custom-call | flops 805306368 | bytes 4000000 | tf_op jit(solution)/shard_map/inner4/pallas_call | solution.py:426
  21.2 0.8 %collective-permute-done.4.got_ref.rest_0_ = bf16[272,128]{1,0:T(8,128)(2,1)S(1)} collective-permute-done((bf16[272,128]{1,0:T(8,128)(2,1)S(1)}, bf16[272,128]{1,0:T(8,128)(2,1)S(1)}, u32[]{:S(2)}, u32[]{:S(2)}) %collective-permute-start.4) | collective-permute-done | bytes 69664 | tf_op jit(solution)/shard_map/ppermute | solution.py:560
  22.0 0.2 join3.1
  22.1 3.5 %collective-permute-start.5 = (bf16[272,128]{1,0:T(8,128)(2,1)S(1)}, bf16[272,128]{1,0:T(8,128)(2,1)S(1)}, u32[]{:S(2)}, u32[]{:S(2)}) collective-permute-start(bf16[272,128]{1,0:T(8,128)(2,1)S(1)} %get-tuple-element.108), channel_id=1, source_target_pairs={{0,64},{4,68},{8,72},{12,76},{16,80},{20,84},{24,88},{28,92},{32,9... | collective-permute-start | bytes 208904 | tf_op jit(solution)/shard_map/ppermute | solution.py:560
  25.7 2.0 %inner6.1 = (f32[8,1024,256]{2,1,0:T(8,128)S(1)}, bf16[128,2048]{1,0:T(8,128)(2,1)S(1)}, f32[5,16,2048]{2,1,0:T(8,128)S(1)}) custom-call(s32[4]{0:T(128)} %listed.9, f32[16]{0:T(128)} %skip.7, bf16[8,1024,256]{2,1,0:T(8,128)(2,1)S(1)} %get-tuple-element.73.x_ref, ...), custom_call_target="tpu_custom_call", output_to_operand_aliasing={{0}: (11, {}), {1}: (12, {}), {2}: (13, {})} | custom-call | flops 805306368 | bytes 4000000 | tf_op jit(solution)/shard_map/inner6/pallas_call | solution.py:426
  27.7 0.0 collective-permute-done.6.rest_1_
  27.7 2.4 %levels2.1.rest_4_ = f32[8,1024,256]{2,1,0:T(8,128)S(1)} custom-call(bf16[128,2048]{1,0:T(8,128)(2,1)S(1)} %get-tuple-element.115.flipped_ref, f32[5,16,2048]{2,1,0:T(8,128)S(1)} %get-tuple-element.116.coef_ref, bf16[1024,128]{1,0:T(8,128)(2,1)S(1)} %get-tuple-element.121.rest_0_, ...), custom_call_target="tpu_custom_call", output_to_operand_aliasing={{}: (6, {})} | custom-call | flops 2147483648 | bytes 4000000 | tf_op jit(solution)/shard_map/levels2/pallas_call | solution.py:482
  30.1 0.0 collective-permute-done.5.got_ref
  30.1 0.2 join4.1
  30.3 2.0 %collective-permute-start.7 = (bf16[512,128]{1,0:T(8,128)(2,1)S(1)}, bf16[512,128]{1,0:T(8,128)(2,1)S(1)}, u32[]{:S(2)}, u32[]{:S(2)}) collective-permute-start(bf16[512,128]{1,0:T(8,128)(2,1)S(1)} %get-tuple-element.128.refs_0_), channel_id=1, source_target_pairs={{0,8},{4,12},{8,0},{12,4},{16,24},{20,28},{24,16},{28,20},{32,40},... | collective-permute-start | bytes 393224 | tf_op jit(solution)/shard_map/ppermute | solution.py:560
  32.3 4.3 %collective-permute-start.8 = (bf16[272,128]{1,0:T(8,128)(2,1)S(1)}, bf16[272,128]{1,0:T(8,128)(2,1)S(1)}, u32[]{:S(2)}, u32[]{:S(2)}) collective-permute-start(bf16[272,128]{1,0:T(8,128)(2,1)S(1)} %get-tuple-element.129), channel_id=1, source_target_pairs={{0,192},{4,196},{8,200},{12,204},{16,208},{20,212},{24,216},{28,22... | collective-permute-start | bytes 208904 | tf_op jit(solution)/shard_map/ppermute | solution.py:560
  36.6 2.3 %collective-permute-done.8.refs_0_ = bf16[272,128]{1,0:T(8,128)(2,1)S(1)} collective-permute-done((bf16[272,128]{1,0:T(8,128)(2,1)S(1)}, bf16[272,128]{1,0:T(8,128)(2,1)S(1)}, u32[]{:S(2)}, u32[]{:S(2)}) %collective-permute-start.8) | collective-permute-done | bytes 69664 | tf_op jit(solution)/shard_map/ppermute | solution.py:560
  38.9 0.0 collective-permute-done.7.refs_1_
  39.0 0.1 collective-permute-start.10
  39.1 0.2 collective-permute-start.9
  39.3 1.3 %collective-permute-done.10.rest_1_ = bf16[1024,128]{1,0:T(8,128)(2,1)S(1)} collective-permute-done((bf16[1024,128]{1,0:T(8,128)(2,1)S(1)}, bf16[1024,128]{1,0:T(8,128)(2,1)S(1)}, u32[]{:S(2)}, u32[]{:S(2)}) %collective-permute-start.10) | collective-permute-done | bytes 262176 | tf_op jit(solution)/shard_map/ppermute | solution.py:560
  40.6 2.4 %levels4.1.rest_3_ = f32[8,1024,256]{2,1,0:T(8,128)S(1)} custom-call(bf16[128,2048]{1,0:T(8,128)(2,1)S(1)} %get-tuple-element.115.flipped_ref, f32[5,16,2048]{2,1,0:T(8,128)S(1)} %get-tuple-element.116.coef_ref, bf16[1024,128]{1,0:T(8,128)(2,1)S(1)} %gather2.1.rest_0_, ...), custom_call_target="tpu_custom_call", output_to_operand_aliasing={{}: (6, {})} | custom-call | flops 2147483648 | bytes 4000000 | tf_op jit(solution)/shard_map/levels4/pallas_call | solution.py:482
  43.0 0.0 copy-start
  43.0 0.7 %collective-permute-done.9.refs_1_ = bf16[272,128]{1,0:T(8,128)(2,1)S(1)} collective-permute-done((bf16[272,128]{1,0:T(8,128)(2,1)S(1)}, bf16[272,128]{1,0:T(8,128)(2,1)S(1)}, u32[]{:S(2)}, u32[]{:S(2)}) %collective-permute-start.9) | collective-permute-done | bytes 69664 | tf_op jit(solution)/shard_map/ppermute | solution.py:560
  43.7 0.1 collective-permute-start.11
  43.8 1.3 %collective-permute-done.11.rest_1_ = bf16[512,128]{1,0:T(8,128)(2,1)S(1)} collective-permute-done((bf16[512,128]{1,0:T(8,128)(2,1)S(1)}, bf16[512,128]{1,0:T(8,128)(2,1)S(1)}, u32[]{:S(2)}, u32[]{:S(2)}) %collective-permute-start.11) | collective-permute-done | bytes 131104 | tf_op jit(solution)/shard_map/ppermute | solution.py:560
  45.1 1.7 %levels6.1 = (f32[8,1024,256]{2,1,0:T(8,128)S(1)}, f32[8,1,256]{2,1,0:T(1,128)S(1)}) custom-call(bf16[128,2048]{1,0:T(8,128)(2,1)S(1)} %get-tuple-element.115.flipped_ref, f32[5,16,2048]{2,1,0:T(8,128)S(1)} %get-tuple-element.116.coef_ref, bf16[512,128]{1,0:T(8,128)(2,1)S(1)} %gather1.1.rest_0_, ...), custom_call_target="tpu_custom_call", output_to_operand_aliasing={{0}: (5, {})} | custom-call | flops 1073741824 | bytes 4000000 | tf_op jit(solution)/shard_map/levels6/pallas_call | solution.py:482
  46.8 1.6 %collective-permute-start.12 = (f32[8,1,256]{2,1,0:T(1,128)S(1)}, f32[8,1,256]{2,1,0:T(1,128)S(1)}, u32[]{:S(2)}, u32[]{:S(2)}) collective-permute-start(f32[8,1,256]{2,1,0:T(1,128)S(1)} %get-tuple-element.140.s0), channel_id=1, source_target_pairs={{0,1},{1,0},{2,3},{3,2},{4,5},{5,4},{6,7},{7,6},{8,9},{9,8},{10,11... | collective-permute-start | bytes 24584 | tf_op jit(solution)/shard_map/ppermute | solution.py:603
  48.4 2.1 %collective-permute-start.13 = (f32[8,1,256]{2,1,0:T(1,128)S(1)}, f32[8,1,256]{2,1,0:T(1,128)S(1)}, u32[]{:S(2)}, u32[]{:S(2)}) collective-permute-start(f32[8,1,256]{2,1,0:T(1,128)S(1)} %get-tuple-element.140.s0), channel_id=1, source_target_pairs={{0,3},{1,2},{2,1},{3,0},{4,7},{5,6},{6,5},{7,4},{8,11},{9,10},{10,... | collective-permute-start | bytes 24584 | tf_op jit(solution)/shard_map/ppermute | solution.py:603
  50.5 0.6 %collective-permute-start.14 = (f32[8,1,256]{2,1,0:T(1,128)S(1)}, f32[8,1,256]{2,1,0:T(1,128)S(1)}, u32[]{:S(2)}, u32[]{:S(2)}) collective-permute-start(f32[8,1,256]{2,1,0:T(1,128)S(1)} %get-tuple-element.140.s0), channel_id=1, source_target_pairs={{0,2},{1,3},{2,0},{3,1},{4,6},{5,7},{6,4},{7,5},{8,10},{9,11},{10,... | collective-permute-start | bytes 24584 | tf_op jit(solution)/shard_map/ppermute | solution.py:603
  51.1 0.0 copy-done
  51.1 2.2 %flip.1.y_ref = f32[2048,1024]{1,0:T(8,128)S(1)} custom-call(f32[8,1024,256]{2,1,0:T(8,128)S(1)} %get-tuple-element.139.y_ref, f32[1,1024]{1,0:T(1,128)S(1)} %bitcast.1), custom_call_target="tpu_custom_call" | custom-call | bytes 16000000 | tf_op jit(solution)/shard_map/flip/pallas_call | solution.py:509
  53.4 0.0 collective-permute-done.12.s1
  53.4 0.0 collective-permute-done.13.s2
  53.4 2.3 %collective-permute-done.14.s3 = f32[8,1,256]{2,1,0:T(1,128)S(1)} collective-permute-done((f32[8,1,256]{2,1,0:T(1,128)S(1)}, f32[8,1,256]{2,1,0:T(1,128)S(1)}, u32[]{:S(2)}, u32[]{:S(2)}) %collective-permute-start.14) | collective-permute-done | bytes 8224 | tf_op jit(solution)/shard_map/ppermute | solution.py:603
  55.6 2.2 %normalize.1 = bf16[2048,1024]{1,0:T(8,128)(2,1)} custom-call(f32[2048,1024]{1,0:T(8,128)S(1)} %flip.1.y_ref, f32[8,1,256]{2,1,0:T(1,128)S(1)} %get-tuple-element.140.s0, f32[8,1,256]{2,1,0:T(1,128)S(1)} %collective-permute-done.12.s1, f32[8,1,256]{2,1,0:T(1,128)S(1)} %collective-permute-done.13.s2, f32[8,1,256]{2,1,0:T(1,128)S(1)} %collective-permute-done.14.s3), custom_call_target="tpu_custom_call" | custom-call | tf_op jit(solution)/shard_map/normalize/pallas_call | solution.py:539
  (2 shorter events, 0.0 us)
Async XLA Ops:
  5.4 1.6 %collective-permute-start = (bf16[1040,128]{1,0:T(8,128)(2,1)S(1)}, bf16[1040,128]{1,0:T(8,128)(2,1)S(1)}, u32[]{:S(2)}, u32[]{:S(2)}) collective-permute-start(bf16[1040,128]{1,0:T(8,128)(2,1)S(1)} %get-tuple-element.80), channel_id=1, source_target_pairs={{0,4},{4,0},{8,12},{12,8},{16,20},{20,16},{24,28},{28,24},{32,36},... | collective-permute-start | bytes 798728 | tf_op jit(solution)/shard_map/ppermute | solution.py:560
  7.2 8.1 %collective-permute-start.1 = (bf16[528,128]{1,0:T(8,128)(2,1)S(1)}, bf16[528,128]{1,0:T(8,128)(2,1)S(1)}, u32[]{:S(2)}, u32[]{:S(2)}) collective-permute-start(bf16[528,128]{1,0:T(8,128)(2,1)S(1)} %get-tuple-element.87), channel_id=1, source_target_pairs={{0,8},{4,12},{8,0},{12,4},{16,24},{20,28},{24,16},{28,20},{32,40},... | collective-permute-start | bytes 405512 | tf_op jit(solution)/shard_map/ppermute | solution.py:560
  8.6 8.2 %collective-permute-start.2 = (bf16[528,128]{1,0:T(8,128)(2,1)S(1)}, bf16[528,128]{1,0:T(8,128)(2,1)S(1)}, u32[]{:S(2)}, u32[]{:S(2)}) collective-permute-start(bf16[528,128]{1,0:T(8,128)(2,1)S(1)} %get-tuple-element.87), channel_id=1, source_target_pairs={{0,24},{4,28},{8,16},{12,20},{16,8},{20,12},{24,0},{28,4},{32,56},... | collective-permute-start | bytes 405512 | tf_op jit(solution)/shard_map/ppermute | solution.py:560
  10.0 6.9 %collective-permute-start.3 = (bf16[528,128]{1,0:T(8,128)(2,1)S(1)}, bf16[528,128]{1,0:T(8,128)(2,1)S(1)}, u32[]{:S(2)}, u32[]{:S(2)}) collective-permute-start(bf16[528,128]{1,0:T(8,128)(2,1)S(1)} %get-tuple-element.87), channel_id=1, source_target_pairs={{0,16},{4,20},{8,24},{12,28},{16,0},{20,4},{24,8},{28,12},{32,48},... | collective-permute-start | bytes 405512 | tf_op jit(solution)/shard_map/ppermute | solution.py:560
  17.1 10.5 %collective-permute-start.6 = (bf16[1024,128]{1,0:T(8,128)(2,1)S(1)}, bf16[1024,128]{1,0:T(8,128)(2,1)S(1)}, u32[]{:S(2)}, u32[]{:S(2)}) collective-permute-start(bf16[1024,128]{1,0:T(8,128)(2,1)S(1)} %get-tuple-element.121.rest_0_), channel_id=1, source_target_pairs={{0,4},{4,0},{8,12},{12,8},{16,20},{20,16},{24,28},{28,24},{32,36},... | collective-permute-start | bytes 786440 | tf_op jit(solution)/shard_map/ppermute | solution.py:560
  17.2 4.8 %collective-permute-start.4 = (bf16[272,128]{1,0:T(8,128)(2,1)S(1)}, bf16[272,128]{1,0:T(8,128)(2,1)S(1)}, u32[]{:S(2)}, u32[]{:S(2)}) collective-permute-start(bf16[272,128]{1,0:T(8,128)(2,1)S(1)} %get-tuple-element.100), channel_id=1, source_target_pairs={{0,32},{4,36},{8,40},{12,44},{16,48},{20,52},{24,56},{28,60},{32,0... | collective-permute-start | bytes 208904 | tf_op jit(solution)/shard_map/ppermute | solution.py:560
  22.1 7.9 %collective-permute-start.5 = (bf16[272,128]{1,0:T(8,128)(2,1)S(1)}, bf16[272,128]{1,0:T(8,128)(2,1)S(1)}, u32[]{:S(2)}, u32[]{:S(2)}) collective-permute-start(bf16[272,128]{1,0:T(8,128)(2,1)S(1)} %get-tuple-element.108), channel_id=1, source_target_pairs={{0,64},{4,68},{8,72},{12,76},{16,80},{20,84},{24,88},{28,92},{32,9... | collective-permute-start | bytes 208904 | tf_op jit(solution)/shard_map/ppermute | solution.py:560
  30.3 8.7 %collective-permute-start.7 = (bf16[512,128]{1,0:T(8,128)(2,1)S(1)}, bf16[512,128]{1,0:T(8,128)(2,1)S(1)}, u32[]{:S(2)}, u32[]{:S(2)}) collective-permute-start(bf16[512,128]{1,0:T(8,128)(2,1)S(1)} %get-tuple-element.128.refs_0_), channel_id=1, source_target_pairs={{0,8},{4,12},{8,0},{12,4},{16,24},{20,28},{24,16},{28,20},{32,40},... | collective-permute-start | bytes 393224 | tf_op jit(solution)/shard_map/ppermute | solution.py:560
  32.3 6.6 %collective-permute-start.8 = (bf16[272,128]{1,0:T(8,128)(2,1)S(1)}, bf16[272,128]{1,0:T(8,128)(2,1)S(1)}, u32[]{:S(2)}, u32[]{:S(2)}) collective-permute-start(bf16[272,128]{1,0:T(8,128)(2,1)S(1)} %get-tuple-element.129), channel_id=1, source_target_pairs={{0,192},{4,196},{8,200},{12,204},{16,208},{20,212},{24,216},{28,22... | collective-permute-start | bytes 208904 | tf_op jit(solution)/shard_map/ppermute | solution.py:560
  39.0 1.6 %collective-permute-start.10 = (bf16[1024,128]{1,0:T(8,128)(2,1)S(1)}, bf16[1024,128]{1,0:T(8,128)(2,1)S(1)}, u32[]{:S(2)}, u32[]{:S(2)}) collective-permute-start(bf16[1024,128]{1,0:T(8,128)(2,1)S(1)} %gather2.1.rest_0_), channel_id=1, source_target_pairs={{0,4},{4,0},{8,12},{12,8},{16,20},{20,16},{24,28},{28,24},{32,36},... | collective-permute-start | bytes 786440 | tf_op jit(solution)/shard_map/ppermute | solution.py:560
  39.1 4.6 %collective-permute-start.9 = (bf16[272,128]{1,0:T(8,128)(2,1)S(1)}, bf16[272,128]{1,0:T(8,128)(2,1)S(1)}, u32[]{:S(2)}, u32[]{:S(2)}) collective-permute-start(bf16[272,128]{1,0:T(8,128)(2,1)S(1)} %collective-permute-done.8.refs_0_), channel_id=1, source_target_pairs={{0,8},{4,12},{8,0},{12,4},{16,24},{20,28},{24,16},{28,20},{32,40},... | collective-permute-start | bytes 208904 | tf_op jit(solution)/shard_map/ppermute | solution.py:560
  43.0 8.1 %copy-start = (f32[1024]{0:T(1024)S(1)}, f32[1024]{0:T(1024)}, u32[]{:S(2)}) copy-start(f32[1024]{0:T(1024)} %param.14) | copy-start | bytes 12292
  43.7 1.4 %collective-permute-start.11 = (bf16[512,128]{1,0:T(8,128)(2,1)S(1)}, bf16[512,128]{1,0:T(8,128)(2,1)S(1)}, u32[]{:S(2)}, u32[]{:S(2)}) collective-permute-start(bf16[512,128]{1,0:T(8,128)(2,1)S(1)} %gather1.1.rest_0_), channel_id=1, source_target_pairs={{0,4},{4,0},{8,12},{12,8},{16,20},{20,16},{24,28},{28,24},{32,36},... | collective-permute-start | bytes 393224 | tf_op jit(solution)/shard_map/ppermute | solution.py:560
  46.8 6.5 %collective-permute-start.12 = (f32[8,1,256]{2,1,0:T(1,128)S(1)}, f32[8,1,256]{2,1,0:T(1,128)S(1)}, u32[]{:S(2)}, u32[]{:S(2)}) collective-permute-start(f32[8,1,256]{2,1,0:T(1,128)S(1)} %get-tuple-element.140.s0), channel_id=1, source_target_pairs={{0,1},{1,0},{2,3},{3,2},{4,5},{5,4},{6,7},{7,6},{8,9},{9,8},{10,11... | collective-permute-start | bytes 24584 | tf_op jit(solution)/shard_map/ppermute | solution.py:603
  48.4 5.0 %collective-permute-start.13 = (f32[8,1,256]{2,1,0:T(1,128)S(1)}, f32[8,1,256]{2,1,0:T(1,128)S(1)}, u32[]{:S(2)}, u32[]{:S(2)}) collective-permute-start(f32[8,1,256]{2,1,0:T(1,128)S(1)} %get-tuple-element.140.s0), channel_id=1, source_target_pairs={{0,3},{1,2},{2,1},{3,0},{4,7},{5,6},{6,5},{7,4},{8,11},{9,10},{10,... | collective-permute-start | bytes 24584 | tf_op jit(solution)/shard_map/ppermute | solution.py:603
  50.5 5.2 %collective-permute-start.14 = (f32[8,1,256]{2,1,0:T(1,128)S(1)}, f32[8,1,256]{2,1,0:T(1,128)S(1)}, u32[]{:S(2)}, u32[]{:S(2)}) collective-permute-start(f32[8,1,256]{2,1,0:T(1,128)S(1)} %get-tuple-element.140.s0), channel_id=1, source_target_pairs={{0,2},{1,3},{2,0},{3,1},{4,6},{5,7},{6,4},{7,5},{8,10},{9,11},{10,... | collective-permute-start | bytes 24584 | tf_op jit(solution)/shard_map/ppermute | solution.py:603

commit v6 on v5

--- a/solution.py
+++ b/solution.py
@@ -583,13 +583,13 @@
     five = swap(pay, "seq", 16)
     pay, parts = lax.optimization_barrier((pay, parts))
     parts = inner(6, within, parts)
+    five, parts = lax.optimization_barrier((five, parts))
     y, flipped, coef = parts
-    (y,) = add_levels((2, 3), False, [mine], [other], [two_factor, three_factor], y, flipped, coef)
-    five, y = lax.optimization_barrier((five, y))
     both, lead, five_factor, pay = join(4, shard, span, lead, five, four)
     six = swap(pay, "seq", 48)
     both, y = lax.optimization_barrier((both, y))
     both_got = swap(both, "seq", 2)
+    (y,) = add_levels((2, 3), False, [mine], [other], [two_factor, three_factor], y, flipped, coef)
     both_got, six, y = lax.optimization_barrier((both_got, six, y))
     six_got = swap(six, "seq", 2)
     mine = gather(2, both, [both_got])

time: 58.5 us -> 58 us (level)
  no operation moved by 1% of the time
where the time goes in v6:
time: 58 us; the launch traced here: 57.7 us
  Pallas kernels  25 us (43%)
  starting transfers between devices  21 us (36%)
  waiting for transfers between devices  11.2 us (19%)
    ppermute x12, starting transfers between devices, swap(): return lax.ppermute(array, axis, route)  16.7 us
    ppermute x12, waiting for transfers between devices, swap(): return lax.ppermute(array, axis, route)  8.93 us
    pallas_call x4, Pallas kernels, inner(): pl.pallas_call(functools.partial(inner_kernel, range(chunk0, chunk0 + PIE...  7.86 us
    pallas_call x3, Pallas kernels, add_levels(): pl.pallas_call(functools.partial(level_kernel, levels, len(mine), final),...  6.5 us
    pallas_call x1, Pallas kernels, block_states(): pl.pallas_call(state_kernel, in_specs=[SMEM] + [ANY] * 5, out_specs=[VMEM...  5.41 us
    ppermute x3, starting transfers between devices, per_device(): lax.ppermute(squares, 'head', [(i, i ^ d) for i in range(4)])  4.32 us
    ppermute x3, waiting for transfers between devices, per_device(): lax.ppermute(squares, 'head', [(i, i ^ d) for i in range(4)])  2.27 us
    pallas_call x1, Pallas kernels, normalize(): pl.pallas_call(norm_kernel, in_specs=[VMEM] * 5, out_specs=ANY, out_shape...  2.23 us
  transfers between devices with their start and end apart: 15, of which 8 were waited for; matrix products, arithmetic and copies ran while one was open for 0% of the time, Pallas kernels for 26%

profile of v6, /device:TPU:16, one launch (start us, length us, event | category | flops | bytes accessed | tf_op | source)
XLA Modules:
  0.0 57.7 jit_solution(4741157170089883471)
XLA Ops:
  0.0 5.4 %block_states.1 = (f32[1024,128]{1,0:T(8,128)S(1)}, bf16[1040,128]{1,0:T(8,128)(2,1)S(1)}, bf16[8,1024,128]{2,1,0:T(8,128)(2,1)S(1)}, f32[16,2048]{1,0:T(8,128)S...) custom-call(s32[4]{0:T(128)} %listed.9, ...), custom_call_target="tpu_custom_call" | custom-call | tf_op jit(solution)/shard_map/block_states/pallas_call | solution.py:166
  5.4 0.1 collective-permute-start
  5.5 1.5 %collective-permute-done.got_ref = bf16[1040,128]{1,0:T(8,128)(2,1)S(1)} collective-permute-done((bf16[1040,128]{1,0:T(8,128)(2,1)S(1)}, bf16[1040,128]{1,0:T(8,128)(2,1)S(1)}, u32[]{:S(2)}, u32[]{:S(2)}) %collective-permute-start) | collective-permute-done | bytes 266272 | tf_op jit(solution)/shard_map/ppermute | solution.py:560
  7.0 0.2 join_cores.1
  7.2 1.4 %collective-permute-start.1 = (bf16[528,128]{1,0:T(8,128)(2,1)S(1)}, bf16[528,128]{1,0:T(8,128)(2,1)S(1)}, u32[]{:S(2)}, u32[]{:S(2)}) collective-permute-start(bf16[528,128]{1,0:T(8,128)(2,1)S(1)} %get-tuple-element.81), channel_id=1, source_target_pairs={{0,8},{4,12},{8,0},{12,4},{16,24},{20,28},{24,16},{28,20},{32,40},... | collective-permute-start | bytes 405512 | tf_op jit(solution)/shard_map/ppermute | solution.py:560
  8.6 1.4 %collective-permute-start.2 = (bf16[528,128]{1,0:T(8,128)(2,1)S(1)}, bf16[528,128]{1,0:T(8,128)(2,1)S(1)}, u32[]{:S(2)}, u32[]{:S(2)}) collective-permute-start(bf16[528,128]{1,0:T(8,128)(2,1)S(1)} %get-tuple-element.81), channel_id=1, source_target_pairs={{0,24},{4,28},{8,16},{12,20},{16,8},{20,12},{24,0},{28,4},{32,56},... | collective-permute-start | bytes 405512 | tf_op jit(solution)/shard_map/ppermute | solution.py:560
  10.0 1.5 %collective-permute-start.3 = (bf16[528,128]{1,0:T(8,128)(2,1)S(1)}, bf16[528,128]{1,0:T(8,128)(2,1)S(1)}, u32[]{:S(2)}, u32[]{:S(2)}) collective-permute-start(bf16[528,128]{1,0:T(8,128)(2,1)S(1)} %get-tuple-element.81), channel_id=1, source_target_pairs={{0,16},{4,20},{8,24},{12,28},{16,0},{20,4},{24,8},{28,12},{32,48},... | collective-permute-start | bytes 405512 | tf_op jit(solution)/shard_map/ppermute | solution.py:560
  11.4 2.0 %inner0.1 = (f32[8,1024,256]{2,1,0:T(8,128)S(1)}, bf16[128,2048]{1,0:T(8,128)(2,1)S(1)}, f32[5,16,2048]{2,1,0:T(8,128)S(1)}) custom-call(s32[4]{0:T(128)} %listed.9, f32[16]{0:T(128)} %skip.7, bf16[8,1024,256]{2,1,0:T(8,128)(2,1)S(1)} %get-tuple-element.82.x_ref, bf16[2048,128]{1,0:T(8,128)(2,1)S(1)} %get-tuple-element.83.b_ref, ...), custom_call_target="tpu_custom_call" | custom-call | flops 805306368 | bytes 4000000 | tf_op jit(solution)/shard_map/inner0/pallas_call | solution.py:426
  13.4 2.0 %inner2.1 = (f32[8,1024,256]{2,1,0:T(8,128)S(1)}, bf16[128,2048]{1,0:T(8,128)(2,1)S(1)}, f32[5,16,2048]{2,1,0:T(8,128)S(1)}) custom-call(s32[4]{0:T(128)} %listed.9, f32[16]{0:T(128)} %skip.7, bf16[8,1024,256]{2,1,0:T(8,128)(2,1)S(1)} %get-tuple-element.82.x_ref, ...), custom_call_target="tpu_custom_call", output_to_operand_aliasing={{0}: (11, {}), {1}: (12, {}), {2}: (13, {})} | custom-call | flops 805306368 | bytes 4000000 | tf_op jit(solution)/shard_map/inner2/pallas_call | solution.py:426
  15.4 0.0 collective-permute-done.1.one_ref
  15.4 1.5 %collective-permute-done.2.three_ref = bf16[528,128]{1,0:T(8,128)(2,1)S(1)} collective-permute-done((bf16[528,128]{1,0:T(8,128)(2,1)S(1)}, bf16[528,128]{1,0:T(8,128)(2,1)S(1)}, u32[]{:S(2)}, u32[]{:S(2)}) %collective-permute-start.2) | collective-permute-done | bytes 135200 | tf_op jit(solution)/shard_map/ppermute | solution.py:560
  16.8 0.0 collective-permute-done.3.two_ref
  16.8 0.3 join_chips.1
  17.1 0.1 collective-permute-start.8
  17.2 2.0 %collective-permute-start.4 = (bf16[272,128]{1,0:T(8,128)(2,1)S(1)}, bf16[272,128]{1,0:T(8,128)(2,1)S(1)}, u32[]{:S(2)}, u32[]{:S(2)}) collective-permute-start(bf16[272,128]{1,0:T(8,128)(2,1)S(1)} %get-tuple-element.102), channel_id=1, source_target_pairs={{0,32},{4,36},{8,40},{12,44},{16,48},{20,52},{24,56},{28,60},{32,0... | collective-permute-start | bytes 208904 | tf_op jit(solution)/shard_map/ppermute | solution.py:560
  19.2 2.0 %inner4.1 = (f32[8,1024,256]{2,1,0:T(8,128)S(1)}, bf16[128,2048]{1,0:T(8,128)(2,1)S(1)}, f32[5,16,2048]{2,1,0:T(8,128)S(1)}) custom-call(s32[4]{0:T(128)} %listed.9, f32[16]{0:T(128)} %skip.7, bf16[8,1024,256]{2,1,0:T(8,128)(2,1)S(1)} %get-tuple-element.82.x_ref, ...), custom_call_target="tpu_custom_call", output_to_operand_aliasing={{0}: (11, {}), {1}: (12, {}), {2}: (13, {})} | custom-call | flops 805306368 | bytes 4000000 | tf_op jit(solution)/shard_map/inner4/pallas_call | solution.py:426
  21.2 0.8 %collective-permute-done.4.got_ref.rest_0_ = bf16[272,128]{1,0:T(8,128)(2,1)S(1)} collective-permute-done((bf16[272,128]{1,0:T(8,128)(2,1)S(1)}, bf16[272,128]{1,0:T(8,128)(2,1)S(1)}, u32[]{:S(2)}, u32[]{:S(2)}) %collective-permute-start.4) | collective-permute-done | bytes 69664 | tf_op jit(solution)/shard_map/ppermute | solution.py:560
  22.0 0.2 join3.1
  22.1 3.5 %collective-permute-start.5 = (bf16[272,128]{1,0:T(8,128)(2,1)S(1)}, bf16[272,128]{1,0:T(8,128)(2,1)S(1)}, u32[]{:S(2)}, u32[]{:S(2)}) collective-permute-start(bf16[272,128]{1,0:T(8,128)(2,1)S(1)} %get-tuple-element.110), channel_id=1, source_target_pairs={{0,64},{4,68},{8,72},{12,76},{16,80},{20,84},{24,88},{28,92},{32,9... | collective-permute-start | bytes 208904 | tf_op jit(solution)/shard_map/ppermute | solution.py:560
  25.7 2.0 %inner6.1 = (f32[8,1024,256]{2,1,0:T(8,128)S(1)}, bf16[128,2048]{1,0:T(8,128)(2,1)S(1)}, f32[5,16,2048]{2,1,0:T(8,128)S(1)}) custom-call(s32[4]{0:T(128)} %listed.9, f32[16]{0:T(128)} %skip.7, bf16[8,1024,256]{2,1,0:T(8,128)(2,1)S(1)} %get-tuple-element.82.x_ref, ...), custom_call_target="tpu_custom_call", output_to_operand_aliasing={{0}: (11, {}), {1}: (12, {}), {2}: (13, {})} | custom-call | flops 805306368 | bytes 4000000 | tf_op jit(solution)/shard_map/inner6/pallas_call | solution.py:426
  27.7 1.8 %collective-permute-done.5.got_ref = bf16[272,128]{1,0:T(8,128)(2,1)S(1)} collective-permute-done((bf16[272,128]{1,0:T(8,128)(2,1)S(1)}, bf16[272,128]{1,0:T(8,128)(2,1)S(1)}, u32[]{:S(2)}, u32[]{:S(2)}) %collective-permute-start.5) | collective-permute-done | bytes 69664 | tf_op jit(solution)/shard_map/ppermute | solution.py:560
  29.5 0.2 join4.1
  29.6 2.0 %collective-permute-start.6 = (bf16[512,128]{1,0:T(8,128)(2,1)S(1)}, bf16[512,128]{1,0:T(8,128)(2,1)S(1)}, u32[]{:S(2)}, u32[]{:S(2)}) collective-permute-start(bf16[512,128]{1,0:T(8,128)(2,1)S(1)} %get-tuple-element.128.refs_0_), channel_id=1, source_target_pairs={{0,8},{4,12},{8,0},{12,4},{16,24},{20,28},{24,16},{28,20},{32,40},... | collective-permute-start | bytes 393224 | tf_op jit(solution)/shard_map/ppermute | solution.py:560
  31.7 4.4 %collective-permute-start.7 = (bf16[272,128]{1,0:T(8,128)(2,1)S(1)}, bf16[272,128]{1,0:T(8,128)(2,1)S(1)}, u32[]{:S(2)}, u32[]{:S(2)}) collective-permute-start(bf16[272,128]{1,0:T(8,128)(2,1)S(1)} %get-tuple-element.129), channel_id=1, source_target_pairs={{0,192},{4,196},{8,200},{12,204},{16,208},{20,212},{24,216},{28,22... | collective-permute-start | bytes 208904 | tf_op jit(solution)/shard_map/ppermute | solution.py:560
  36.1 0.0 collective-permute-done.8.rest_1_
  36.1 2.4 %levels2.1.rest_4_ = f32[8,1024,256]{2,1,0:T(8,128)S(1)} custom-call(bf16[128,2048]{1,0:T(8,128)(2,1)S(1)} %get-tuple-element.120.flipped_ref, f32[5,16,2048]{2,1,0:T(8,128)S(1)} %get-tuple-element.121.coef_ref, bf16[1024,128]{1,0:T(8,128)(2,1)S(1)} %get-tuple-element.131.rest_0_, ...), custom_call_target="tpu_custom_call", output_to_operand_aliasing={{}: (6, {})} | custom-call | flops 2147483648 | bytes 4000000 | tf_op jit(solution)/shard_map/levels2/pallas_call | solution.py:482
  38.5 0.0 collective-permute-done.7.refs_0_
  38.5 0.0 collective-permute-done.6.refs_1_
  38.6 0.1 collective-permute-start.10
  38.7 0.2 collective-permute-start.9
  38.8 1.3 %collective-permute-done.10.rest_1_ = bf16[1024,128]{1,0:T(8,128)(2,1)S(1)} collective-permute-done((bf16[1024,128]{1,0:T(8,128)(2,1)S(1)}, bf16[1024,128]{1,0:T(8,128)(2,1)S(1)}, u32[]{:S(2)}, u32[]{:S(2)}) %collective-permute-start.10) | collective-permute-done | bytes 262176 | tf_op jit(solution)/shard_map/ppermute | solution.py:560
  40.2 2.4 %levels4.1.rest_3_ = f32[8,1024,256]{2,1,0:T(8,128)S(1)} custom-call(bf16[128,2048]{1,0:T(8,128)(2,1)S(1)} %get-tuple-element.120.flipped_ref, f32[5,16,2048]{2,1,0:T(8,128)S(1)} %get-tuple-element.121.coef_ref, bf16[1024,128]{1,0:T(8,128)(2,1)S(1)} %gather2.1.rest_0_, ...), custom_call_target="tpu_custom_call", output_to_operand_aliasing={{}: (6, {})} | custom-call | flops 2147483648 | bytes 4000000 | tf_op jit(solution)/shard_map/levels4/pallas_call | solution.py:482
  42.6 0.0 copy-start
  42.6 0.7 %collective-permute-done.9.refs_1_ = bf16[272,128]{1,0:T(8,128)(2,1)S(1)} collective-permute-done((bf16[272,128]{1,0:T(8,128)(2,1)S(1)}, bf16[272,128]{1,0:T(8,128)(2,1)S(1)}, u32[]{:S(2)}, u32[]{:S(2)}) %collective-permute-start.9) | collective-permute-done | bytes 69664 | tf_op jit(solution)/shard_map/ppermute | solution.py:560
  43.3 0.1 collective-permute-start.11
  43.4 1.3 %collective-permute-done.11.rest_1_ = bf16[512,128]{1,0:T(8,128)(2,1)S(1)} collective-permute-done((bf16[512,128]{1,0:T(8,128)(2,1)S(1)}, bf16[512,128]{1,0:T(8,128)(2,1)S(1)}, u32[]{:S(2)}, u32[]{:S(2)}) %collective-permute-start.11) | collective-permute-done | bytes 131104 | tf_op jit(solution)/shard_map/ppermute | solution.py:560
  44.7 1.7 %levels6.1 = (f32[8,1024,256]{2,1,0:T(8,128)S(1)}, f32[8,1,256]{2,1,0:T(1,128)S(1)}) custom-call(bf16[128,2048]{1,0:T(8,128)(2,1)S(1)} %get-tuple-element.120.flipped_ref, f32[5,16,2048]{2,1,0:T(8,128)S(1)} %get-tuple-element.121.coef_ref, bf16[512,128]{1,0:T(8,128)(2,1)S(1)} %gather1.1.rest_0_, ...), custom_call_target="tpu_custom_call", output_to_operand_aliasing={{0}: (5, {})} | custom-call | flops 1073741824 | bytes 4000000 | tf_op jit(solution)/shard_map/levels6/pallas_call | solution.py:482
  46.4 1.6 %collective-permute-start.12 = (f32[8,1,256]{2,1,0:T(1,128)S(1)}, f32[8,1,256]{2,1,0:T(1,128)S(1)}, u32[]{:S(2)}, u32[]{:S(2)}) collective-permute-start(f32[8,1,256]{2,1,0:T(1,128)S(1)} %get-tuple-element.144.s0), channel_id=1, source_target_pairs={{0,1},{1,0},{2,3},{3,2},{4,5},{5,4},{6,7},{7,6},{8,9},{9,8},{10,11... | collective-permute-start | bytes 24584 | tf_op jit(solution)/shard_map/ppermute | solution.py:603
  48.0 2.1 %collective-permute-start.13 = (f32[8,1,256]{2,1,0:T(1,128)S(1)}, f32[8,1,256]{2,1,0:T(1,128)S(1)}, u32[]{:S(2)}, u32[]{:S(2)}) collective-permute-start(f32[8,1,256]{2,1,0:T(1,128)S(1)} %get-tuple-element.144.s0), channel_id=1, source_target_pairs={{0,3},{1,2},{2,1},{3,0},{4,7},{5,6},{6,5},{7,4},{8,11},{9,10},{10,... | collective-permute-start | bytes 24584 | tf_op jit(solution)/shard_map/ppermute | solution.py:603
  50.1 0.6 %collective-permute-start.14 = (f32[8,1,256]{2,1,0:T(1,128)S(1)}, f32[8,1,256]{2,1,0:T(1,128)S(1)}, u32[]{:S(2)}, u32[]{:S(2)}) collective-permute-start(f32[8,1,256]{2,1,0:T(1,128)S(1)} %get-tuple-element.144.s0), channel_id=1, source_target_pairs={{0,2},{1,3},{2,0},{3,1},{4,6},{5,7},{6,4},{7,5},{8,10},{9,11},{10,... | collective-permute-start | bytes 24584 | tf_op jit(solution)/shard_map/ppermute | solution.py:603
  50.7 0.0 copy-done
  50.7 2.2 %flip.1.y_ref = f32[2048,1024]{1,0:T(8,128)S(1)} custom-call(f32[8,1024,256]{2,1,0:T(8,128)S(1)} %get-tuple-element.143.y_ref, f32[1,1024]{1,0:T(1,128)S(1)} %bitcast.1), custom_call_target="tpu_custom_call" | custom-call | bytes 16000000 | tf_op jit(solution)/shard_map/flip/pallas_call | solution.py:509
  53.0 0.0 collective-permute-done.12.s1
  53.0 0.0 collective-permute-done.13.s2
  53.0 2.3 %collective-permute-done.14.s3 = f32[8,1,256]{2,1,0:T(1,128)S(1)} collective-permute-done((f32[8,1,256]{2,1,0:T(1,128)S(1)}, f32[8,1,256]{2,1,0:T(1,128)S(1)}, u32[]{:S(2)}, u32[]{:S(2)}) %collective-permute-start.14) | collective-permute-done | bytes 8224 | tf_op jit(solution)/shard_map/ppermute | solution.py:603
  55.2 2.2 %normalize.1 = bf16[2048,1024]{1,0:T(8,128)(2,1)} custom-call(f32[2048,1024]{1,0:T(8,128)S(1)} %flip.1.y_ref, f32[8,1,256]{2,1,0:T(1,128)S(1)} %get-tuple-element.144.s0, f32[8,1,256]{2,1,0:T(1,128)S(1)} %collective-permute-done.12.s1, f32[8,1,256]{2,1,0:T(1,128)S(1)} %collective-permute-done.13.s2, f32[8,1,256]{2,1,0:T(1,128)S(1)} %collective-permute-done.14.s3), custom_call_target="tpu_custom_call" | custom-call | tf_op jit(solution)/shard_map/normalize/pallas_call | solution.py:539
  (2 shorter events, 0.0 us)
Async XLA Ops:
  5.4 1.6 %collective-permute-start = (bf16[1040,128]{1,0:T(8,128)(2,1)S(1)}, bf16[1040,128]{1,0:T(8,128)(2,1)S(1)}, u32[]{:S(2)}, u32[]{:S(2)}) collective-permute-start(bf16[1040,128]{1,0:T(8,128)(2,1)S(1)} %get-tuple-element.77), channel_id=1, source_target_pairs={{0,4},{4,0},{8,12},{12,8},{16,20},{20,16},{24,28},{28,24},{32,36},... | collective-permute-start | bytes 798728 | tf_op jit(solution)/shard_map/ppermute | solution.py:560
  7.2 8.1 %collective-permute-start.1 = (bf16[528,128]{1,0:T(8,128)(2,1)S(1)}, bf16[528,128]{1,0:T(8,128)(2,1)S(1)}, u32[]{:S(2)}, u32[]{:S(2)}) collective-permute-start(bf16[528,128]{1,0:T(8,128)(2,1)S(1)} %get-tuple-element.81), channel_id=1, source_target_pairs={{0,8},{4,12},{8,0},{12,4},{16,24},{20,28},{24,16},{28,20},{32,40},... | collective-permute-start | bytes 405512 | tf_op jit(solution)/shard_map/ppermute | solution.py:560
  8.6 8.2 %collective-permute-start.2 = (bf16[528,128]{1,0:T(8,128)(2,1)S(1)}, bf16[528,128]{1,0:T(8,128)(2,1)S(1)}, u32[]{:S(2)}, u32[]{:S(2)}) collective-permute-start(bf16[528,128]{1,0:T(8,128)(2,1)S(1)} %get-tuple-element.81), channel_id=1, source_target_pairs={{0,24},{4,28},{8,16},{12,20},{16,8},{20,12},{24,0},{28,4},{32,56},... | collective-permute-start | bytes 405512 | tf_op jit(solution)/shard_map/ppermute | solution.py:560
  10.0 6.9 %collective-permute-start.3 = (bf16[528,128]{1,0:T(8,128)(2,1)S(1)}, bf16[528,128]{1,0:T(8,128)(2,1)S(1)}, u32[]{:S(2)}, u32[]{:S(2)}) collective-permute-start(bf16[528,128]{1,0:T(8,128)(2,1)S(1)} %get-tuple-element.81), channel_id=1, source_target_pairs={{0,16},{4,20},{8,24},{12,28},{16,0},{20,4},{24,8},{28,12},{32,48},... | collective-permute-start | bytes 405512 | tf_op jit(solution)/shard_map/ppermute | solution.py:560
  17.1 19.0 %collective-permute-start.8 = (bf16[1024,128]{1,0:T(8,128)(2,1)S(1)}, bf16[1024,128]{1,0:T(8,128)(2,1)S(1)}, u32[]{:S(2)}, u32[]{:S(2)}) collective-permute-start(bf16[1024,128]{1,0:T(8,128)(2,1)S(1)} %get-tuple-element.131.rest_0_), channel_id=1, source_target_pairs={{0,4},{4,0},{8,12},{12,8},{16,20},{20,16},{24,28},{28,24},{32,36},... | collective-permute-start | bytes 786440 | tf_op jit(solution)/shard_map/ppermute | solution.py:560
  17.2 4.8 %collective-permute-start.4 = (bf16[272,128]{1,0:T(8,128)(2,1)S(1)}, bf16[272,128]{1,0:T(8,128)(2,1)S(1)}, u32[]{:S(2)}, u32[]{:S(2)}) collective-permute-start(bf16[272,128]{1,0:T(8,128)(2,1)S(1)} %get-tuple-element.102), channel_id=1, source_target_pairs={{0,32},{4,36},{8,40},{12,44},{16,48},{20,52},{24,56},{28,60},{32,0... | collective-permute-start | bytes 208904 | tf_op jit(solution)/shard_map/ppermute | solution.py:560
  22.1 7.3 %collective-permute-start.5 = (bf16[272,128]{1,0:T(8,128)(2,1)S(1)}, bf16[272,128]{1,0:T(8,128)(2,1)S(1)}, u32[]{:S(2)}, u32[]{:S(2)}) collective-permute-start(bf16[272,128]{1,0:T(8,128)(2,1)S(1)} %get-tuple-element.110), channel_id=1, source_target_pairs={{0,64},{4,68},{8,72},{12,76},{16,80},{20,84},{24,88},{28,92},{32,9... | collective-permute-start | bytes 208904 | tf_op jit(solution)/shard_map/ppermute | solution.py:560
  29.6 8.9 %collective-permute-start.6 = (bf16[512,128]{1,0:T(8,128)(2,1)S(1)}, bf16[512,128]{1,0:T(8,128)(2,1)S(1)}, u32[]{:S(2)}, u32[]{:S(2)}) collective-permute-start(bf16[512,128]{1,0:T(8,128)(2,1)S(1)} %get-tuple-element.128.refs_0_), channel_id=1, source_target_pairs={{0,8},{4,12},{8,0},{12,4},{16,24},{20,28},{24,16},{28,20},{32,40},... | collective-permute-start | bytes 393224 | tf_op jit(solution)/shard_map/ppermute | solution.py:560
  31.7 6.8 %collective-permute-start.7 = (bf16[272,128]{1,0:T(8,128)(2,1)S(1)}, bf16[272,128]{1,0:T(8,128)(2,1)S(1)}, u32[]{:S(2)}, u32[]{:S(2)}) collective-permute-start(bf16[272,128]{1,0:T(8,128)(2,1)S(1)} %get-tuple-element.129), channel_id=1, source_target_pairs={{0,192},{4,196},{8,200},{12,204},{16,208},{20,212},{24,216},{28,22... | collective-permute-start | bytes 208904 | tf_op jit(solution)/shard_map/ppermute | solution.py:560
  38.6 1.6 %collective-permute-start.10 = (bf16[1024,128]{1,0:T(8,128)(2,1)S(1)}, bf16[1024,128]{1,0:T(8,128)(2,1)S(1)}, u32[]{:S(2)}, u32[]{:S(2)}) collective-permute-start(bf16[1024,128]{1,0:T(8,128)(2,1)S(1)} %gather2.1.rest_0_), channel_id=1, source_target_pairs={{0,4},{4,0},{8,12},{12,8},{16,20},{20,16},{24,28},{28,24},{32,36},... | collective-permute-start | bytes 786440 | tf_op jit(solution)/shard_map/ppermute | solution.py:560
  38.7 4.6 %collective-permute-start.9 = (bf16[272,128]{1,0:T(8,128)(2,1)S(1)}, bf16[272,128]{1,0:T(8,128)(2,1)S(1)}, u32[]{:S(2)}, u32[]{:S(2)}) collective-permute-start(bf16[272,128]{1,0:T(8,128)(2,1)S(1)} %collective-permute-done.7.refs_0_), channel_id=1, source_target_pairs={{0,8},{4,12},{8,0},{12,4},{16,24},{20,28},{24,16},{28,20},{32,40},... | collective-permute-start | bytes 208904 | tf_op jit(solution)/shard_map/ppermute | solution.py:560
  42.6 8.1 %copy-start = (f32[1024]{0:T(1024)S(1)}, f32[1024]{0:T(1024)}, u32[]{:S(2)}) copy-start(f32[1024]{0:T(1024)} %param.14) | copy-start | bytes 12292
  43.3 1.4 %collective-permute-start.11 = (bf16[512,128]{1,0:T(8,128)(2,1)S(1)}, bf16[512,128]{1,0:T(8,128)(2,1)S(1)}, u32[]{:S(2)}, u32[]{:S(2)}) collective-permute-start(bf16[512,128]{1,0:T(8,128)(2,1)S(1)} %gather1.1.rest_0_), channel_id=1, source_target_pairs={{0,4},{4,0},{8,12},{12,8},{16,20},{20,16},{24,28},{28,24},{32,36},... | collective-permute-start | bytes 393224 | tf_op jit(solution)/shard_map/ppermute | solution.py:560
  46.4 6.5 %collective-permute-start.12 = (f32[8,1,256]{2,1,0:T(1,128)S(1)}, f32[8,1,256]{2,1,0:T(1,128)S(1)}, u32[]{:S(2)}, u32[]{:S(2)}) collective-permute-start(f32[8,1,256]{2,1,0:T(1,128)S(1)} %get-tuple-element.144.s0), channel_id=1, source_target_pairs={{0,1},{1,0},{2,3},{3,2},{4,5},{5,4},{6,7},{7,6},{8,9},{9,8},{10,11... | collective-permute-start | bytes 24584 | tf_op jit(solution)/shard_map/ppermute | solution.py:603
  48.0 5.0 %collective-permute-start.13 = (f32[8,1,256]{2,1,0:T(1,128)S(1)}, f32[8,1,256]{2,1,0:T(1,128)S(1)}, u32[]{:S(2)}, u32[]{:S(2)}) collective-permute-start(f32[8,1,256]{2,1,0:T(1,128)S(1)} %get-tuple-element.144.s0), channel_id=1, source_target_pairs={{0,3},{1,2},{2,1},{3,0},{4,7},{5,6},{6,5},{7,4},{8,11},{9,10},{10,... | collective-permute-start | bytes 24584 | tf_op jit(solution)/shard_map/ppermute | solution.py:603
  50.1 5.2 %collective-permute-start.14 = (f32[8,1,256]{2,1,0:T(1,128)S(1)}, f32[8,1,256]{2,1,0:T(1,128)S(1)}, u32[]{:S(2)}, u32[]{:S(2)}) collective-permute-start(f32[8,1,256]{2,1,0:T(1,128)S(1)} %get-tuple-element.144.s0), channel_id=1, source_target_pairs={{0,2},{1,3},{2,0},{3,1},{4,6},{5,7},{6,4},{7,5},{8,10},{9,11},{10,... | collective-permute-start | bytes 24584 | tf_op jit(solution)/shard_map/ppermute | solution.py:603
